TPU v7x, 32 devices: a whole 2x2x4 slice. The times are simulated.
32 devices in a mesh: dp: 8 (over y, x, core), tensor: 4 (over z).
Axes of the slice: x: 2, y: 2, z: 4, core: 2. Of those that a mesh axis runs over, the one named last changes fastest.
Arguments:
- block_input: bfloat16 [24, 1376, 1024], P('dp', 'tensor'), may hold values from -6 to 6
- cotangent: bfloat16 [24, 1376, 1024], P('dp', 'tensor'), may hold values from -6 to 6
- lengths: int32 [24], P('dp'), may hold values from 685 to 1370, as said below
- w_qkv: bfloat16 [3, 1024, 1024], P(None, 'dp', 'tensor'), may hold values from -0.1875 to 0.1875
- b_qv: bfloat16 [2, 64, 16], P(None, 'dp', 'tensor'), may hold values from -2 to 2
- w_out: bfloat16 [1024, 1024], P('tensor', 'dp'), may hold values from -0.1875 to 0.1875
- w_fc1: bfloat16 [1024, 4096], P('dp', 'tensor'), may hold values from -0.1875 to 0.1875
- b_fc1: bfloat16 [64, 64], P('dp', 'tensor'), may hold values from -3 to 3
- w_fc2: bfloat16 [4096, 1024], P('tensor', 'dp'), may hold values from -0.09375 to 0.09375
- ln_gain: float32 [2, 1024], P(None, ('dp', 'tensor')), may hold values from 0.25 to 1.75
- ln_shift: float32 [2, 1024], P(None, ('dp', 'tensor')), may hold values from -2 to 2
- layer_scale: float32 [2, 1024], P(None, ('dp', 'tensor')), may hold values from 0.5 to 2
- out_bias: float32 [2, 1024], P(None, ('dp', 'tensor')), may hold values from -2 to 2
Outputs:
- block_out: bfloat16 [24, 1376, 1024], P('dp', 'tensor')
- grad_input: float32 [24, 1376, 1024], P('dp', 'tensor')
- grad_w_qkv: float32 [3, 1024, 1024], P(None, 'dp', 'tensor')
- grad_b_qv: float32 [2, 64, 16], P(None, 'dp', 'tensor')
- grad_w_out: float32 [1024, 1024], P('tensor', 'dp')
- grad_w_fc1: float32 [1024, 4096], P('dp', 'tensor')
- grad_b_fc1: float32 [64, 64], P('dp', 'tensor')
- grad_w_fc2: float32 [4096, 1024], P('tensor', 'dp')
- grad_ln_gain: float32 [2, 1024], P(None, ('dp', 'tensor'))
- grad_ln_shift: float32 [2, 1024], P(None, ('dp', 'tensor'))
- grad_layer_scale: float32 [2, 1024], P(None, ('dp', 'tensor'))
- grad_out_bias: float32 [2, 1024], P(None, ('dp', 'tensor'))
Inputs may be any that keep to these rules, and one draw needn't show every extreme that they name: `lengths`: image 0 has exactly 1370 valid tokens.
All inputs are finite; a program needn't handle non-finite values.
Results may differ from a plain program's by a relative error of at most 0.011.
Values may be sent and summed in bfloat16 or wider, within the bound.
A program may use at most 320 MiB of HBM per device.

v0:
```python
import jax
import jax.numpy as jnp
from jax import lax
from jax.sharding import PartitionSpec as P

HD = 64


def norm_rows(values, gain, shift):
    center = values - jnp.mean(values, axis=-1, keepdims=True)
    inverse = lax.rsqrt(jnp.mean(center * center, axis=-1, keepdims=True) + 1e-06)
    normed = center * inverse
    return (normed * gain + shift, normed, inverse)


def norm_back(grad_norm, normed, inverse, gain):
    scaled = grad_norm * gain
    return inverse * (
        scaled
        - jnp.mean(scaled, axis=-1, keepdims=True)
        - normed * jnp.mean(scaled * normed, axis=-1, keepdims=True)
    )


def gelu_back(pre_act, grad_act):
    return jax.vjp(lambda argument: jax.nn.gelu(argument, approximate=False), pre_act)[1](grad_act)[
        0
    ]


def head_scores(queries, keys_in, key_mask):
    scores = jnp.einsum(
        "qhe,khe->hqk", queries, keys_in, preferred_element_type=jnp.float32
    ) * HD ** (-0.5)
    return jnp.where(key_mask[None, None, :], scores, -1e30)


def attend_forward(sample):
    queries, keys_in, values_in, key_mask = sample
    scores = head_scores(queries, keys_in, key_mask)
    row_max = jnp.max(scores, axis=-1, keepdims=True)
    log_total = row_max + jnp.log(jnp.sum(jnp.exp(scores - row_max), axis=-1, keepdims=True))
    probs = jnp.exp(scores - log_total).astype(jnp.bfloat16)
    context = jnp.einsum(
        "hqk,khe->qhe", probs, values_in, preferred_element_type=jnp.float32
    ).astype(jnp.bfloat16)
    return (context, log_total)


def attend_backward(sample):
    queries, keys_in, values_in, key_mask, context, log_total, grad_context = sample
    scores = head_scores(queries, keys_in, key_mask)
    probs_f = jnp.exp(scores - log_total)
    probs = probs_f.astype(jnp.bfloat16)
    grad_value = jnp.einsum("hqk,qhe->khe", probs, grad_context, preferred_element_type=jnp.float32)
    grad_probs = jnp.einsum(
        "qhe,khe->hqk", grad_context, values_in, preferred_element_type=jnp.float32
    )
    correction = jnp.sum(grad_context.astype(jnp.float32) * context.astype(jnp.float32), axis=-1)
    grad_scores = (probs_f * (grad_probs - correction.T[:, :, None]) * HD ** (-0.5)).astype(
        jnp.bfloat16
    )
    grad_query = jnp.einsum(
        "hqk,khe->qhe", grad_scores, keys_in, preferred_element_type=jnp.float32
    )
    grad_key = jnp.einsum("hqk,qhe->khe", grad_scores, queries, preferred_element_type=jnp.float32)
    return (grad_query, grad_key, grad_value)


def body(
    block_input,
    cotangent,
    lengths,
    w_qkv,
    b_qv,
    w_out,
    w_fc1,
    b_fc1,
    w_fc2,
    ln_gain,
    ln_shift,
    layer_scale,
    out_bias,
):
    image_count, row_count, model_width = block_input.shape
    full_length = row_count * lax.axis_size("tensor")
    own_position = lax.axis_index("tensor") * row_count + jnp.arange(row_count, dtype=jnp.int32)
    own_valid = (own_position[None, :] < lengths[:, None]).astype(jnp.float32)[:, :, None]
    key_valid = jnp.arange(full_length, dtype=jnp.int32)[None, :] < lengths[:, None]
    wqkv_all, bqv_all, wout_all, wfc1_all, bfc1_all, wfc2_all = (
        lax.all_gather(w_qkv, "dp", axis=1, tiled=True),
        lax.all_gather(b_qv, "dp", axis=1, tiled=True),
        lax.all_gather(w_out, "dp", axis=1, tiled=True),
        lax.all_gather(w_fc1, "dp", axis=0, tiled=True),
        lax.all_gather(b_fc1, "dp", axis=0, tiled=True),
        lax.all_gather(w_fc2, "dp", axis=1, tiled=True),
    )
    local_heads = bqv_all.shape[2]
    fc1_bias = bfc1_all.T.reshape(-1)
    gains, shifts, scales, biases = (
        lax.all_gather(ln_gain, ("dp", "tensor"), axis=1, tiled=True),
        lax.all_gather(ln_shift, ("dp", "tensor"), axis=1, tiled=True),
        lax.all_gather(layer_scale, ("dp", "tensor"), axis=1, tiled=True),
        lax.all_gather(out_bias, ("dp", "tensor"), axis=1, tiled=True),
    )
    source = block_input.astype(jnp.float32)
    normed_one, hat_first, inv_first = norm_rows(source, gains[0], shifts[0])
    normed1 = normed_one.astype(jnp.bfloat16)
    head_shape = (image_count, full_length, local_heads, HD)
    qv_bias = jnp.transpose(bqv_all, (0, 2, 1)).reshape(2, local_heads * HD).astype(jnp.float32)
    normed1_all = lax.all_gather(normed1, "tensor", axis=1, tiled=True)
    projected = jnp.einsum(
        "isd,kdc->kisc", normed1_all, wqkv_all, preferred_element_type=jnp.float32
    )
    queries = (projected[0] + qv_bias[0]).astype(jnp.bfloat16).reshape(head_shape)
    keys_all = projected[1].astype(jnp.bfloat16).reshape(head_shape)
    values_all = (projected[2] + qv_bias[1]).astype(jnp.bfloat16).reshape(head_shape)
    context, log_total = lax.map(attend_forward, (queries, keys_all, values_all, key_valid))
    context_flat = context.reshape(image_count, full_length, local_heads * HD)
    attn_part = jnp.einsum(
        "isc,cd->isd", context_flat, wout_all, preferred_element_type=jnp.float32
    )
    attn_own = lax.psum_scatter(attn_part, "tensor", scatter_dimension=1, tiled=True) + biases[0]
    hidden = source + scales[0] * attn_own
    normed_two, hat_second, inv_second = norm_rows(hidden, gains[1], shifts[1])
    normed2 = normed_two.astype(jnp.bfloat16)
    fc1_full, fc1_bias_full, fc2_full = (
        lax.all_gather(wfc1_all, "tensor", axis=1, tiled=True),
        lax.all_gather(fc1_bias, "tensor", axis=0, tiled=True),
        lax.all_gather(wfc2_all, "tensor", axis=0, tiled=True),
    )
    pre_act = (
        jnp.einsum("isd,df->isf", normed2, fc1_full, preferred_element_type=jnp.float32)
        + fc1_bias_full
    )
    activation = jax.nn.gelu(pre_act, approximate=False).astype(jnp.bfloat16)
    mlp_own = (
        jnp.einsum("isf,fd->isd", activation, fc2_full, preferred_element_type=jnp.float32)
        + biases[1]
    )
    block_out = (own_valid * (hidden + scales[1] * mlp_own)).astype(jnp.bfloat16)
    grad_out = own_valid * cotangent.astype(jnp.float32)
    grad_scale2 = jnp.sum(grad_out * mlp_own, axis=(0, 1))
    grad_mlp = grad_out * scales[1]
    grad_bias2 = jnp.sum(grad_mlp, axis=(0, 1))
    grad_mlp_b = grad_mlp.astype(jnp.bfloat16)
    grad_fc2_full = jnp.einsum(
        "isf,isd->fd", activation, grad_mlp_b, preferred_element_type=jnp.float32
    )
    grad_act = jnp.einsum("isd,fd->isf", grad_mlp_b, fc2_full, preferred_element_type=jnp.float32)
    grad_pre = gelu_back(pre_act, grad_act)
    grad_bias_full = jnp.sum(grad_pre, axis=(0, 1))
    grad_pre_b = grad_pre.astype(jnp.bfloat16)
    grad_fc1_full = jnp.einsum(
        "isd,isf->df", normed2, grad_pre_b, preferred_element_type=jnp.float32
    )
    grad_normed2 = jnp.einsum(
        "isf,df->isd", grad_pre_b, fc1_full, preferred_element_type=jnp.float32
    )
    grad_fc1, grad_fc1_bias, grad_fc2 = (
        lax.psum_scatter(grad_fc1_full, "tensor", scatter_dimension=1, tiled=True),
        lax.psum_scatter(grad_bias_full, "tensor", scatter_dimension=0, tiled=True),
        lax.psum_scatter(grad_fc2_full, "tensor", scatter_dimension=0, tiled=True),
    )
    grad_gain2 = jnp.sum(grad_normed2 * hat_second, axis=(0, 1))
    grad_shift2 = jnp.sum(grad_normed2, axis=(0, 1))
    grad_hidden = grad_out + norm_back(grad_normed2, hat_second, inv_second, gains[1])
    grad_scale1 = jnp.sum(grad_hidden * attn_own, axis=(0, 1))
    grad_attn = grad_hidden * scales[0]
    grad_bias1 = jnp.sum(grad_attn, axis=(0, 1))
    grad_attn_b = grad_attn.astype(jnp.bfloat16)
    grad_attn_all = lax.all_gather(grad_attn_b, "tensor", axis=1, tiled=True)
    grad_wout = jnp.einsum(
        "isc,isd->cd", context_flat, grad_attn_all, preferred_element_type=jnp.float32
    )
    grad_context = (
        jnp.einsum("isd,cd->isc", grad_attn_all, wout_all, preferred_element_type=jnp.float32)
        .astype(jnp.bfloat16)
        .reshape(head_shape)
    )
    grad_query, grad_key, grad_value = lax.map(
        attend_backward,
        (queries, keys_all, values_all, key_valid, context, log_total, grad_context),
    )
    grad_qv = jnp.stack(
        [jnp.sum(grad_query, axis=(0, 1)).reshape(-1), jnp.sum(grad_value, axis=(0, 1)).reshape(-1)]
    )
    flat_shape = (image_count, full_length, local_heads * HD)
    grad_proj = jnp.stack(
        [
            grad_query.reshape(flat_shape),
            grad_key.reshape(flat_shape),
            grad_value.reshape(flat_shape),
        ]
    ).astype(jnp.bfloat16)
    grad_wqkv = jnp.einsum(
        "isd,kisc->kdc", normed1_all, grad_proj, preferred_element_type=jnp.float32
    )
    grad_normed1 = lax.psum_scatter(
        jnp.einsum("kisc,kdc->isd", grad_proj, wqkv_all, preferred_element_type=jnp.float32),
        "tensor",
        scatter_dimension=1,
        tiled=True,
    )
    grad_gain1 = jnp.sum(grad_normed1 * hat_first, axis=(0, 1))
    grad_shift1 = jnp.sum(grad_normed1, axis=(0, 1))
    grad_input = grad_hidden + norm_back(grad_normed1, hat_first, inv_first, gains[0])
    grad_bqv = jnp.transpose(grad_qv.reshape(2, local_heads, HD), (0, 2, 1))
    grad_bfc1 = grad_fc1_bias.reshape(-1, HD).T
    shard_wqkv, shard_bqv, shard_wout, shard_fc1, shard_bfc1, shard_fc2 = (
        lax.psum_scatter(grad_wqkv, "dp", scatter_dimension=1, tiled=True),
        lax.psum_scatter(grad_bqv, "dp", scatter_dimension=1, tiled=True),
        lax.psum_scatter(grad_wout, "dp", scatter_dimension=1, tiled=True),
        lax.psum_scatter(grad_fc1, "dp", scatter_dimension=0, tiled=True),
        lax.psum_scatter(grad_bfc1, "dp", scatter_dimension=0, tiled=True),
        lax.psum_scatter(grad_fc2, "dp", scatter_dimension=1, tiled=True),
    )
    shard_gain, shard_shift, shard_scale, shard_bias = (
        lax.psum_scatter(
            jnp.stack([grad_gain1, grad_gain2]), ("dp", "tensor"), scatter_dimension=1, tiled=True
        ),
        lax.psum_scatter(
            jnp.stack([grad_shift1, grad_shift2]), ("dp", "tensor"), scatter_dimension=1, tiled=True
        ),
        lax.psum_scatter(
            jnp.stack([grad_scale1, grad_scale2]), ("dp", "tensor"), scatter_dimension=1, tiled=True
        ),
        lax.psum_scatter(
            jnp.stack([grad_bias1, grad_bias2]), ("dp", "tensor"), scatter_dimension=1, tiled=True
        ),
    )
    return (
        block_out,
        grad_input,
        shard_wqkv,
        shard_bqv,
        shard_wout,
        shard_fc1,
        shard_bfc1,
        shard_fc2,
        shard_gain,
        shard_shift,
        shard_scale,
        shard_bias,
    )


def solution(mesh):
    placed = (
        P("dp", "tensor", None),
        P("dp", "tensor", None),
        P("dp"),
        P(None, "dp", "tensor"),
        P(None, "dp", "tensor"),
        P("tensor", "dp"),
        P("dp", "tensor"),
        P("dp", "tensor"),
        P("tensor", "dp"),
        P(None, ("dp", "tensor")),
        P(None, ("dp", "tensor")),
        P(None, ("dp", "tensor")),
        P(None, ("dp", "tensor")),
    )
    return jax.shard_map(
        body,
        mesh=mesh,
        in_specs=placed,
        out_specs=(
            P("dp", "tensor", None),
            P("dp", "tensor", None),
            P(None, "dp", "tensor"),
            P(None, "dp", "tensor"),
            P("tensor", "dp"),
            P("dp", "tensor"),
            P("dp", "tensor"),
            P("tensor", "dp"),
            P(None, ("dp", "tensor")),
            P(None, ("dp", "tensor")),
            P(None, ("dp", "tensor")),
            P(None, ("dp", "tensor")),
        ),
        check_vma=False,
    )
```

profile of v0, /device:TPU:0, one launch (start us, length us, event | category | flops | bytes accessed | tf_op | source)
XLA Modules:
  0.0 3101.6 jit_solution(1680076214962877858)
XLA Ops:
  8.0 70.1 %all-gather.1 = f32[32,32,2]{1,2,0:T(2,128)S(1)} all-gather(f32[1,32,2]{1,2,0:T(2,128)} %bitcast.300), channel_id=1, replica_groups=mesh['dp'=8,'tensor'=4] {'dp','tensor'}, dimensions={0}, use_global_device_ids=true | all-gather | bytes 8448 | tf_op jit(solution)/shard_map/all_gather | solution.py:101
  78.1 63.8 %all-gather.2 = f32[32,32,2]{1,2,0:T(2,128)S(1)} all-gather(f32[1,32,2]{1,2,0:T(2,128)} %bitcast.301), channel_id=1, replica_groups=mesh['dp'=8,'tensor'=4] {'dp','tensor'}, dimensions={0}, use_global_device_ids=true | all-gather | bytes 8448 | tf_op jit(solution)/shard_map/all_gather | solution.py:102
  170.6 128.0 %all-gather.12.cloned.1.call-done = bf16[3,1376,1024]{2,1,0:T(8,128)(2,1)} async-done(((bf16[3,344,1024]{2,1,0:T(8,128)(2,1)}), bf16[3,1376,1024]{2,1,0:T(8,128)(2,1)}) %all-gather.12.cloned.1.call-update) | async-done | bytes 8454160 | tf_op jit(solution)/shard_map/all_gather | solution.py:111
  335.1 126.6 %while.26 = (s32[]{:T(128)}, bf16[3,1376,4,64]{1,3,2,0:T(8,128)(2,1)}, f32[3,4,1376,1]{2,1,3,0:T(4,128)S(1)}, bf16[3,1376,4,64]{1,3,2,0:T(8,128)(2,1)}, pred[3,1...) while((s32[]{:T(128)}, ...), condition=%wide.region_5.6_spmd, body=%wide.region_2.5_spmd.sunk | while | flops 1992178304 | bytes 94655272 | solution.py:118
  494.4 66.6 %all-gather = f32[32,32,2]{1,2,0:T(2,128)S(1)} all-gather(f32[1,32,2]{1,2,0:T(2,128)S(1)} %bitcast.302), channel_id=1, replica_groups=mesh['dp'=8,'tensor'=4] {'dp','tensor'}, dimensions={0}, use_global_device_ids=true | all-gather | bytes 8448 | tf_op jit(solution)/shard_map/all_gather | solution.py:103
  561.1 68.7 %all-gather.3 = f32[32,32,2]{1,2,0:T(2,128)S(1)} all-gather(f32[1,32,2]{1,2,0:T(2,128)S(1)} %bitcast.303), channel_id=1, replica_groups=mesh['dp'=8,'tensor'=4] {'dp','tensor'}, dimensions={0}, use_global_device_ids=true | all-gather | bytes 8448 | tf_op jit(solution)/shard_map/all_gather | solution.py:104
  630.5 124.3 %reduce-scatter.23.cloned.1.call-done = f32[3,344,1024]{2,1,0:T(8,128)} async-done(((f32[3,1376,1024]{2,1,0:T(8,128)}), f32[3,344,1024]{2,1,0:T(8,128)}) %reduce-scatter.23.cloned.1.call-update) | async-done | bytes 4227088 | tf_op jit(solution)/shard_map/reduce_scatter | solution.py:123
  760.5 145.8 %all-gather.18.cloned.1.call-done = bf16[1024,4096]{1,0:T(8,128)(2,1)} async-done(((bf16[1024,1024]{1,0:T(8,128)(2,1)}), bf16[1024,4096]{1,0:T(8,128)(2,1)}) %all-gather.18.cloned.1.call-update) | async-done | bytes 8388624 | tf_op jit(solution)/shard_map/all_gather | solution.py:128
  906.3 23.5 fusion.93
  929.8 41.7 %multiply_convert_fusion = (bf16[3,344,4096]{2,1,0:T(8,128)(2,1)}, f32[3,344,4096]{2,1,0:T(8,128)}) fusion(f32[3,344,4096]{2,1,0:T(8,128)} %get-tuple-element.249, f32[4096]{0:T(1024)S(1)} %convert_element_type.94, u8[344,4096]{1,0:T(8,128)(4,1)S(1)} %get-tuple-element.169, u8[344,4096]{1,0:T(8,128)(4,1)S(1)} %get-tuple-element.168), kind=kLoop, calls=%fused_computation.67 | loop fusion | flops 300122112 | bytes 45105152 | tf_op jit(solution)/shard_map/convert_element_type | solution.py:136
  971.5 84.2 %all-gather.22.cloned.1.call-done = bf16[4096,1024]{1,0:T(8,128)(2,1)} async-done(((bf16[1024,1024]{1,0:T(8,128)(2,1)}), bf16[4096,1024]{1,0:T(8,128)(2,1)}) %all-gather.22.cloned.1.call-update) | async-done | bytes 8388624 | tf_op jit(solution)/shard_map/all_gather | solution.py:130
  1055.7 26.5 fusion.117
  1122.3 149.0 %all-gather.24.cloned.1.call-done = bf16[3,1376,1024]{2,1,0:T(8,128)(2,1)} async-done(((bf16[3,344,1024]{2,1,0:T(8,128)(2,1)}), bf16[3,1376,1024]{2,1,0:T(8,128)(2,1)}) %all-gather.24.cloned.1.call-update) | async-done | bytes 8454160 | tf_op jit(solution)/shard_map/all_gather | solution.py:172
  1281.3 202.6 %while.27 = (s32[]{:T(128)}, f32[3,1376,4,64]{1,3,2,0:T(8,128)}, bf16[3,1376,4,64]{1,3,2,0:T(8,128)(2,1)}, f32[3,1376,4,64]{1,3,2,0:T(8,128)}, bf16[3,1376,4,64]...) while((s32[]{:T(128)}, f32[3,1376,4,64]{1,3,2,0:T(8,128)}, ...), condition=%wide.region_13.14_spmd, body=%wide.region_11.13_spmd.sunk | while | flops 4909033984 | bytes 149337264 | solution.py:181
  1567.7 226.8 %reduce-scatter.25.cloned.1.call-done = f32[3,344,1024]{2,1,0:T(8,128)} async-done(((f32[3,1376,1024]{2,1,0:T(8,128)}), f32[3,344,1024]{2,1,0:T(8,128)}) %reduce-scatter.25.cloned.1.call-update) | async-done | bytes 4227088 | tf_op jit(solution)/shard_map/reduce_scatter | solution.py:199
  1809.6 268.2 %reduce-scatter.31.cloned.1.call-done = f32[1024,1024]{1,0:T(8,128)} async-done(((f32[1024,4096]{1,0:T(8,128)}), f32[1024,1024]{1,0:T(8,128)}) %reduce-scatter.31.cloned.1.call-update) | async-done | bytes 4194320 | tf_op jit(solution)/shard_map/reduce_scatter | solution.py:161
  2077.9 283.5 %reduce-scatter.35.cloned.1.call-done = f32[1024,1024]{1,0:T(8,128)} async-done(((f32[4096,1024]{1,0:T(8,128)}), f32[1024,1024]{1,0:T(8,128)}) %reduce-scatter.35.cloned.1.call-update) | async-done | bytes 4194320 | tf_op jit(solution)/shard_map/reduce_scatter | solution.py:163
  2382.2 116.5 %reduce-scatter.43.cloned.1.call-done = f32[32,2]{1,0:T(8,128)} async-done(((f32[1024,2]{1,0:T(8,128)}), f32[32,2]{1,0:T(8,128)}) %reduce-scatter.43.cloned.1.call-update) | async-done | bytes 272
  2500.0 131.3 %reduce-scatter.45.cloned.1.call-done = f32[32,2]{1,0:T(8,128)} async-done(((f32[1024,2]{1,0:T(8,128)}), f32[32,2]{1,0:T(8,128)}) %reduce-scatter.45.cloned.1.call-update) | async-done | bytes 272
  2685.6 128.9 %reduce-scatter.41.cloned.1.call-done = f32[32,2]{1,0:T(8,128)} async-done(((f32[1024,2]{1,0:T(8,128)}), f32[32,2]{1,0:T(8,128)}) %reduce-scatter.41.cloned.1.call-update) | async-done | bytes 272
  2815.8 131.4 %reduce-scatter.39.cloned.1.call-done = f32[32,2]{1,0:T(8,128)} async-done(((f32[1024,2]{1,0:T(8,128)}), f32[32,2]{1,0:T(8,128)}) %reduce-scatter.39.cloned.1.call-update) | async-done | bytes 272
  2948.6 35.3 %reduce-scatter.29.cloned.1.call-done = f32[256,128]{1,0:T(8,128)} async-done(((f32[256,1024]{1,0:T(8,128)}), f32[256,128]{1,0:T(8,128)}) %reduce-scatter.29.cloned.1.call-update) | async-done | bytes 131088 | tf_op jit(solution)/shard_map/reduce_scatter | solution.py:213
  2983.9 55.5 %reduce-scatter.33.cloned.1.call-done = f32[128,1024]{1,0:T(8,128)} async-done(((f32[1024,1024]{1,0:T(8,128)}), f32[128,1024]{1,0:T(8,128)}) %reduce-scatter.33.cloned.1.call-update) | async-done | bytes 524304 | tf_op jit(solution)/shard_map/reduce_scatter | solution.py:214
  3039.4 55.3 %reduce-scatter.37.cloned.1.call-done = f32[1024,128]{1,0:T(8,128)} async-done(((f32[1024,1024]{1,0:T(8,128)}), f32[1024,128]{1,0:T(8,128)}) %reduce-scatter.37.cloned.1.call-update) | async-done | bytes 524304 | tf_op jit(solution)/shard_map/reduce_scatter | solution.py:216
  (264 shorter events, 659.9 us)
Async XLA Ops:
  7.2 163.4 %all-gather.14.cloned.1.call-start = ((), (), s32[]{:S(2)}) async-start(), calls=%async_computation.13 | async-start | bytes 1769472 | tf_op jit(solution)/shard_map/all_gather | solution.py:91
  7.9 290.7 %all-gather.12.cloned.1.call-start = ((), (), s32[]{:S(2)}) async-start(), calls=%async_computation.12 | async-start | bytes 10567680 | tf_op jit(solution)/shard_map/all_gather | solution.py:111
  149.7 322.7 %all-gather.16.cloned.1.call-start = ((), (), s32[]{:S(2)}) async-start(), calls=%async_computation.15 | async-start | bytes 2359296 | tf_op jit(solution)/shard_map/all_gather | solution.py:94
  150.5 479.5 %all-gather.20.cloned.1.call-start = ((), (), s32[]{:S(2)}) async-start(), calls=%async_computation.17 | async-start | bytes 2359296 | tf_op jit(solution)/shard_map/all_gather | solution.py:96
  151.1 603.8 %reduce-scatter.23.cloned.1.call-start = ((), (), s32[]{:S(2)}) async-start(), calls=%async_computation.14 | async-start | bytes 21135360 | tf_op jit(solution)/shard_map/reduce_scatter | solution.py:123
  472.4 433.9 %all-gather.18.cloned.1.call-start = ((), (), s32[]{:S(2)}) async-start(), calls=%async_computation.16 | async-start | bytes 10485760 | tf_op jit(solution)/shard_map/all_gather | solution.py:128
  473.0 582.7 %all-gather.22.cloned.1.call-start = ((), (), s32[]{:S(2)}) async-start(), calls=%async_computation.18 | async-start | bytes 10485760 | tf_op jit(solution)/shard_map/all_gather | solution.py:130
  629.9 469.9 %copy-start.22 = (f32[3,344]{1,0:T(4,128)}, f32[3,344]{1,0:T(4,128)S(1)}, u32[]{:S(2)}) copy-start(f32[3,344]{1,0:T(4,128)S(1)} %compare_convert_fusion) | copy-start | bytes 12388
  629.9 469.9 %copy-start.30 = (f32[1,1024]{1,0:T(1,128)}, f32[1,1024]{1,0:T(1,128)S(1)}, u32[]{:S(2)}) copy-start(f32[1,1024]{1,0:T(1,128)S(1)} %get-tuple-element.241) | copy-start | bytes 12292
  630.0 641.3 %all-gather.24.cloned.1.call-start = ((), (), s32[]{:S(2)}) async-start(), calls=%async_computation.19 | async-start | bytes 10567680 | tf_op jit(solution)/shard_map/all_gather | solution.py:172
  1122.2 672.3 %reduce-scatter.25.cloned.1.call-start = ((), (), s32[]{:S(2)}) async-start(), calls=%async_computation.20 | async-start | bytes 21135360 | tf_op jit(solution)/shard_map/reduce_scatter | solution.py:199
  1513.7 564.0 %reduce-scatter.31.cloned.1.call-start = ((), (), s32[]{:S(2)}) async-start(), calls=%async_computation.23 | async-start | bytes 20971520 | tf_op jit(solution)/shard_map/reduce_scatter | solution.py:161
  1533.4 827.9 %reduce-scatter.35.cloned.1.call-start = ((), (), s32[]{:S(2)}) async-start(), calls=%async_computation.25 | async-start | bytes 20971520 | tf_op jit(solution)/shard_map/reduce_scatter | solution.py:163
  1552.6 946.0 %reduce-scatter.43.cloned.1.call-start = ((), (), s32[]{:S(2)}) async-start(), calls=%async_computation.29 | async-start | bytes 540672
  1554.3 1077.0 %reduce-scatter.45.cloned.1.call-start = ((), (), s32[]{:S(2)}) async-start(), calls=%async_computation.30 | async-start | bytes 540672
  1555.5 1122.6 %reduce-scatter.27.cloned.1.call-start = ((), (), s32[]{:S(2)}) async-start(), calls=%async_computation.21 | async-start | bytes 3538944 | tf_op jit(solution)/shard_map/reduce_scatter | solution.py:211
  1567.6 1246.8 %reduce-scatter.41.cloned.1.call-start = ((), (), s32[]{:S(2)}) async-start(), calls=%async_computation.28 | async-start | bytes 540672
  1799.8 1147.5 %reduce-scatter.39.cloned.1.call-start = ((), (), s32[]{:S(2)}) async-start(), calls=%async_computation.27 | async-start | bytes 540672
  1800.9 1183.0 %reduce-scatter.29.cloned.1.call-start = ((), (), s32[]{:S(2)}) async-start(), calls=%async_computation.22 | async-start | bytes 1179648 | tf_op jit(solution)/shard_map/reduce_scatter | solution.py:213
  1809.5 551.8 %copy-start.44 = (u32[32]{0:T(128)S(1)}, u32[32]{0:T(128)}, u32[]{:S(2)}) copy-start(u32[32]{0:T(128)} %constant.142) | copy-start | bytes 388
  1809.5 552.4 %copy-start.43 = (u32[32]{0:T(128)S(1)}, u32[32]{0:T(128)}, u32[]{:S(2)}) copy-start(u32[32]{0:T(128)} %constant.138) | copy-start | bytes 388
  1809.5 554.3 %copy-start.19 = (f32[4096]{0:T(1024)S(1)}, f32[4096]{0:T(1024)}, u32[]{:S(2)}) copy-start(f32[4096]{0:T(1024)} %get-tuple-element.251) | copy-start | bytes 49156
  1809.6 1229.9 %reduce-scatter.33.cloned.1.call-start = ((), (), s32[]{:S(2)}) async-start(), calls=%async_computation.24 | async-start | bytes 4718592 | tf_op jit(solution)/shard_map/reduce_scatter | solution.py:214
  2077.8 1016.9 %reduce-scatter.37.cloned.1.call-start = ((), (), s32[]{:S(2)}) async-start(), calls=%async_computation.26 | async-start | bytes 4718592 | tf_op jit(solution)/shard_map/reduce_scatter | solution.py:216
  (40 other events, 3444.6 us)
Sparse Core Ops, SparseCore 0:
  9.9 28.3 all-gather.13
  149.9 148.6 all-gather.11
  300.5 26.0 all-gather.15
  328.3 28.1 all-gather.19
  472.5 282.2 reduce-scatter.22
  756.2 149.9 all-gather.17
  907.8 147.8 all-gather.21
  1122.3 148.9 all-gather.23
  1513.9 280.5 reduce-scatter.24
  1796.7 281.0 reduce-scatter.30
  2080.3 281.0 reduce-scatter.34
  2363.4 135.1 reduce-scatter.42
  2501.0 130.3 reduce-scatter.44
  2635.1 42.9 reduce-scatter.26
  2680.3 134.1 reduce-scatter.40
  2816.6 130.6 reduce-scatter.38
  2951.2 32.6 reduce-scatter.28
  2988.1 51.3 reduce-scatter.32
  3043.3 51.2 reduce-scatter.36
where the time goes:
time: 3110 us; the launch traced here: 3100 us
  waiting for transfers between devices  2090 us (67%)
  matrix products  470 us (15%)
  blocking collectives  350 us (11%)
  other arithmetic  120 us (4%)
  local copies, waits for them, and re-layouts  55.1 us (2%)
    unnamed x23, waiting for transfers between devices  511 us
    reduce_scatter x1, waiting for transfers between devices, body(): lax.psum_scatter(grad_fc2_full, 'tensor', scatter_dimension=0, tiled=True)  283 us
    reduce_scatter x1, waiting for transfers between devices, body(): lax.psum_scatter(grad_fc1_full, 'tensor', scatter_dimension=1, tiled=True)  268 us
    reduce_scatter x1, waiting for transfers between devices, body(): lax.psum_scatter(jnp.einsum('kisc,kdc->isd', grad_proj, wqkv_all, preferr...  227 us
    all_gather x1, waiting for transfers between devices, body(): grad_attn_all = lax.all_gather(grad_attn_b, 'tensor', axis=1, tiled=True)  149 us
    all_gather x1, waiting for transfers between devices, body(): lax.all_gather(wfc1_all, 'tensor', axis=1, tiled=True)  146 us
    all_gather x1, waiting for transfers between devices, body(): normed1_all = lax.all_gather(normed1, 'tensor', axis=1, tiled=True)  128 us
    reduce_scatter x1, waiting for transfers between devices, body(): lax.psum_scatter(attn_part, 'tensor', scatter_dimension=1, tiled=True)  124 us
  transfers between devices with their start and end apart: 19, of which 16 were waited for; matrix products, arithmetic and copies ran while one was open for 11% of the time, Pallas kernels for 0%

commit v1 on v0

v1 whole, which is shorter than its diff:
```python
import functools
import math

import jax
import jax.numpy as jnp
from jax import lax
from jax.experimental import pallas as pl
from jax.experimental.pallas import tpu as pltpu
from jax.sharding import PartitionSpec as P

HD = 64
LANES = 128
LOG2E = math.log2(math.e)
NEG = -1e30
NT = (((1,), (1,)), ((), ()))
NN = (((1,), (0,)), ((), ()))
f32 = jnp.float32
bf16 = jnp.bfloat16


def round_up(n, m):
    return (n + m - 1) // m * m


def parts(x):
    hi = x.astype(bf16).astype(f32)
    rest = x - hi
    mid = rest.astype(bf16).astype(f32)
    return hi, mid, rest - mid


def keys_with_bias(keys, lane, row, length, own, spare):
    bias = jnp.where(row < length, 0.0, NEG)
    ones = jnp.where((lane >= spare) & (lane < spare + 3), 1.0, 0.0)
    return jnp.where(own, keys, jnp.where(lane == spare + 3, bias, ones)).astype(bf16)


def attend_forward_kernel(rows, padded, len_ref, q_ref, k_ref, v_ref, ctx_ref, qa_ref, ka, va):
    length = len_ref[0]
    lane = lax.broadcasted_iota(jnp.int32, (padded, LANES), 1)
    row = lax.broadcasted_iota(jnp.int32, (padded, LANES), 0)
    lb = lane[:rows]
    if padded > rows:
        va[rows:] = jnp.zeros((padded - rows, LANES), bf16)
    for half in range(2):
        own = (lb < HD) if half == 0 else (lb >= HD)
        spare = HD if half == 0 else 0
        ka[:rows] = keys_with_bias(k_ref[...].astype(f32), lb, row[:rows], length, own, spare)
        if padded > rows:
            ka[rows:] = jnp.where(lane[rows:] == spare + 3, NEG, 0.0).astype(bf16)
        va[:rows] = jnp.where(
            own, v_ref[...].astype(f32), jnp.where(lb == spare, 1.0, 0.0)
        ).astype(bf16)
        qa = jnp.where(own, q_ref[...].astype(f32), jnp.where(lb == spare + 3, 1.0, 0.0))
        s = lax.dot_general(qa.astype(bf16), ka[...], NT, preferred_element_type=f32)
        m = jnp.max(s, axis=1, keepdims=True)
        p = jnp.exp2(s - m).astype(bf16)
        o = lax.dot_general(p, va[...], NN, preferred_element_type=f32)
        total = o[:, spare : spare + 1]
        o = o / total
        hi, mid, lo = parts(-(m + jnp.log2(total)))
        if half == 0:
            ctx_ref[...] = o.astype(bf16)
        else:
            ctx_ref[...] = jnp.where(own, o, ctx_ref[...].astype(f32)).astype(bf16)
        stats = jnp.where(lb == spare + 2, lo, qa)
        stats = jnp.where(lb == spare + 1, mid, stats)
        qa_ref[half] = jnp.where(lb == spare, hi, stats).astype(bf16)


def attend_forward(length, q, k, v):
    rows, width = q.shape
    padded = round_up(rows, LANES)
    spec = pl.BlockSpec((rows, LANES), lambda j: (0, j))
    return pl.pallas_call(
        functools.partial(attend_forward_kernel, rows, padded),
        grid=(width // LANES,),
        in_specs=[pl.BlockSpec(memory_space=pltpu.SMEM), spec, spec, spec],
        out_specs=[spec, pl.BlockSpec((2, rows, LANES), lambda j: (j, 0, 0))],
        out_shape=[
            jax.ShapeDtypeStruct((rows, width), bf16),
            jax.ShapeDtypeStruct((width // HD, rows, LANES), bf16),
        ],
        scratch_shapes=[pltpu.VMEM((padded, LANES), bf16), pltpu.VMEM((padded, LANES), bf16)],
        compiler_params=pltpu.CompilerParams(vmem_limit_bytes=56 * 2**20),
        cost_estimate=pl.CostEstimate(
            flops=16 * rows * rows * width,
            bytes_accessed=12 * rows * width,
            transcendentals=rows * rows * width // HD,
        ),
        name="attend_forward",
    )(length, q, k, v)


def attend_backward_kernel(
    rows,
    padded,
    blocks,
    len_ref,
    qa_ref,
    k_ref,
    v_ref,
    gc_ref,
    ctx_ref,
    gq_ref,
    gk_ref,
    gv_ref,
    ka,
    va,
    qs,
    ga,
    acc,
):
    length = len_ref[0]
    lane = lax.broadcasted_iota(jnp.int32, (padded, LANES), 1)
    row = lax.broadcasted_iota(jnp.int32, (padded, LANES), 0)
    size = rows // blocks
    ls = lane[:rows]
    for half in range(2):
        own = (ls < HD) if half == 0 else (ls >= HD)
        spare = HD if half == 0 else 0
        ownb = own[:size]
        gc = gc_ref[...].astype(f32)
        corr = jnp.sum(
            jnp.where(own, gc * ctx_ref[...].astype(f32), 0.0), axis=1, keepdims=True
        )
        hi, mid, lo = parts(-corr)
        extra = jnp.where(ls == spare + 1, mid, jnp.where(ls == spare + 2, lo, 0.0))
        ga[:rows] = jnp.where(own, gc, jnp.where(ls == spare, hi, extra)).astype(bf16)
        qs[:rows] = qa_ref[half]
        if padded > rows:
            ga[rows:] = jnp.zeros((padded - rows, LANES), bf16)
            qs[rows:] = jnp.where(lane[rows:] == spare, NEG, 0.0).astype(bf16)
        ka[...] = keys_with_bias(k_ref[...].astype(f32), ls, row[:rows], length, own, spare)
        ones = jnp.where((ls >= spare) & (ls < spare + 3), 1.0, 0.0)
        va[...] = jnp.where(own, v_ref[...].astype(f32), ones).astype(bf16)
        acc[...] = jnp.zeros_like(acc)

        def block(b, carry):
            r = pl.ds(pl.multiple_of(b * size, 16), size)
            kb = ka[r, :]
            p = jnp.exp2(lax.dot_general(kb, qs[...], NT, preferred_element_type=f32))
            gp = lax.dot_general(va[r, :], ga[...], NT, preferred_element_type=f32)
            ds = (p * gp).astype(bf16)
            gv = lax.dot_general(p.astype(bf16), ga[...], NN, preferred_element_type=f32)
            gk = lax.dot_general(ds, qs[...], NN, preferred_element_type=f32) * (1.0 / LOG2E)
            acc[...] += lax.dot_general(kb.T, ds, NN, preferred_element_type=f32)
            if half == 0:
                gv_ref[r, :] = gv.astype(bf16)
                gk_ref[r, :] = gk.astype(bf16)
            else:
                gv_ref[r, :] = jnp.where(ownb, gv, gv_ref[r, :].astype(f32)).astype(bf16)
                gk_ref[r, :] = jnp.where(ownb, gk, gk_ref[r, :].astype(f32)).astype(bf16)
            return carry

        lax.fori_loop(0, blocks, block, 0)
        gq = acc[...].T[:rows] * HD ** (-0.5)
        if half == 0:
            gq_ref[...] = gq.astype(bf16)
        else:
            gq_ref[...] = jnp.where(own, gq, gq_ref[...].astype(f32)).astype(bf16)


def attend_backward(length, qa, k, v, gc, ctx):
    rows, width = k.shape
    padded = round_up(rows, LANES)
    blocks = 2 if rows % 32 == 0 else 1
    spec = pl.BlockSpec((rows, LANES), lambda j: (0, j))
    return pl.pallas_call(
        functools.partial(attend_backward_kernel, rows, padded, blocks),
        grid=(width // LANES,),
        in_specs=[
            pl.BlockSpec(memory_space=pltpu.SMEM),
            pl.BlockSpec((2, rows, LANES), lambda j: (j, 0, 0)),
            spec,
            spec,
            spec,
            spec,
        ],
        out_specs=[spec] * 3,
        out_shape=[jax.ShapeDtypeStruct((rows, width), bf16)] * 3,
        scratch_shapes=[
            pltpu.VMEM((rows, LANES), bf16),
            pltpu.VMEM((rows, LANES), bf16),
            pltpu.VMEM((padded, LANES), bf16),
            pltpu.VMEM((padded, LANES), bf16),
            pltpu.VMEM((LANES, padded), f32),
        ],
        compiler_params=pltpu.CompilerParams(vmem_limit_bytes=56 * 2**20),
        cost_estimate=pl.CostEstimate(
            flops=40 * rows * rows * width,
            bytes_accessed=16 * rows * width,
            transcendentals=rows * rows * width // HD,
        ),
        name="attend_backward",
    )(length, qa, k, v, gc, ctx)


def feed_forward_kernel(
    n2_ref, n2t_ref, gm_ref, gmt_ref, w1_ref, b1_ref, w2_ref, mlp_ref, gn_ref, gw1_ref, gw2_ref, gb_ref
):
    step = pl.program_id(0)
    pre = lax.dot_general(n2_ref[...], w1_ref[...], NN, preferred_element_type=f32) + b1_ref[...]
    gact = lax.dot_general(gm_ref[...], w2_ref[...], NT, preferred_element_type=f32)
    cdf = 0.5 * (1.0 + lax.erf(pre * (1 / math.sqrt(2))))
    act = (pre * cdf).astype(bf16)
    pdf = jnp.exp2(pre * pre * (-0.5 * LOG2E)) * (1 / math.sqrt(2 * math.pi))
    gpre = gact * (cdf + pre * pdf)
    gb_ref[...] = jnp.sum(gpre, axis=0, keepdims=True)
    gpre = gpre.astype(bf16)
    mlp = lax.dot_general(act, w2_ref[...], NN, preferred_element_type=f32)
    gn = lax.dot_general(gpre, w1_ref[...], NT, preferred_element_type=f32)

    @pl.when(step == 0)
    def _():
        mlp_ref[...] = mlp
        gn_ref[...] = gn

    @pl.when(step > 0)
    def _():
        mlp_ref[...] += mlp
        gn_ref[...] += gn

    gw1_ref[...] = lax.dot_general(
        n2t_ref[...], gpre, NN, preferred_element_type=f32
    ).astype(bf16)
    gw2_ref[...] = lax.dot_general(
        gmt_ref[...], act, NN, preferred_element_type=f32
    ).astype(bf16)


def feed_forward(n2, n2t, gm, gmt, w1, b1, w2):
    rows, width = n2.shape
    units = w1.shape[1]
    tile = 512

    def whole(a, b):
        return pl.BlockSpec((a, b), lambda j: (0, 0), pipeline_mode=pl.Buffered(1))

    return pl.pallas_call(
        feed_forward_kernel,
        grid=(units // tile,),
        in_specs=[
            whole(rows, width),
            whole(width, rows),
            whole(rows, width),
            whole(width, rows),
            pl.BlockSpec((width, tile), lambda j: (0, j)),
            pl.BlockSpec((1, tile), lambda j: (0, j)),
            pl.BlockSpec((tile, width), lambda j: (j, 0)),
        ],
        out_specs=[
            whole(rows, width),
            whole(rows, width),
            pl.BlockSpec((width, tile), lambda j: (0, j)),
            pl.BlockSpec((width, tile), lambda j: (0, j)),
            pl.BlockSpec((1, tile), lambda j: (0, j)),
        ],
        out_shape=[
            jax.ShapeDtypeStruct((rows, width), f32),
            jax.ShapeDtypeStruct((rows, width), f32),
            jax.ShapeDtypeStruct((width, units), bf16),
            jax.ShapeDtypeStruct((width, units), bf16),
            jax.ShapeDtypeStruct((1, units), f32),
        ],
        compiler_params=pltpu.CompilerParams(vmem_limit_bytes=60 * 2**20),
        cost_estimate=pl.CostEstimate(
            flops=16 * rows * width * units,
            bytes_accessed=8 * width * units,
            transcendentals=2 * rows * units,
        ),
        name="feed_forward",
    )(n2, n2t, gm, gmt, w1, b1, w2)


def norm_rows(values, gain, shift):
    center = values - jnp.mean(values, axis=-1, keepdims=True)
    inverse = lax.rsqrt(jnp.mean(center * center, axis=-1, keepdims=True) + 1e-06)
    normed = center * inverse
    return normed * gain + shift, normed, inverse


def norm_back(grad_norm, normed, inverse, gain):
    scaled = grad_norm * gain
    return inverse * (
        scaled
        - jnp.mean(scaled, axis=-1, keepdims=True)
        - normed * jnp.mean(scaled * normed, axis=-1, keepdims=True)
    )


def body(
    block_input,
    cotangent,
    lengths,
    w_qkv,
    b_qv,
    w_out,
    w_fc1,
    b_fc1,
    w_fc2,
    ln_gain,
    ln_shift,
    layer_scale,
    out_bias,
):
    images, part_rows, width = block_input.shape
    groups = lax.axis_size("dp")
    line = lax.axis_size("tensor")
    rows = part_rows * line
    group = lax.axis_index("dp")
    place = lax.axis_index("tensor")
    flip = group % 2
    mine = jnp.where(flip == 1, line - 1 - place, place)
    active = mine < images

    def image_of(g, z):
        return line - 1 - z if g % 2 else z

    def to_owner(x):
        own = jnp.where(active, x[jnp.minimum(mine, images - 1)], jnp.zeros_like(x[0]))
        out = jnp.zeros((rows, width), x.dtype)
        out = lax.dynamic_update_slice(out, own, (place * part_rows, 0))
        for shift in range(1, line):
            pairs = [
                (g * line + z, g * line + (z + shift) % line)
                for g in range(groups)
                for z in range(line)
                if image_of(g, (z + shift) % line) < images
            ]
            to = (place + shift) % line
            image = jnp.where(flip == 1, line - 1 - to, to)
            sent = lax.ppermute(x[jnp.minimum(image, images - 1)], ("dp", "tensor"), pairs)
            out = lax.dynamic_update_slice(
                out, sent, (((place - shift) % line) * part_rows, 0)
            )
        return out

    def from_owner(y):
        split = y.reshape(line, part_rows, width)
        arrived = [split[place]]
        for shift in range(1, line):
            pairs = [
                (g * line + z, g * line + (z + shift) % line)
                for g in range(groups)
                for z in range(line)
                if image_of(g, z) < images
            ]
            arrived.append(lax.ppermute(split[(place + shift) % line], ("dp", "tensor"), pairs))
        stacked = jnp.stack(arrived)
        out = []
        for i in range(images):
            source = jnp.where(flip == 1, line - 1 - i, i)
            out.append(stacked[(place - source) % line])
        return jnp.stack(out)

    small = jnp.concatenate(
        [
            ln_gain.reshape(-1),
            ln_shift.reshape(-1),
            layer_scale.reshape(-1),
            out_bias.reshape(-1),
            b_qv.astype(f32).reshape(-1),
            b_fc1.astype(f32).reshape(-1),
        ]
    )[None]
    small = lax.all_gather(small, "tensor", axis=0, tiled=False)
    small = lax.all_gather(small, "dp", axis=0, tiled=False).reshape(groups, line, -1)
    own_width = ln_gain.shape[1]
    at = 0

    def take(count):
        nonlocal at
        at += count
        return small[:, :, at - count : at]

    def vectors(x):
        return jnp.transpose(x.reshape(groups, line, 2, own_width), (2, 0, 1, 3)).reshape(2, width)

    gains = vectors(take(2 * own_width))
    shifts = vectors(take(2 * own_width))
    scales = vectors(take(2 * own_width))
    biases = vectors(take(2 * own_width))
    _, bq_rows, bq_cols = b_qv.shape
    qv_bias = jnp.transpose(
        take(2 * bq_rows * bq_cols).reshape(groups, line, 2, bq_rows, bq_cols), (2, 1, 4, 0, 3)
    ).reshape(2, width)
    f_rows, f_cols = b_fc1.shape
    fc1_bias = jnp.transpose(
        take(f_rows * f_cols).reshape(groups, line, f_rows, f_cols), (1, 3, 0, 2)
    ).reshape(1, -1)

    x_all = to_owner(block_input)
    wqkv = lax.all_gather(
        lax.all_gather(w_qkv, "tensor", axis=2, tiled=True), "dp", axis=1, tiled=True
    )
    wout = lax.all_gather(
        lax.all_gather(w_out, "tensor", axis=0, tiled=True), "dp", axis=1, tiled=True
    )
    wfc1 = lax.all_gather(
        lax.all_gather(w_fc1, "tensor", axis=1, tiled=True), "dp", axis=0, tiled=True
    )
    wfc2 = lax.all_gather(
        lax.all_gather(w_fc2, "tensor", axis=0, tiled=True), "dp", axis=1, tiled=True
    )
    cot = to_owner(cotangent)

    length = jnp.where(active, lengths[jnp.minimum(mine, images - 1)], 0).astype(jnp.int32)
    length_array = length.reshape(1)
    valid = (jnp.arange(rows, dtype=jnp.int32) < length).astype(f32)[:, None]

    source = x_all.astype(f32)
    normed_one, hat_first, inv_first = norm_rows(source, gains[0], shifts[0])
    normed1 = normed_one.astype(bf16)
    scale_q = HD ** (-0.5) * LOG2E

    def dot(a, b, dims=NN):
        return lax.dot_general(a, b, dims, preferred_element_type=f32)

    query = ((dot(normed1, wqkv[0]) + qv_bias[0]) * scale_q).astype(bf16)
    key = dot(normed1, wqkv[1]).astype(bf16)
    value = (dot(normed1, wqkv[2]) + qv_bias[1]).astype(bf16)
    context, query_stats = attend_forward(length_array, query, key, value)
    attn = dot(context, wout) + biases[0]
    hidden = source + scales[0] * attn
    normed_two, hat_second, inv_second = norm_rows(hidden, gains[1], shifts[1])
    normed2 = normed_two.astype(bf16)
    grad_out = valid * cot.astype(f32)
    grad_mlp = grad_out * scales[1]
    grad_mlp_b = grad_mlp.astype(bf16)
    mlp, grad_normed2, grad_fc1, grad_fc2, grad_bfc1 = feed_forward(
        normed2, normed2.T, grad_mlp_b, grad_mlp_b.T, wfc1, fc1_bias, wfc2
    )
    mlp = mlp + biases[1]
    block_out = from_owner((valid * (hidden + scales[1] * mlp)).astype(bf16))

    def reduced(grad):
        part = lax.psum_scatter(grad, "dp", scatter_dimension=0, tiled=True)
        return lax.psum_scatter(part, "tensor", scatter_dimension=1, tiled=True).astype(f32)

    shard_fc1 = reduced(grad_fc1)
    shard_fc2 = reduced(grad_fc2).T

    grad_scale2 = jnp.sum(grad_out * mlp, axis=0)
    grad_bias2 = jnp.sum(grad_mlp, axis=0)
    grad_gain2 = jnp.sum(grad_normed2 * hat_second, axis=0)
    grad_shift2 = jnp.sum(grad_normed2, axis=0)
    grad_hidden = grad_out + norm_back(grad_normed2, hat_second, inv_second, gains[1])
    grad_scale1 = jnp.sum(grad_hidden * attn, axis=0)
    grad_attn = grad_hidden * scales[0]
    grad_bias1 = jnp.sum(grad_attn, axis=0)
    grad_attn_b = grad_attn.astype(bf16)
    grad_context = dot(grad_attn_b, wout, NT).astype(bf16)
    grad_wout = dot(grad_attn_b.T, context).astype(bf16)
    shard_wout = reduced(grad_wout).T
    grad_query, grad_key, grad_value = attend_backward(
        length_array, query_stats, key, value, grad_context, context
    )
    grad_bq = jnp.sum(grad_query.astype(f32), axis=0)
    grad_bv = jnp.sum(grad_value.astype(f32), axis=0)
    normed1_t = normed1.T
    grad_wqkv = [dot(normed1_t, g).astype(bf16) for g in (grad_query, grad_key, grad_value)]
    shard_wqkv = jnp.stack([reduced(g) for g in grad_wqkv])
    grad_normed1 = (
        dot(grad_query, wqkv[0], NT) + dot(grad_key, wqkv[1], NT) + dot(grad_value, wqkv[2], NT)
    )
    grad_gain1 = jnp.sum(grad_normed1 * hat_first, axis=0)
    grad_shift1 = jnp.sum(grad_normed1, axis=0)
    grad_source = grad_hidden + norm_back(grad_normed1, hat_first, inv_first, gains[0])
    grad_input = from_owner(grad_source.astype(bf16)).astype(f32)

    small_grads = jnp.concatenate(
        [
            grad_gain1,
            grad_gain2,
            grad_shift1,
            grad_shift2,
            grad_scale1,
            grad_scale2,
            grad_bias1,
            grad_bias2,
            grad_bq,
            grad_bv,
            grad_bfc1.reshape(-1),
        ]
    ).reshape(-1, width)
    small_grads = lax.psum(lax.psum(small_grads, "tensor"), "dp")

    def own_columns(x):
        return lax.dynamic_slice_in_dim(x, (group * line + place) * own_width, own_width, 1)

    shard_gain, shard_shift, shard_scale, shard_bias = (
        own_columns(small_grads[2 * n : 2 * n + 2]) for n in range(4)
    )
    by_head = small_grads[8:10].reshape(2, line, bq_cols, groups, bq_rows)
    shard_bqv = jnp.transpose(by_head[:, place, :, group], (0, 2, 1))
    by_unit = small_grads[10:].reshape(line, f_cols, groups, f_rows)
    shard_bfc1 = by_unit[place, :, group].T
    return (
        block_out,
        grad_input,
        shard_wqkv,
        shard_bqv,
        shard_wout,
        shard_fc1,
        shard_bfc1,
        shard_fc2,
        shard_gain,
        shard_shift,
        shard_scale,
        shard_bias,
    )


def solution(mesh):
    rows = P("dp", "tensor", None)
    vector = P(None, ("dp", "tensor"))
    weights = (
        P(None, "dp", "tensor"),
        P(None, "dp", "tensor"),
        P("tensor", "dp"),
        P("dp", "tensor"),
        P("dp", "tensor"),
        P("tensor", "dp"),
    )
    return jax.shard_map(
        body,
        mesh=mesh,
        in_specs=(rows, rows, P("dp")) + weights + (vector,) * 4,
        out_specs=(rows, rows) + weights + (vector,) * 4,
        check_vma=False,
    )
```

time: 3110 us -> 1060 us (0.34)
  waiting for transfers between devices: 2090 us -> 289 us
  matrix products: 470 us -> 88.4 us
  Pallas kernels: 0 us -> 252 us
  blocking collectives: 350 us -> 150 us
  local copies, waits for them, and re-layouts: 55.1 us -> 147 us
  other arithmetic: 120 us -> 61.9 us
  starting transfers between devices: 1.49 us -> 44.9 us
    reduce_scatter x8 -> x12, waiting for transfers between devices: 1070 us -> 258 us  [the longest x6 143 us: reduced(): part = lax.psum_scatter(grad, 'dp', scatter_dimension=0, tiled=True)]
    unnamed x23 -> x18, waiting for transfers between devices: 511 us -> 3.3 us
    all_gather x7 -> x6, waiting for transfers between devices: 507 us -> 24.2 us  [the longest x1 24.1 us: body(): lax.all_gather(w_fc2, 'tensor', axis=0, tiled=True)]
    dot_general x33 -> x12, matrix products: 470 us -> 88.4 us  [dot(): return lax.dot_general(a, b, dims, preferred_element_type=f32)]
    all_gather x8 -> x3, blocking collectives: 309 us -> 55.6 us  [the longest x1 27.2 us: body(): lax.all_gather(w_qkv, 'tensor', axis=2, tiled=True)]
    pallas_call x0 -> x3, Pallas kernels: none -> 252 us  [the longest x1 104 us: attend_backward(): pl.pallas_call(functools.partial(attend_backward_kernel, rows, padded, bl...]
    dynamic_update_slice x0 -> x8, local copies, waits for them, and re-layouts: none -> 74.8 us  [the longest x6 57.8 us: to_owner(): lax.dynamic_update_slice(out, sent, ((place - shift) % line * part_rows, 0))]
    ppermute x0 -> x12, starting transfers between devices: none -> 43.9 us  [the longest x6 24.3 us: to_owner(): lax.ppermute(x[jnp.minimum(image, images - 1)], ('dp', 'tensor'), pairs)]
  transfers between devices with their start and end apart: 19 -> 30, of which waited for: 16 -> 12; matrix products, arithmetic and copies ran while one was open for 11% -> 24% of each run, Pallas kernels for 0% -> 15%
where the time goes in v1:
time: 1060 us; the launch traced here: 1050 us
  waiting for transfers between devices  289 us (27%)
  Pallas kernels  252 us (24%)
  blocking collectives  150 us (14%)
  local copies, waits for them, and re-layouts  147 us (14%)
  matrix products  88.4 us (8%)
  other arithmetic  61.9 us (6%)
  starting transfers between devices  44.9 us (4%)
  between operations  17.1 us (2%)
    reduce_scatter x6, waiting for transfers between devices, reduced(): part = lax.psum_scatter(grad, 'dp', scatter_dimension=0, tiled=True)  143 us
    reduce_scatter x6, waiting for transfers between devices, reduced(): lax.psum_scatter(part, 'tensor', scatter_dimension=1, tiled=True)  115 us
    pallas_call x1, Pallas kernels, attend_backward(): pl.pallas_call(functools.partial(attend_backward_kernel, rows, padded, bl...  104 us
    pallas_call x1, Pallas kernels, feed_forward(): pl.pallas_call(feed_forward_kernel, grid=(units // tile,), in_specs=[whol...  93.6 us
    dot_general x12, matrix products, dot(): return lax.dot_general(a, b, dims, preferred_element_type=f32)  88.4 us
    dynamic_update_slice x6, local copies, waits for them, and re-layouts, to_owner(): lax.dynamic_update_slice(out, sent, ((place - shift) % line * part_rows, 0))  57.8 us
    pallas_call x1, Pallas kernels, attend_forward(): pl.pallas_call(functools.partial(attend_forward_kernel, rows, padded), gr...  54.8 us
    unnamed x1, blocking collectives  50.6 us
  transfers between devices with their start and end apart: 30, of which 12 were waited for; matrix products, arithmetic and copies ran while one was open for 24% of the time, Pallas kernels for 15%

profile of v1, /device:TPU:0, one launch (start us, length us, event | category | flops | bytes accessed | tf_op | source)
XLA Modules:
  0.0 1051.4 jit_solution(18331499273175396705)
XLA Ops:
  8.7 27.2 %all_gather.36 = bf16[3,128,1024]{2,1,0:T(8,128)(2,1)} all-gather(bf16[3,128,256]{2,1,0:T(8,128)(2,1)} %param.16), channel_id=1, replica_groups=mesh['dp'=8,'tensor'=4] {'tensor'}, dimensions={2}, use_global_device_ids=true | all-gather | bytes 983040 | tf_op jit(solution)/shard_map/all_gather | solution.py:395
  36.0 17.9 %all_gather.38 = bf16[1024,128]{1,0:T(8,128)(2,1)} all-gather(bf16[256,128]{1,0:T(8,128)(2,1)} %param.18), channel_id=1, replica_groups=mesh['dp'=8,'tensor'=4] {'tensor'}, dimensions={0}, use_global_device_ids=true | all-gather | bytes 327680 | tf_op jit(solution)/shard_map/all_gather | solution.py:398
  54.6 24.1 %all-gather.17.cloned.1.call-done = bf16[4096,128]{1,0:T(8,128)(2,1)} async-done(((bf16[1024,128]{1,0:T(8,128)(2,1)}), bf16[4096,128]{1,0:T(8,128)(2,1)}) %all-gather.17.cloned.1.call-update) | async-done | bytes 1048592 | tf_op jit(solution)/shard_map/all_gather | solution.py:404
  97.8 50.6 %all-reduce = f32[1792]{0:T(1024)S(1)} all-reduce(f32[1792]{0:T(1024)S(1)} %dynamic-update-slice), channel_id=2, replica_groups=mesh['dp'=8,'tensor'=4] {'tensor'}, use_global_device_ids=true, to_apply=%add | all-reduce | flops 1792 | bytes 14336
  148.5 10.5 all-gather.1
  162.9 10.4 collective-permute-start.1
  252.1 10.4 dynamic_update_slice.26
  264.7 10.6 %dynamic_update_slice.27 = bf16[1376,1024]{0,1:T(8,128)(2,1)S(1)} dynamic-update-slice(bf16[1376,1024]{0,1:T(8,128)(2,1)S(1)} %dynamic_update_slice.26, bf16[344,1024]{0,1:T(8,128)(2,1)} %copy.118, s32[]{:T(128)S(6)} %select_n.218, s32[]{:T(128)} %constant.113.clone.1) | dynamic-update-slice | bytes 1409028 | tf_op jit(solution)/shard_map/dynamic_update_slice | solution.py:334
  298.3 54.8 %attend_forward.1 = (bf16[1376,1024]{1,0:T(8,128)(2,1)}, bf16[16,1376,128]{2,1,0:T(8,128)(2,1)}) custom-call(s32[1]{0:T(128)} %bitcast.7.len_ref, bf16[1376,1024]{1,0:T(8,128)(2,1)} %multiply_convert_fusion.1.q_ref, bf16[1376,1024]{1,0:T(8,128)(2,1)} %convolution_convert_fusion.1.k_ref, bf16[1376,1024]{1,0:T(8,128)(2,1)} %add_convert_fusion.1.v_ref), custom_call_target="tpu_custom_call" | custom-call | flops 31021072384 | bytes 16908288 | tf_op jit(solution)/shard_map/attend_forward/pallas_call | solution.py:75
  373.4 93.6 %feed_forward.1 = (f32[1376,1024]{1,0:T(8,128)}, f32[1376,1024]{1,0:T(8,128)}, bf16[1024,4096]{1,0:T(8,128)(2,1)}, bf16[1024,4096]{1,0:T(8,128)(2,1)}, f32[1,4096]{1,0:T(1,128)}) custom-call(bf16[1376,1024]{1,0:T(8,128)(2,1)} %copy.134.n2_ref, bf16[1024,1376]{1,0:T(8,128)(2,1)} %fusion.46.n2t_ref, bf16[1376,1024]{1,0:T(8,128)(2,1)} %copy.135.gm_ref, ...), custom_call_target="tpu_custom_call" | custom-call | flops 92341796864 | bytes 33554432 | tf_op jit(solution)/shard_map/feed_forward/pallas_call | solution.py:240
  485.4 13.0 %fusion.16 = (f32[1024]{0:T(1024)}, f32[1024]{0:T(1024)}, bf16[1376,1024]{0,1:T(8,128)(2,1)}, f32[1024]{0:T(1024)}, f32[1024]{0:T(1024)}, /*index=5*/f32[1376,1024]{0,1:T(8,128)S(1)}) fusion(bf16[1376,1024]{0,1:T(8,128)(2,1)} %dynamic_update_slice.31, f32[1024]{0:T(1024)S(1)} %copy-done.13, f32[1376]{0:T(1024)S(1)} %copy-done.9, f32[1376,1024]{0,1:T(8,128)} %copy.136, ...), kind=kLoop, calls=%fused_computation.27 | loop fusion | flops 33812480 | bytes 33880960 | tf_op jit(solution)/shard_map/reduce_sum | solution.py:445
  514.1 103.9 %attend_backward.1 = (bf16[1376,1024]{1,0:T(8,128)(2,1)}, bf16[1376,1024]{1,0:T(8,128)(2,1)}, bf16[1376,1024]{1,0:T(8,128)(2,1)}) custom-call(s32[1]{0:T(128)} %bitcast.7.len_ref, bf16[16,1376,128]{2,1,0:T(8,128)(2,1)} %get-tuple-element.25.qa_ref, bf16[1376,1024]{1,0:T(8,128)(2,1)} %convolution_convert_fusion.1.k_ref, ...), custom_call_target="tpu_custom_call" | custom-call | flops 77552680960 | bytes 22544384 | tf_op jit(solution)/shard_map/attend_backward/pallas_call | solution.py:169
  675.6 13.4 %fusion.13 = (f32[1024]{0:T(1024)S(1)}, f32[1376]{0:T(1024)S(1)}, f32[1376]{0:T(1024)S(1)}, f32[1024]{0:T(1024)S(1)}, f32[1376,1024]{0,1:T(8,128)}) fusion(bf16[1376,1024]{0,1:T(8,128)(2,1)S(1)} %copy-done.2, f32[1376]{0:T(1024)S(1)} %copy-done.15, f32[1376]{0:T(1024)S(1)} %copy-done.11, f32[1024]{0:T(1024)S(1)} %copy-done.18, ...), kind=kOutput, calls=%fused_computation.16 | convolution fusion | flops 2902584832 | bytes 24937984 | tf_op jit(solution)/shard_map/dot_general | solution.py:418
  689.2 19.7 %reduce-scatter.13.cloned.1.call-done = bf16[128,1024]{1,0:T(8,128)(2,1)} async-done(((bf16[1024,1024]{1,0:T(8,128)(2,1)}), bf16[128,1024]{1,0:T(8,128)(2,1)}) %reduce-scatter.13.cloned.1.call-update) | async-done | bytes 262160 | tf_op jit(solution)/shard_map/reduce_scatter | solution.py:438
  713.8 40.4 %reduce-scatter.21.cloned.1.call-done = bf16[128,1024]{1,0:T(8,128)(2,1)} async-done(((bf16[1024,1024]{1,0:T(8,128)(2,1)}), bf16[128,1024]{1,0:T(8,128)(2,1)}) %reduce-scatter.21.cloned.1.call-update) | async-done | bytes 262160 | tf_op jit(solution)/shard_map/reduce_scatter | solution.py:438
  754.3 19.7 %psum.14 = f32[14,1024]{1,0:T(8,128)S(1)} all-reduce(f32[14,1024]{1,0:T(8,128)S(1)} %reshape.189), channel_id=1, replica_groups=mesh['dp'=8,'tensor'=4] {'tensor'}, use_global_device_ids=true, to_apply=%region_24.25 | all-reduce | flops 14336 | bytes 114688 | tf_op jit(solution)/shard_map/psum | solution.py:487
  774.1 54.9 %reduce-scatter.33.cloned.1.call-done = bf16[128,4096]{1,0:T(8,128)(2,1)} async-done(((bf16[1024,4096]{1,0:T(8,128)(2,1)}), bf16[128,4096]{1,0:T(8,128)(2,1)}) %reduce-scatter.33.cloned.1.call-update) | async-done | bytes 1048592 | tf_op jit(solution)/shard_map/reduce_scatter | solution.py:438
  835.7 24.1 %psum.15 = f32[14,1024]{1,0:T(8,128)} all-reduce(f32[14,1024]{1,0:T(8,128)S(1)} %psum.14), channel_id=1, replica_groups=mesh['dp'=8,'tensor'=4] {'dp'}, use_global_device_ids=true, to_apply=%region_25.26 | all-reduce | flops 14336 | bytes 114688 | tf_op jit(solution)/shard_map/psum | solution.py:487
  876.2 27.8 %reduce-scatter.29.cloned.1.call-done = bf16[128,4096]{1,0:T(8,128)(2,1)} async-done(((bf16[1024,4096]{1,0:T(8,128)(2,1)}), bf16[128,4096]{1,0:T(8,128)(2,1)}) %reduce-scatter.29.cloned.1.call-update) | async-done | bytes 1048592 | tf_op jit(solution)/shard_map/reduce_scatter | solution.py:438
  928.2 18.5 %reduce-scatter.19.cloned.1.call-done = bf16[128,256]{1,0:T(8,128)(2,1)} async-done(((bf16[128,1024]{1,0:T(8,128)(2,1)}), bf16[128,256]{1,0:T(8,128)(2,1)}) %reduce-scatter.19.cloned.1.call-update) | async-done | bytes 65552 | tf_op jit(solution)/shard_map/reduce_scatter | solution.py:439
  946.7 20.0 %reduce-scatter.15.cloned.1.call-done = bf16[128,256]{1,0:T(8,128)(2,1)} async-done(((bf16[128,1024]{1,0:T(8,128)(2,1)}), bf16[128,256]{1,0:T(8,128)(2,1)}) %reduce-scatter.15.cloned.1.call-update) | async-done | bytes 65552 | tf_op jit(solution)/shard_map/reduce_scatter | solution.py:439
  966.7 20.1 %reduce-scatter.23.cloned.1.call-done = bf16[128,256]{1,0:T(8,128)(2,1)} async-done(((bf16[128,1024]{1,0:T(8,128)(2,1)}), bf16[128,256]{1,0:T(8,128)(2,1)}) %reduce-scatter.23.cloned.1.call-update) | async-done | bytes 65552 | tf_op jit(solution)/shard_map/reduce_scatter | solution.py:439
  988.5 26.0 %reduce-scatter.35.cloned.1.call-done = bf16[128,1024]{1,0:T(8,128)(2,1)} async-done(((bf16[128,4096]{1,0:T(8,128)(2,1)}), bf16[128,1024]{1,0:T(8,128)(2,1)}) %reduce-scatter.35.cloned.1.call-update) | async-done | bytes 262160 | tf_op jit(solution)/shard_map/reduce_scatter | solution.py:439
  1016.4 26.1 %reduce-scatter.31.cloned.1.call-done = bf16[128,1024]{1,0:T(8,128)(2,1)} async-done(((bf16[128,4096]{1,0:T(8,128)(2,1)}), bf16[128,1024]{1,0:T(8,128)(2,1)}) %reduce-scatter.31.cloned.1.call-update) | async-done | bytes 262160 | tf_op jit(solution)/shard_map/reduce_scatter | solution.py:439
  (286 shorter events, 296.7 us)
Async XLA Ops:
  8.7 272.1 %all-gather.9.cloned.1.call-start = ((), (), s32[]{:S(2)}) async-start(), calls=%async_computation.12 | async-start | bytes 7077888 | tf_op jit(solution)/shard_map/all_gather | solution.py:394
  35.9 317.1 %all-gather.11.cloned.1.call-start = ((), (), s32[]{:S(2)}) async-start(), calls=%async_computation.13 | async-start | bytes 2359296 | tf_op jit(solution)/shard_map/all_gather | solution.py:397
  53.9 319.5 %all-gather.15.cloned.1.call-start = ((), (), s32[]{:S(2)}) async-start(), calls=%async_computation.15 | async-start | bytes 9437184 | tf_op jit(solution)/shard_map/all_gather | solution.py:400
  54.5 318.9 %all-gather.19.cloned.1.call-start = ((), (), s32[]{:S(2)}) async-start(), calls=%async_computation.17 | async-start | bytes 9437184 | tf_op jit(solution)/shard_map/all_gather | solution.py:403
  78.8 596.7 %reduce-scatter.25.cloned.1.call-start = ((), (), s32[]{:S(2)}) async-start(), calls=%async_computation.24 | async-start | bytes 2359296 | tf_op jit(solution)/shard_map/reduce_scatter | solution.py:438
  80.4 182.1 %collective-permute-start.2 = (bf16[344,1024]{1,0:T(8,128)(2,1)}, bf16[344,1024]{1,0:T(8,128)(2,1)}, u32[]{:S(2)}, u32[]{:S(2)}) collective-permute-start(bf16[344,1024]{1,0:T(8,128)(2,1)} %get-tuple-element.116), channel_id=1, source_target_pairs={{1,0},{2,1},{3,2},{4,7},{6,5},{7,6},{9,8},{10,9},{11,10},{12,15},{... | collective-permute-start | bytes 2113544 | tf_op jit(solution)/shard_map/ppermute | solution.py:333
  81.7 155.9 %collective-permute-start = (bf16[344,1024]{1,0:T(8,128)(2,1)}, bf16[344,1024]{1,0:T(8,128)(2,1)}, u32[]{:S(2)}, u32[]{:S(2)}) collective-permute-start(bf16[344,1024]{1,0:T(8,128)(2,1)} %get-tuple-element.117), channel_id=1, source_target_pairs={{0,1},{1,2},{3,0},{4,5},{5,6},{6,7},{8,9},{9,10},{11,8},{12,13},{1... | collective-permute-start | bytes 2113544 | tf_op jit(solution)/shard_map/ppermute | solution.py:333
  87.6 129.7 %collective-permute-start.5 = (bf16[344,1024]{1,0:T(8,128)(2,1)}, bf16[344,1024]{1,0:T(8,128)(2,1)}, u32[]{:S(2)}, u32[]{:S(2)}) collective-permute-start(bf16[344,1024]{1,0:T(8,128)(2,1)} %get-tuple-element.112), channel_id=1, source_target_pairs={{1,0},{2,1},{3,2},{4,7},{6,5},{7,6},{9,8},{10,9},{11,10},{12,15},{... | collective-permute-start | bytes 2113544 | tf_op jit(solution)/shard_map/ppermute | solution.py:333
  93.5 112.6 %collective-permute-start.4 = (bf16[344,1024]{1,0:T(8,128)(2,1)}, bf16[344,1024]{1,0:T(8,128)(2,1)}, u32[]{:S(2)}, u32[]{:S(2)}) collective-permute-start(bf16[344,1024]{1,0:T(8,128)(2,1)} %get-tuple-element.115), channel_id=1, source_target_pairs={{0,2},{2,0},{3,1},{4,6},{5,7},{7,5},{8,10},{10,8},{11,9},{12,14},{... | collective-permute-start | bytes 2113544 | tf_op jit(solution)/shard_map/ppermute | solution.py:333
  162.9 86.9 %collective-permute-start.1 = (bf16[344,1024]{1,0:T(8,128)(2,1)}, bf16[344,1024]{1,0:T(8,128)(2,1)}, u32[]{:S(2)}, u32[]{:S(2)}) collective-permute-start(bf16[344,1024]{1,0:T(8,128)(2,1)} %get-tuple-element.119), channel_id=1, source_target_pairs={{0,2},{2,0},{3,1},{4,6},{5,7},{7,5},{8,10},{10,8},{11,9},{12,14},{... | collective-permute-start | bytes 2113544 | tf_op jit(solution)/shard_map/ppermute | solution.py:333
  505.9 183.2 %reduce-scatter.17.cloned.1.call-start = ((), (), s32[]{:S(2)}) async-start(), calls=%async_computation.20 | async-start | bytes 2359296 | tf_op jit(solution)/shard_map/reduce_scatter | solution.py:438
  624.8 84.1 %reduce-scatter.13.cloned.1.call-start = ((), (), s32[]{:S(2)}) async-start(), calls=%async_computation.18 | async-start | bytes 2359296 | tf_op jit(solution)/shard_map/reduce_scatter | solution.py:438
  631.6 122.6 %reduce-scatter.21.cloned.1.call-start = ((), (), s32[]{:S(2)}) async-start(), calls=%async_computation.22 | async-start | bytes 2359296 | tf_op jit(solution)/shard_map/reduce_scatter | solution.py:438
  638.7 190.3 %reduce-scatter.33.cloned.1.call-start = ((), (), s32[]{:S(2)}) async-start(), calls=%async_computation.28 | async-start | bytes 9437184 | tf_op jit(solution)/shard_map/reduce_scatter | solution.py:438
  639.4 264.6 %reduce-scatter.29.cloned.1.call-start = ((), (), s32[]{:S(2)}) async-start(), calls=%async_computation.26 | async-start | bytes 9437184 | tf_op jit(solution)/shard_map/reduce_scatter | solution.py:438
  640.0 286.6 %reduce-scatter.27.cloned.1.call-start = ((), (), s32[]{:S(2)}) async-start(), calls=%async_computation.25 | async-start | bytes 327680 | tf_op jit(solution)/shard_map/reduce_scatter | solution.py:439
  651.2 252.8 %collective-permute-start.8 = (bf16[344,1024]{1,0:T(8,128)(2,1)}, bf16[344,1024]{1,0:T(8,128)(2,1)}, u32[]{:S(2)}, u32[]{:S(2)}) collective-permute-start(bf16[344,1024]{1,0:T(8,128)(2,1)} %get-tuple-element.109), channel_id=1, source_target_pairs={{0,3},{1,0},{2,1},{5,4},{6,5},{7,6},{8,11},{9,8},{10,9},{13,12},{1... | collective-permute-start | bytes 2113544 | tf_op jit(solution)/shard_map/ppermute | solution.py:349
  654.5 257.0 %collective-permute-start.7 = (bf16[344,1024]{1,0:T(8,128)(2,1)}, bf16[344,1024]{1,0:T(8,128)(2,1)}, u32[]{:S(2)}, u32[]{:S(2)}) collective-permute-start(bf16[344,1024]{1,0:T(8,128)(2,1)} %get-tuple-element.110), channel_id=1, source_target_pairs={{0,2},{1,3},{2,0},{5,7},{6,4},{7,5},{8,10},{9,11},{10,8},{13,15},{... | collective-permute-start | bytes 2113544 | tf_op jit(solution)/shard_map/ppermute | solution.py:349
  656.5 255.1 %collective-permute-start.6 = (bf16[344,1024]{1,0:T(8,128)(2,1)}, bf16[344,1024]{1,0:T(8,128)(2,1)}, u32[]{:S(2)}, u32[]{:S(2)}) collective-permute-start(bf16[344,1024]{1,0:T(8,128)(2,1)} %get-tuple-element.111), channel_id=1, source_target_pairs={{0,1},{1,2},{2,3},{5,6},{6,7},{7,4},{8,9},{9,10},{10,11},{13,14},{... | collective-permute-start | bytes 2113544 | tf_op jit(solution)/shard_map/ppermute | solution.py:349
  675.6 271.2 %reduce-scatter.19.cloned.1.call-start = ((), (), s32[]{:S(2)}) async-start(), calls=%async_computation.21 | async-start | bytes 327680 | tf_op jit(solution)/shard_map/reduce_scatter | solution.py:439
  689.1 277.6 %reduce-scatter.15.cloned.1.call-start = ((), (), s32[]{:S(2)}) async-start(), calls=%async_computation.19 | async-start | bytes 327680 | tf_op jit(solution)/shard_map/reduce_scatter | solution.py:439
  708.9 277.9 %reduce-scatter.23.cloned.1.call-start = ((), (), s32[]{:S(2)}) async-start(), calls=%async_computation.23 | async-start | bytes 327680 | tf_op jit(solution)/shard_map/reduce_scatter | solution.py:439
  754.2 260.2 %reduce-scatter.35.cloned.1.call-start = ((), (), s32[]{:S(2)}) async-start(), calls=%async_computation.29 | async-start | bytes 1310720 | tf_op jit(solution)/shard_map/reduce_scatter | solution.py:439
  829.0 213.5 %reduce-scatter.31.cloned.1.call-start = ((), (), s32[]{:S(2)}) async-start(), calls=%async_computation.27 | async-start | bytes 1310720 | tf_op jit(solution)/shard_map/reduce_scatter | solution.py:439
  (45 other events, 1966.5 us)
Sparse Core Ops, SparseCore 0:
  9.6 39.6 all-gather.12
  50.9 27.7 all-gather.16
  80.6 45.0 all-gather.8
  127.4 28.1 all-gather.10
  157.4 54.4 all-gather.14
  213.6 55.9 all-gather.18
  506.0 39.4 reduce-scatter.24
  624.9 39.4 reduce-scatter.16
  667.6 41.1 reduce-scatter.12
  712.9 41.2 reduce-scatter.20
  757.7 71.2 reduce-scatter.32
  832.7 71.2 reduce-scatter.28
  906.3 20.3 reduce-scatter.26
  928.8 17.8 reduce-scatter.18
  948.8 17.8 reduce-scatter.14
  969.0 17.7 reduce-scatter.22
  988.9 25.4 reduce-scatter.34
  1016.7 25.7 reduce-scatter.30

commit v2 on v1

v2 whole, which is shorter than its diff:
```python
import functools
import math

import jax
import jax.numpy as jnp
from jax import lax
from jax.experimental import pallas as pl
from jax.experimental.pallas import tpu as pltpu
from jax.sharding import PartitionSpec as P

HD = 64
LANES = 128
LOG2E = math.log2(math.e)
NEG = -1e30
NT = (((1,), (1,)), ((), ()))
NN = (((1,), (0,)), ((), ()))
f32 = jnp.float32
bf16 = jnp.bfloat16


def round_up(n, m):
    return (n + m - 1) // m * m


def parts(x):
    hi = x.astype(bf16).astype(f32)
    rest = x - hi
    mid = rest.astype(bf16).astype(f32)
    return hi, mid, rest - mid


def keys_with_bias(keys, lane, row, length, own, spare):
    bias = jnp.where(row < length, 0.0, NEG)
    ones = jnp.where((lane >= spare) & (lane < spare + 3), 1.0, 0.0)
    return jnp.where(own, keys, jnp.where(lane == spare + 3, bias, ones)).astype(bf16)


MESH = pl.DeviceIdType.MESH
ANY = pl.BlockSpec(memory_space=pl.ANY)
DMA = pltpu.SemaphoreType.DMA


def flipped(g, mask):
    bit = 1
    while bit <= mask:
        if mask & bit:
            g = g + bit * (1 - 2 * ((g // bit) % 2))
        bit *= 2
    return g


class Place:
    def __init__(self, groups, line):
        self.groups, self.line = groups, line
        self.g, self.z = lax.axis_index("dp"), lax.axis_index("tensor")
        self.masks = list(range(0, groups, 2))
        self.square = groups == 8
        self.direct = [2, 4] if self.square else self.masks[1:]

    def image(self, z):
        odd = self.g % 2
        return z + odd * (self.line - 1 - 2 * z)

    def up(self, k):
        return lax.rem(self.z + k, self.line)

    def down(self, k):
        return lax.rem(self.z + self.line - k, self.line)

    def barrier(self):
        semaphore = pltpu.get_barrier_semaphore()
        peers = [(self.g, self.up(s)) for s in range(1, self.line)]
        peers += [(flipped(self.g, m), self.z) for m in self.direct + [1]]
        for peer in peers:
            pl.semaphore_signal(semaphore, inc=1, device_id=peer, device_id_type=MESH)
        pl.semaphore_wait(semaphore, len(peers))


def remote(src, dst, send, recv, device):
    return pltpu.make_async_remote_copy(
        src_ref=src, dst_ref=dst, send_sem=send, recv_sem=recv, device_id=device, device_id_type=MESH
    )


class Gather:
    @staticmethod
    def sems(groups, line):
        chips = groups // 2
        return [
            DMA((line,)),
            DMA((line,)),
            DMA((chips, line)),
            DMA((chips, line)),
            DMA((chips, line)),
            DMA((chips, line)),
        ]

    def __init__(self, at, shard, full, sems):
        self.at, self.shard, self.full = at, shard, full
        self.zs, self.zr, self.ds, self.dr, self.cs, self.cr = sems
        self.rows = shard.shape[0]

    def piece(self, mask, k):
        at = self.at
        rows = pl.ds(pl.multiple_of(flipped(at.g, mask) * self.rows, 8), self.rows)
        return self.full.at[at.down(k), rows, :]

    def own(self, k):
        return self.shard if k == 0 else self.piece(0, k)

    def local(self):
        return pltpu.make_async_copy(self.shard, self.piece(0, 0), self.zs.at[0])

    def along(self, k, arriving=False):
        dst = self.piece(0, k if arriving else 0)
        src = dst if arriving else self.shard
        return remote(src, dst, self.zs.at[k], self.zr.at[k], (self.at.g, self.at.up(k)))

    def across(self, mask, k, arriving=False):
        at = self.at
        if at.square and mask == 6:
            via, peer = (2, 4) if k < at.line // 2 else (4, 2)
            src = dst = self.piece(via, k)
        else:
            peer = mask
            src, dst = self.own(k), self.piece(0, k)
        if arriving:
            src = dst = self.piece(mask, k)
        return remote(
            src, dst, self.ds.at[mask // 2, k], self.dr.at[mask // 2, k], (flipped(at.g, peer), at.z)
        )

    def core(self, mask, k, arriving=False):
        at = self.at
        if arriving:
            dst = self.piece(mask ^ 1, k)
            src = dst
        else:
            dst = self.piece(mask, k)
            src = self.own(k) if mask == 0 else dst
        return remote(src, dst, self.cs.at[mask // 2, k], self.cr.at[mask // 2, k], (flipped(at.g, 1), at.z))

    def start(self):
        self.local().start()
        for k in range(1, self.at.line):
            self.along(k).start()
        self.spread(0)

    def spread(self, k):
        if k:
            self.along(k, True).wait_recv()
        for mask in self.at.direct:
            self.across(mask, k).start()
        self.core(0, k).start()

    def passing(self, k):
        at = self.at
        for mask in at.direct:
            self.across(mask, k, True).wait_recv()
            if at.square and mask == (2 if k < at.line // 2 else 4):
                self.across(6, k).start()
            self.core(mask, k).start()

    def last(self, k):
        if self.at.square:
            self.across(6, k, True).wait_recv()
            self.core(6, k).start()

    def finish(self):
        at = self.at
        for k in range(at.line):
            for mask in at.masks:
                self.core(mask, k, True).wait_recv()
                self.core(mask, k).wait_send()
                if mask:
                    self.across(mask, k).wait_send()
            if k:
                self.along(k).wait_send()
        self.local().wait()

    def steps(self):
        line = self.at.line
        out = [self.start]
        for k in range(1, line):
            out.append(functools.partial(self.spread, k))
        for k in range(line):
            out.append(functools.partial(self.passing, k))
        for k in range(line):
            out.append(functools.partial(self.last, k))
        out.append(self.finish)
        return out


class ToOwner:
    @staticmethod
    def sems(groups, line):
        return [DMA((line,)), DMA((line,))]

    def __init__(self, at, rows, image, sems):
        self.at, self.rows, self.image = at, rows, image
        self.send, self.recv = sems
        self.count = rows.shape[0]

    def local(self):
        at = self.at
        return pltpu.make_async_copy(
            self.rows.at[jnp.minimum(at.image(at.z), self.count - 1)], self.image.at[at.z], self.send.at[0]
        )

    def copy(self, k, arriving=False):
        at = self.at
        to = at.up(k)
        src = self.rows.at[jnp.minimum(at.image(to), self.count - 1)]
        dst = self.image.at[at.down(k) if arriving else at.z]
        return remote(src, dst, self.send.at[k], self.recv.at[k], (at.g, to))

    def start(self):
        at = self.at
        self.local().start()
        for k in range(1, at.line):
            pl.when(at.image(at.up(k)) < self.count)(self.copy(k).start)

    def finish(self):
        at = self.at
        for k in range(1, at.line):
            pl.when(at.image(at.up(k)) < self.count)(self.copy(k).wait_send)
            pl.when(at.image(at.z) < self.count)(self.copy(k, True).wait_recv)
        self.local().wait()


class FromOwner:
    sems = ToOwner.sems

    def __init__(self, at, image, rows, sems):
        self.at, self.rows, self.image = at, rows, image
        self.send, self.recv = sems
        self.count = rows.shape[0]

    def local(self):
        at = self.at
        return pltpu.make_async_copy(
            self.image.at[at.z], self.rows.at[jnp.minimum(at.image(at.z), self.count - 1)], self.send.at[0]
        )

    def copy(self, k, arriving=False):
        at = self.at
        owner = at.down(k) if arriving else at.z
        dst = self.rows.at[jnp.minimum(at.image(owner), self.count - 1)]
        return remote(self.image.at[at.up(k)], dst, self.send.at[k], self.recv.at[k], (at.g, at.up(k)))

    def start(self):
        at = self.at

        @pl.when(at.image(at.z) < self.count)
        def _():
            self.local().start()
            for k in range(1, at.line):
                self.copy(k).start()

    def finish(self):
        at = self.at

        @pl.when(at.image(at.z) < self.count)
        def _():
            for k in range(1, at.line):
                self.copy(k).wait_send()
            self.local().wait()

        for k in range(1, at.line):
            pl.when(at.image(at.down(k)) < self.count)(self.copy(k, True).wait_recv)


class Reduce:
    @staticmethod
    def scratch(groups, line, r, c, dtype):
        chips = groups // 2
        return [
            pltpu.VMEM((chips, line, r, c), dtype),
            pltpu.VMEM((chips, line, r, c), dtype),
            pltpu.VMEM((chips, line, r, c), dtype),
            pltpu.VMEM((line, r, c), dtype),
            DMA((chips, line)),
            DMA((chips, line)),
            DMA((chips, line)),
            DMA((chips, line)),
            DMA((chips, line)),
            DMA((line,)),
            DMA((line,)),
        ]

    def __init__(self, at, full, scratch, rows):
        self.at, self.full, self.rows = at, full, rows
        self.cbuf, self.sums, self.dbuf, self.zbuf = scratch[:4]
        self.ls, self.cs, self.cr, self.ds, self.dr, self.zs, self.zr = scratch[4:]
        self.order = [6, 2, 4, 0] if at.square else at.masks[1:] + [0]

    def piece(self, mask, k):
        at = self.at
        rows = pl.ds(pl.multiple_of(flipped(at.g, mask) * self.rows, 8), self.rows)
        return self.full.at[at.down(k), rows, :]

    def local(self, mask, k):
        return pltpu.make_async_copy(
            self.piece(mask, k), self.sums.at[mask // 2, k], self.ls.at[mask // 2, k]
        )

    def core(self, mask, k):
        at, m = self.at, mask // 2
        return remote(
            self.piece(mask ^ 1, k), self.cbuf.at[m, k], self.cs.at[m, k], self.cr.at[m, k],
            (flipped(at.g, 1), at.z),
        )

    def across(self, mask, k):
        at, m = self.at, mask // 2
        peer = mask
        if at.square and mask == 6:
            peer = 4 if k < at.line // 2 else 2
        return remote(
            self.sums.at[m, k], self.dbuf.at[m, k], self.ds.at[m, k], self.dr.at[m, k],
            (flipped(at.g, peer), at.z),
        )

    def along(self, k):
        at = self.at
        return remote(
            self.sums.at[0, k], self.zbuf.at[k], self.zs.at[k], self.zr.at[k], (at.g, at.down(k))
        )

    def start(self):
        for mask in self.order:
            for k in range(self.at.line):
                self.core(mask, k).start()
                self.local(mask, k).start()

    def add(self, m, k, other):
        total = self.sums[m, k].astype(f32) + other.astype(f32)
        self.sums[m, k] = total.astype(self.sums.dtype)

    def pair(self, mask, k):
        self.local(mask, k).wait()
        self.core(mask, k).wait_recv()
        self.add(mask // 2, k, self.cbuf[mask // 2, k])

    def pairs(self, mask):
        at = self.at
        for k in range(at.line):
            self.pair(mask, k)
            waits = at.square and mask == (2 if k < at.line // 2 else 4)
            if mask and not waits:
                self.across(mask, k).start()

    def joined(self, k):
        at = self.at
        if at.square:
            mask = 2 if k < at.line // 2 else 4
            self.across(6, k).wait_recv()
            self.add(mask // 2, k, self.dbuf[3, k])
            self.across(mask, k).start()

    def own(self, k):
        for mask in self.at.direct:
            self.across(mask, k).wait_recv()
            self.add(0, k, self.dbuf[mask // 2, k])
        if k:
            self.along(k).start()

    def finish(self):
        at = self.at
        for k in range(at.line):
            for mask in at.masks:
                self.core(mask, k).wait_send()
                if mask:
                    self.across(mask, k).wait_send()
            if k:
                self.along(k).wait_send()
                self.along(k).wait_recv()
        total = self.sums[0, 0].astype(f32)
        for k in range(1, at.line):
            total += self.zbuf[k].astype(f32)
        return total

    def steps(self):
        ks = range(self.at.line)
        out = [self.start]
        out += [functools.partial(self.pairs, mask) for mask in self.order]
        out += [functools.partial(self.joined, k) for k in ks]
        return out + [functools.partial(self.own, k) for k in ks]


def run_ticks(ticks, step, half):
    for at, work in ticks:
        if at % 2 == half:
            pl.when(step == at // 2)(work)


def arrive_kernel(groups, line, x_ref, shard_ref, small_ref, xo_ref, full_ref, smalls_ref, *sems):
    at = Place(groups, line)
    n = len(Gather.sems(groups, line))
    rows = ToOwner(at, x_ref, xo_ref, sems[2 * n :])
    weights = Gather(at, shard_ref, full_ref, sems[:n])
    small = Gather(at, small_ref, smalls_ref, sems[n : 2 * n])
    at.barrier()
    for one, two in zip(small.steps(), weights.steps()):
        one()
        two()
        if one == small.start:
            rows.start()
    rows.finish()


def arrive(groups, line, x, shard, small):
    images, part_rows, width = x.shape
    return pl.pallas_call(
        functools.partial(arrive_kernel, groups, line),
        in_specs=[ANY] * 3,
        out_specs=[ANY] * 3,
        out_shape=[
            jax.ShapeDtypeStruct((line, part_rows, width), x.dtype),
            jax.ShapeDtypeStruct((line, groups * shard.shape[0], shard.shape[1]), shard.dtype),
            jax.ShapeDtypeStruct((line, groups * small.shape[0], small.shape[1]), small.dtype),
        ],
        scratch_shapes=Gather.sems(groups, line) * 2 + ToOwner.sems(groups, line),
        compiler_params=pltpu.CompilerParams(collective_id=1, has_side_effects=True),
        name="arrive",
    )(x, shard, small)


def leave_kernel(groups, line, r, y_ref, full_ref, smalls_ref, yo_ref, shard_ref, small_ref, *scratch):
    at = Place(groups, line)
    n = len(ToOwner.sems(groups, line))
    m = (len(scratch) - n) // 2
    rows = FromOwner(at, y_ref, yo_ref, scratch[:n])
    weights = Reduce(at, full_ref, scratch[n : n + m], r)
    small = Reduce(at, smalls_ref, scratch[n + m :], small_ref.shape[0])
    at.barrier()
    for one, two in zip(weights.steps(), small.steps()):
        one()
        two()
        if two == small.start:
            rows.start()
    shard_ref[...] = weights.finish()
    small_ref[...] = small.finish()
    rows.finish()


def leave(groups, line, images, y, full, smalls):
    _, part_rows, width = y.shape
    _, r, c = full.shape
    r = r // groups
    sr, sc = smalls.shape[1] // groups, smalls.shape[2]
    vmem = pl.BlockSpec(memory_space=pltpu.VMEM)
    return pl.pallas_call(
        functools.partial(leave_kernel, groups, line, r),
        in_specs=[ANY] * 3,
        out_specs=[ANY, vmem, vmem],
        out_shape=[
            jax.ShapeDtypeStruct((images, part_rows, width), y.dtype),
            jax.ShapeDtypeStruct((r, c), f32),
            jax.ShapeDtypeStruct((sr, sc), f32),
        ],
        scratch_shapes=ToOwner.sems(groups, line)
        + Reduce.scratch(groups, line, r, c, full.dtype)
        + Reduce.scratch(groups, line, sr, sc, smalls.dtype),
        compiler_params=pltpu.CompilerParams(
            collective_id=2, has_side_effects=True, vmem_limit_bytes=40 * 2**20
        ),
        name="leave",
    )(y, full, smalls)


def project_kernel(n1_ref, w_ref, b_ref, out_ref):
    scale = jnp.where(pl.program_id(1) == 0, HD ** (-0.5) * LOG2E, 1.0)
    out = lax.dot_general(n1_ref[...], w_ref[0], NN, preferred_element_type=f32) + b_ref[0]
    out_ref[0] = (out * scale).astype(bf16)


def project(normed1, weights, bias):
    rows, width = normed1.shape
    line = weights.shape[0]
    cols = width // line
    return pl.pallas_call(
        project_kernel,
        grid=(line, 3),
        in_specs=[
            pl.BlockSpec((rows, width), lambda t, k: (0, 0), pipeline_mode=pl.Buffered(1)),
            pl.BlockSpec((1, width, cols), lambda t, k: (t, 0, k)),
            pl.BlockSpec((1, 1, cols), lambda t, k: (k, 0, t)),
        ],
        out_specs=pl.BlockSpec((1, rows, cols), lambda t, k: (k, 0, t)),
        out_shape=jax.ShapeDtypeStruct((3, rows, width), bf16),
        compiler_params=pltpu.CompilerParams(vmem_limit_bytes=40 * 2**20),
        cost_estimate=pl.CostEstimate(
            flops=6 * rows * width * width, bytes_accessed=16 * rows * width, transcendentals=0
        ),
        name="project",
    )(normed1, weights, bias)


def attend_forward_kernel(
    groups, line, rows, padded, len_ref, q_ref, k_ref, v_ref, shard_ref, cot_ref,
    ctx_ref, qa_ref, full_ref, coto_ref, ka, va, *sems
):
    at = Place(groups, line)
    n = len(Gather.sems(groups, line))
    weights = Gather(at, shard_ref, full_ref, sems[:n])
    cot = ToOwner(at, cot_ref, coto_ref, sems[n:])
    steps = weights.steps()
    halves = 2 * pl.num_programs(0)
    first, spreads, passes, rest = steps[0], steps[1:line], steps[line : 2 * line], steps[2 * line :]

    def begin():
        at.barrier()
        first()

    ticks = [(0, begin), (6, cot.start)]
    for k in range(1, line):
        ticks.append((min(4 * k, 15), spreads[k - 1]))
    for k in range(line):
        ticks.append((min(4 * k + 4, 15), passes[k]))
    step = pl.program_id(0)
    length = len_ref[0]
    lane = lax.broadcasted_iota(jnp.int32, (padded, LANES), 1)
    row = lax.broadcasted_iota(jnp.int32, (padded, LANES), 0)
    lb = lane[:rows]
    if padded > rows:
        va[rows:] = jnp.zeros((padded - rows, LANES), bf16)
    for half in range(2):
        run_ticks(ticks, step, half)
        own = (lb < HD) if half == 0 else (lb >= HD)
        spare = HD if half == 0 else 0
        ka[:rows] = keys_with_bias(k_ref[...].astype(f32), lb, row[:rows], length, own, spare)
        if padded > rows:
            ka[rows:] = jnp.where(lane[rows:] == spare + 3, NEG, 0.0).astype(bf16)
        va[:rows] = jnp.where(
            own, v_ref[...].astype(f32), jnp.where(lb == spare, 1.0, 0.0)
        ).astype(bf16)
        qa = jnp.where(own, q_ref[...].astype(f32), jnp.where(lb == spare + 3, 1.0, 0.0))
        s = lax.dot_general(qa.astype(bf16), ka[...], NT, preferred_element_type=f32)
        m = jnp.max(s, axis=1, keepdims=True)
        p = jnp.exp2(s - m).astype(bf16)
        o = lax.dot_general(p, va[...], NN, preferred_element_type=f32)
        total = o[:, spare : spare + 1]
        o = o / total
        hi, mid, lo = parts(-(m + jnp.log2(total)))
        if half == 0:
            ctx_ref[...] = o.astype(bf16)
        else:
            ctx_ref[...] = jnp.where(own, o, ctx_ref[...].astype(f32)).astype(bf16)
        stats = jnp.where(lb == spare + 2, lo, qa)
        stats = jnp.where(lb == spare + 1, mid, stats)
        qa_ref[half] = jnp.where(lb == spare, hi, stats).astype(bf16)

    @pl.when(step == pl.num_programs(0) - 1)
    def _():
        for work in rest:
            work()
        cot.finish()


def attend_forward(groups, line, length, qkv, shard, cot):
    _, rows, width = qkv.shape
    padded = round_up(rows, LANES)
    spec = pl.BlockSpec((rows, LANES), lambda j: (0, j))

    def third(n):
        return pl.BlockSpec((None, rows, LANES), lambda j: (n, 0, j))

    return pl.pallas_call(
        functools.partial(attend_forward_kernel, groups, line, rows, padded),
        grid=(width // LANES,),
        in_specs=[pl.BlockSpec(memory_space=pltpu.SMEM), third(0), third(1), third(2), ANY, ANY],
        out_specs=[spec, pl.BlockSpec((2, rows, LANES), lambda j: (j, 0, 0)), ANY, ANY],
        out_shape=[
            jax.ShapeDtypeStruct((rows, width), bf16),
            jax.ShapeDtypeStruct((width // HD, rows, LANES), bf16),
            jax.ShapeDtypeStruct((line, groups * shard.shape[0], shard.shape[1]), shard.dtype),
            jax.ShapeDtypeStruct((line,) + cot.shape[1:], cot.dtype),
        ],
        scratch_shapes=[pltpu.VMEM((padded, LANES), bf16), pltpu.VMEM((padded, LANES), bf16)]
        + Gather.sems(groups, line)
        + ToOwner.sems(groups, line),
        compiler_params=pltpu.CompilerParams(
            collective_id=3, has_side_effects=True, vmem_limit_bytes=56 * 2**20
        ),
        cost_estimate=pl.CostEstimate(
            flops=16 * rows * rows * width,
            bytes_accessed=12 * rows * width,
            transcendentals=rows * rows * width // HD,
        ),
        name="attend_forward",
    )(length, qkv, qkv, qkv, shard, cot)


def attend_backward_kernel(
    groups, line, rows, padded, blocks, len_ref, qa_ref, k_ref, v_ref, gc_ref, ctx_ref, y_ref, full_ref,
    gq_ref, gk_ref, gv_ref, yo_ref, shard_ref, ka, va, qs, ga, acc, *scratch
):
    at = Place(groups, line)
    n = len(ToOwner.sems(groups, line))
    back = FromOwner(at, y_ref, yo_ref, scratch[:n])
    weights = Reduce(at, full_ref, scratch[n:], shard_ref.shape[0])
    steps = weights.steps()
    chips = groups // 2

    def begin():
        at.barrier()
        steps[0]()
        back.start()

    ticks = [(0, begin)]
    for i in range(chips):
        ticks.append((min(i + 1, 4), steps[1 + i]))
    for k in range(line):
        ticks.append((min(6 + k // 2, 15), steps[1 + chips + k]))
    for k in range(line):
        ticks.append((12, steps[1 + chips + line + k]))
    step = pl.program_id(0)
    length = len_ref[0]
    lane = lax.broadcasted_iota(jnp.int32, (padded, LANES), 1)
    row = lax.broadcasted_iota(jnp.int32, (padded, LANES), 0)
    size = rows // blocks
    ls = lane[:rows]
    for half in range(2):
        run_ticks(ticks, step, half)
        own = (ls < HD) if half == 0 else (ls >= HD)
        spare = HD if half == 0 else 0
        ownb = own[:size]
        gc = gc_ref[...].astype(f32)
        corr = jnp.sum(
            jnp.where(own, gc * ctx_ref[...].astype(f32), 0.0), axis=1, keepdims=True
        )
        hi, mid, lo = parts(-corr)
        extra = jnp.where(ls == spare + 1, mid, jnp.where(ls == spare + 2, lo, 0.0))
        ga[:rows] = jnp.where(own, gc, jnp.where(ls == spare, hi, extra)).astype(bf16)
        qs[:rows] = qa_ref[half]
        if padded > rows:
            ga[rows:] = jnp.zeros((padded - rows, LANES), bf16)
            qs[rows:] = jnp.where(lane[rows:] == spare, NEG, 0.0).astype(bf16)
        ka[...] = keys_with_bias(k_ref[...].astype(f32), ls, row[:rows], length, own, spare)
        ones = jnp.where((ls >= spare) & (ls < spare + 3), 1.0, 0.0)
        va[...] = jnp.where(own, v_ref[...].astype(f32), ones).astype(bf16)
        acc[...] = jnp.zeros_like(acc)

        def block(b, carry):
            r = pl.ds(pl.multiple_of(b * size, 16), size)
            kb = ka[r, :]
            p = jnp.exp2(lax.dot_general(kb, qs[...], NT, preferred_element_type=f32))
            gp = lax.dot_general(va[r, :], ga[...], NT, preferred_element_type=f32)
            ds = (p * gp).astype(bf16)
            gv = lax.dot_general(p.astype(bf16), ga[...], NN, preferred_element_type=f32)
            gk = lax.dot_general(ds, qs[...], NN, preferred_element_type=f32) * (1.0 / LOG2E)
            acc[...] += lax.dot_general(kb.T, ds, NN, preferred_element_type=f32)
            if half == 0:
                gv_ref[r, :] = gv.astype(bf16)
                gk_ref[r, :] = gk.astype(bf16)
            else:
                gv_ref[r, :] = jnp.where(ownb, gv, gv_ref[r, :].astype(f32)).astype(bf16)
                gk_ref[r, :] = jnp.where(ownb, gk, gk_ref[r, :].astype(f32)).astype(bf16)
            return carry

        lax.fori_loop(0, blocks, block, 0)
        gq = acc[...].T[:rows] * HD ** (-0.5)
        if half == 0:
            gq_ref[...] = gq.astype(bf16)
        else:
            gq_ref[...] = jnp.where(own, gq, gq_ref[...].astype(f32)).astype(bf16)

    @pl.when(step == pl.num_programs(0) - 1)
    def _():
        shard_ref[...] = weights.finish()
        back.finish()


def attend_backward(groups, line, images, length, qa, qkv, gc, ctx, y, full):
    _, rows, width = qkv.shape
    padded = round_up(rows, LANES)
    blocks = 2 if rows % 32 == 0 else 1
    spec = pl.BlockSpec((rows, LANES), lambda j: (0, j))
    r, c = full.shape[1] // groups, full.shape[2]

    def third(n):
        return pl.BlockSpec((None, rows, LANES), lambda j: (n, 0, j))

    return pl.pallas_call(
        functools.partial(attend_backward_kernel, groups, line, rows, padded, blocks),
        grid=(width // LANES,),
        in_specs=[
            pl.BlockSpec(memory_space=pltpu.SMEM),
            pl.BlockSpec((2, rows, LANES), lambda j: (j, 0, 0)),
            third(1),
            third(2),
            spec,
            spec,
            ANY,
            ANY,
        ],
        out_specs=[spec] * 3 + [ANY, pl.BlockSpec((r, c), lambda j: (0, 0))],
        out_shape=[jax.ShapeDtypeStruct((rows, width), bf16)] * 3
        + [jax.ShapeDtypeStruct((images,) + y.shape[1:], y.dtype), jax.ShapeDtypeStruct((r, c), f32)],
        scratch_shapes=[
            pltpu.VMEM((rows, LANES), bf16),
            pltpu.VMEM((rows, LANES), bf16),
            pltpu.VMEM((padded, LANES), bf16),
            pltpu.VMEM((padded, LANES), bf16),
            pltpu.VMEM((LANES, padded), f32),
        ]
        + ToOwner.sems(groups, line)
        + Reduce.scratch(groups, line, r, c, full.dtype),
        compiler_params=pltpu.CompilerParams(
            collective_id=4, has_side_effects=True, vmem_limit_bytes=62 * 2**20
        ),
        cost_estimate=pl.CostEstimate(
            flops=40 * rows * rows * width,
            bytes_accessed=16 * rows * width,
            transcendentals=rows * rows * width // HD,
        ),
        name="attend_backward",
    )(length, qa, qkv, qkv, gc, ctx, y, full)


def feed_forward_kernel(
    tile, n2_ref, n2t_ref, gm_ref, gmt_ref, w_ref, b1_ref, mlp_ref, gn_ref, gw_ref, gb_ref
):
    step = pl.program_id(0)
    w1 = w_ref[0, :, :tile]
    w2t = w_ref[0, :, tile:]
    pre = lax.dot_general(n2_ref[...], w1, NN, preferred_element_type=f32) + b1_ref[...]
    gact = lax.dot_general(gm_ref[...], w2t, NN, preferred_element_type=f32)
    cdf = 0.5 * (1.0 + lax.erf(pre * (1 / math.sqrt(2))))
    act = (pre * cdf).astype(bf16)
    pdf = jnp.exp2(pre * pre * (-0.5 * LOG2E)) * (1 / math.sqrt(2 * math.pi))
    gpre = gact * (cdf + pre * pdf)
    gb_ref[...] = jnp.sum(gpre, axis=0, keepdims=True)
    gpre = gpre.astype(bf16)
    mlp = lax.dot_general(act, w2t, NT, preferred_element_type=f32)
    gn = lax.dot_general(gpre, w1, NT, preferred_element_type=f32)

    @pl.when(step == 0)
    def _():
        mlp_ref[...] = mlp
        gn_ref[...] = gn

    @pl.when(step > 0)
    def _():
        mlp_ref[...] += mlp
        gn_ref[...] += gn

    gw_ref[0, :, :tile] = lax.dot_general(
        n2t_ref[...], gpre, NN, preferred_element_type=f32
    ).astype(bf16)
    gw_ref[0, :, tile:] = lax.dot_general(
        gmt_ref[...], act, NN, preferred_element_type=f32
    ).astype(bf16)


def feed_forward(n2, n2t, gm, gmt, weights, b1, tile):
    rows, width = n2.shape
    units = b1.shape[1]
    per = weights.shape[2] // (2 * tile)

    def whole(a, b):
        return pl.BlockSpec((a, b), lambda j: (0, 0), pipeline_mode=pl.Buffered(1))

    both = pl.BlockSpec((1, width, 2 * tile), lambda j: (j // per, 0, j % per))
    return pl.pallas_call(
        functools.partial(feed_forward_kernel, tile),
        grid=(units // tile,),
        in_specs=[
            whole(rows, width),
            whole(width, rows),
            whole(rows, width),
            whole(width, rows),
            both,
            pl.BlockSpec((1, tile), lambda j: (0, j)),
        ],
        out_specs=[
            whole(rows, width),
            whole(rows, width),
            both,
            pl.BlockSpec((1, tile), lambda j: (0, j)),
        ],
        out_shape=[
            jax.ShapeDtypeStruct((rows, width), f32),
            jax.ShapeDtypeStruct((rows, width), f32),
            jax.ShapeDtypeStruct(weights.shape, bf16),
            jax.ShapeDtypeStruct((1, units), f32),
        ],
        compiler_params=pltpu.CompilerParams(vmem_limit_bytes=60 * 2**20),
        cost_estimate=pl.CostEstimate(
            flops=16 * rows * width * units,
            bytes_accessed=8 * width * units,
            transcendentals=2 * rows * units,
        ),
        name="feed_forward",
    )(n2, n2t, gm, gmt, weights, b1)


def norm_rows(values, gain, shift):
    center = values - jnp.mean(values, axis=-1, keepdims=True)
    inverse = lax.rsqrt(jnp.mean(center * center, axis=-1, keepdims=True) + 1e-06)
    normed = center * inverse
    return normed * gain + shift, normed, inverse


def norm_back(grad_norm, normed, inverse, gain):
    scaled = grad_norm * gain
    return inverse * (
        scaled
        - jnp.mean(scaled, axis=-1, keepdims=True)
        - normed * jnp.mean(scaled * normed, axis=-1, keepdims=True)
    )


def body(
    block_input,
    cotangent,
    lengths,
    w_qkv,
    b_qv,
    w_out,
    w_fc1,
    b_fc1,
    w_fc2,
    ln_gain,
    ln_shift,
    layer_scale,
    out_bias,
):
    images, part_rows, width = block_input.shape
    groups = lax.axis_size("dp")
    line = lax.axis_size("tensor")
    rows = part_rows * line
    group = lax.axis_index("dp")
    place = lax.axis_index("tensor")
    flip = group % 2
    mine = jnp.where(flip == 1, line - 1 - place, place)
    active = mine < images

    tile = min(512, w_fc1.shape[1])
    qkv_out = jnp.concatenate([w_qkv[0], w_qkv[1], w_qkv[2], w_out.T], axis=1)
    tiles = (w_fc1.shape[0], -1, 1, tile)
    fc_both = jnp.concatenate([w_fc1.reshape(tiles), w_fc2.T.reshape(tiles)], axis=2).reshape(
        w_fc1.shape[0], -1
    )
    small = jnp.concatenate(
        [
            ln_gain.reshape(-1),
            ln_shift.reshape(-1),
            layer_scale.reshape(-1),
            out_bias.reshape(-1),
            b_qv.astype(f32).reshape(-1),
            b_fc1.astype(f32).reshape(-1),
        ]
    )
    small = jnp.pad(small, (0, round_up(small.size, 8 * LANES) - small.size)).reshape(-1, LANES)
    x_all, weights, small = arrive(groups, line, block_input, qkv_out, small)
    x_all = jnp.where(active, x_all.reshape(rows, width), 0)
    small = jnp.transpose(small.reshape(line, groups, -1), (1, 0, 2))
    own_width = ln_gain.shape[1]
    at = 0

    def take(count):
        nonlocal at
        at += count
        return small[:, :, at - count : at]

    def vectors(x):
        return jnp.transpose(x.reshape(groups, line, 2, own_width), (2, 0, 1, 3)).reshape(2, width)

    gains = vectors(take(2 * own_width))
    shifts = vectors(take(2 * own_width))
    scales = vectors(take(2 * own_width))
    biases = vectors(take(2 * own_width))
    _, bq_rows, bq_cols = b_qv.shape
    qv_bias = jnp.transpose(
        take(2 * bq_rows * bq_cols).reshape(groups, line, 2, bq_rows, bq_cols), (2, 1, 4, 0, 3)
    ).reshape(2, width)
    f_rows, f_cols = b_fc1.shape
    fc1_bias = jnp.transpose(
        take(f_rows * f_cols).reshape(groups, line, f_rows, f_cols), (1, 3, 0, 2)
    ).reshape(1, -1)

    length = jnp.where(active, lengths[jnp.minimum(mine, images - 1)], 0).astype(jnp.int32)
    length_array = length.reshape(1)
    valid = (jnp.arange(rows, dtype=jnp.int32) < length).astype(f32)[:, None]

    source = x_all.astype(f32)
    normed_one, hat_first, inv_first = norm_rows(source, gains[0], shifts[0])
    normed1 = normed_one.astype(bf16)

    def dot(a, b, dims=NN):
        return lax.dot_general(a, b, dims, preferred_element_type=f32)

    cols = width // line
    zero = jnp.zeros_like(qv_bias[:1])
    qkv = project(normed1, weights, jnp.stack([qv_bias[:1], zero, qv_bias[1:]]))
    context, query_stats, fc_weights, cot = attend_forward(
        groups, line, length_array, qkv, fc_both, cotangent
    )
    cot = jnp.where(active, cot.reshape(rows, width), 0)
    wout_t = weights[:, :, 3 * cols :]
    attn = (
        jnp.einsum(
            "stc,tdc->sd", context.reshape(rows, line, cols), wout_t, preferred_element_type=f32
        )
        + biases[0]
    )
    hidden = source + scales[0] * attn
    normed_two, hat_second, inv_second = norm_rows(hidden, gains[1], shifts[1])
    normed2 = normed_two.astype(bf16)
    grad_out = valid * cot.astype(f32)
    grad_mlp = grad_out * scales[1]
    grad_mlp_b = grad_mlp.astype(bf16)
    mlp, grad_normed2, grad_fc, grad_bfc1 = feed_forward(
        normed2, normed2.T, grad_mlp_b, grad_mlp_b.T, fc_weights, fc1_bias, tile
    )
    mlp = mlp + biases[1]
    block_out = (valid * (hidden + scales[1] * mlp)).astype(bf16).reshape(line, part_rows, width)
    grad_scale2 = jnp.sum(grad_out * mlp, axis=0)
    grad_bias2 = jnp.sum(grad_mlp, axis=0)
    grad_gain2 = jnp.sum(grad_normed2 * hat_second, axis=0)
    grad_shift2 = jnp.sum(grad_normed2, axis=0)
    grad_hidden = grad_out + norm_back(grad_normed2, hat_second, inv_second, gains[1])
    grad_scale1 = jnp.sum(grad_hidden * attn, axis=0)
    grad_attn = grad_hidden * scales[0]
    grad_bias1 = jnp.sum(grad_attn, axis=0)
    grad_attn_b = grad_attn.astype(bf16)
    grad_context = (
        jnp.einsum("sd,tdc->stc", grad_attn_b, wout_t, preferred_element_type=f32)
        .astype(bf16)
        .reshape(rows, width)
    )
    grad_query, grad_key, grad_value, block_out, shard_fc = attend_backward(
        groups,
        line,
        images,
        length_array,
        query_stats,
        qkv,
        grad_context,
        context,
        block_out,
        grad_fc,
    )
    grad_bq = jnp.sum(grad_query.astype(f32), axis=0)
    grad_bv = jnp.sum(grad_value.astype(f32), axis=0)
    split = (rows, line, cols)
    grad_parts = [
        jnp.einsum("sd,stc->tdc", a, b.reshape(split), preferred_element_type=f32).astype(bf16)
        for a, b in (
            (normed1, grad_query),
            (normed1, grad_key),
            (normed1, grad_value),
            (grad_attn_b, context),
        )
    ]
    grad_weights = jnp.concatenate(grad_parts, axis=2)
    grad_normed1 = sum(
        jnp.einsum(
            "stc,tdc->sd",
            g.reshape(split),
            weights[:, :, n * cols : (n + 1) * cols],
            preferred_element_type=f32,
        )
        for n, g in enumerate((grad_query, grad_key, grad_value))
    )
    grad_gain1 = jnp.sum(grad_normed1 * hat_first, axis=0)
    grad_shift1 = jnp.sum(grad_normed1, axis=0)
    grad_source = grad_hidden + norm_back(grad_normed1, hat_first, inv_first, gains[0])
    grad_source = grad_source.astype(bf16).reshape(line, part_rows, width)

    by_device = [
        jnp.transpose(
            jnp.stack(pair).reshape(2, groups, line, own_width), (2, 1, 0, 3)
        ).reshape(line, groups, -1)
        for pair in (
            (grad_gain1, grad_gain2),
            (grad_shift1, grad_shift2),
            (grad_scale1, grad_scale2),
            (grad_bias1, grad_bias2),
        )
    ]
    by_device.append(
        jnp.transpose(
            jnp.stack([grad_bq, grad_bv]).reshape(2, line, bq_cols, groups, bq_rows), (1, 3, 0, 4, 2)
        ).reshape(line, groups, -1)
    )
    by_device.append(
        jnp.transpose(grad_bfc1.reshape(line, f_cols, groups, f_rows), (0, 2, 3, 1)).reshape(
            line, groups, -1
        )
    )
    by_device = jnp.concatenate(by_device, axis=2)
    short = small.shape[2] - by_device.shape[2]
    by_device = jnp.pad(by_device, ((0, 0), (0, 0), (0, short))).reshape(line, -1, LANES)
    grad_input, shard_weights, shard_small = leave(
        groups, line, images, grad_source, grad_weights, by_device
    )
    grad_input = grad_input.astype(f32)
    own = cols
    shard_wqkv = jnp.stack([shard_weights[:, n * own : (n + 1) * own] for n in range(3)])
    shard_wout = shard_weights[:, 3 * own :].T
    shard_fc = shard_fc.reshape(shard_fc.shape[0], -1, 2, tile)
    shard_fc1 = shard_fc[:, :, 0].reshape(w_fc1.shape)
    shard_fc2 = shard_fc[:, :, 1].reshape(w_fc1.shape).T
    shard_small = shard_small.reshape(-1)
    at = 0

    def give(shape):
        nonlocal at
        at += math.prod(shape)
        return shard_small[at - math.prod(shape) : at].reshape(shape)

    shard_gain, shard_shift, shard_scale, shard_bias = (give(ln_gain.shape) for _ in range(4))
    shard_bqv = give(b_qv.shape)
    shard_bfc1 = give(b_fc1.shape)
    return (
        block_out,
        grad_input,
        shard_wqkv,
        shard_bqv,
        shard_wout,
        shard_fc1,
        shard_bfc1,
        shard_fc2,
        shard_gain,
        shard_shift,
        shard_scale,
        shard_bias,
    )


def solution(mesh):
    rows = P("dp", "tensor", None)
    vector = P(None, ("dp", "tensor"))
    weights = (
        P(None, "dp", "tensor"),
        P(None, "dp", "tensor"),
        P("tensor", "dp"),
        P("dp", "tensor"),
        P("dp", "tensor"),
        P("tensor", "dp"),
    )
    return jax.shard_map(
        body,
        mesh=mesh,
        in_specs=(rows, rows, P("dp")) + weights + (vector,) * 4,
        out_specs=(rows, rows) + weights + (vector,) * 4,
        check_vma=False,
    )
```

time: 1060 us -> 757 us (0.71)
  waiting for transfers between devices: 289 us -> 0 us
  Pallas kernels: 252 us -> 501 us
  blocking collectives: 150 us -> 0 us
  local copies, waits for them, and re-layouts: 147 us -> 101 us
  starting transfers between devices: 44.9 us -> 0 us
  matrix products: 88.4 us -> 58 us
  other arithmetic: 61.9 us -> 84.9 us
  between operations: 17.1 us -> 2.35 us
    reduce_scatter x12 -> x0, waiting for transfers between devices: 258 us -> none  [the longest x6 143 us: reduced(): part = lax.psum_scatter(grad, 'dp', scatter_dimension=0, tiled=True)]
    pallas_call x3 -> x6, Pallas kernels: 252 us -> 501 us  [the longest x1 149 us: attend_backward(): pl.pallas_call(functools.partial(attend_backward_kernel, groups, line, ro...]
    dynamic_update_slice x8 -> x0, local copies, waits for them, and re-layouts: 74.8 us -> none  [the longest x6 57.8 us: to_owner(): lax.dynamic_update_slice(out, sent, ((place - shift) % line * part_rows, 0))]
    all_gather x3 -> x0, blocking collectives: 55.6 us -> none  [the longest x1 27.2 us: body(): lax.all_gather(w_qkv, 'tensor', axis=2, tiled=True)]
    unnamed x1 -> x0, blocking collectives: 50.6 us -> none
    ppermute x12 -> x0, starting transfers between devices: 43.9 us -> none  [the longest x6 24.3 us: to_owner(): lax.ppermute(x[jnp.minimum(image, images - 1)], ('dp', 'tensor'), pairs)]
    psum x2 -> x0, blocking collectives: 43.8 us -> none  [body(): small_grads = lax.psum(lax.psum(small_grads, 'tensor'), 'dp')]
    dot_general x12 -> x9, matrix products: 88.4 us -> 58 us  [the longest x4 22.3 us: body(): jnp.einsum('sd,stc->tdc', a, b.reshape(split), preferred_element_type=f32)]
  transfers between devices with their start and end apart: 30 -> 0, of which waited for: 12 -> 0; matrix products, arithmetic and copies ran while one was open for 24% -> 0% of each run, Pallas kernels for 15% -> 0%
where the time goes in v2:
time: 757 us; the launch traced here: 748 us
  Pallas kernels  501 us (66%)
  local copies, waits for them, and re-layouts  101 us (13%)
  other arithmetic  84.9 us (11%)
  matrix products  58 us (8%)
    pallas_call x1, Pallas kernels, attend_backward(): pl.pallas_call(functools.partial(attend_backward_kernel, groups, line, ro...  149 us
    pallas_call x1, Pallas kernels, attend_forward(): pl.pallas_call(functools.partial(attend_forward_kernel, groups, line, row...  103 us
    pallas_call x1, Pallas kernels, feed_forward(): pl.pallas_call(functools.partial(feed_forward_kernel, tile), grid=(units...  94 us
    pallas_call x1, Pallas kernels, leave(): pl.pallas_call(functools.partial(leave_kernel, groups, line, r), in_specs...  73.9 us
    pallas_call x1, Pallas kernels, arrive(): pl.pallas_call(functools.partial(arrive_kernel, groups, line), in_specs=[...  68.4 us
    dot_general x4, matrix products, body(): jnp.einsum('sd,stc->tdc', a, b.reshape(split), preferred_element_type=f32)  22.3 us
    dot_general x3, matrix products, body(): jnp.einsum('stc,tdc->sd', g.reshape(split), weights[:, :, n * cols:(n + 1...  20.8 us
    reduce_sum x1, other arithmetic, body(): grad_scale2 = jnp.sum(grad_out * mlp, axis=0)  15.7 us

profile of v2, /device:TPU:0, one launch (start us, length us, event | category | flops | bytes accessed | tf_op | source)
XLA Modules:
  0.0 747.6 jit_solution(2390581235655719255)
XLA Ops:
  16.1 68.4 %arrive.1 = (bf16[4,344,1024]{2,1,0:T(8,128)(2,1)}, bf16[4,1024,1024]{2,1,0:T(8,128)(2,1)}, f32[4,64,128]{2,1,0:T(8,128)}) custom-call(bf16[3,344,1024]{2,1,0:T(8,128)(2,1)} %x_ref.1, bf16[128,1024]{1,0:T(8,128)(2,1)} %pad_maximum_fusion.3.shard_ref, f32[8,128]{1,0:T(8,128)} %pad_bitcast_fusion.small_ref), custom_call_target="tpu_custom_call" | custom-call | tf_op jit(solution)/shard_map/arrive/pallas_call | solution.py:414
  102.1 6.2 add_convert_fusion.3
  111.1 6.2 copy.165
  117.3 5.1 add_convert_fusion.2
  128.9 12.9 %project.1.q_ref.k_ref.v_ref = bf16[3,1376,1024]{2,1,0:T(8,128)(2,1)} custom-call(bf16[1376,1024]{1,0:T(8,128)(2,1)S(1)} %copy.172.n1_ref, bf16[4,1024,1024]{2,1,0:T(8,128)(2,1)S(1)} %copy-done.2, f32[3,1,1024]{2,1,0:T(1,128)S(1)} %pad_maximum_fusion.4.b_ref), custom_call_target="tpu_custom_call" | custom-call | flops 8657043456 | bytes 22544384 | tf_op jit(solution)/shard_map/project/pallas_call | solution.py:482
  141.8 103.4 %attend_forward.1 = (bf16[1376,1024]{1,0:T(8,128)(2,1)}, bf16[16,1376,128]{2,1,0:T(8,128)(2,1)}, bf16[4,1024,2048]{2,1,0:T(8,128)(2,1)}, bf16[4,344,1024]{2,1,0:T(8,128)(2,1)}) custom-call(s32[1]{0:T(128)} %bitcast.1.len_ref, bf16[3,1376,1024]{2,1,0:T(8,128)(2,1)} %project.1.q_ref.k_ref.v_ref, bf16[3,1376,1024]{2,1,0:T(8,128)(2,1)} %project.1.q_ref.k_ref.v_ref, ...), custom_call_target="tpu_custom_call" | custom-call | flops 31021072384 | bytes 16908288 | tf_op jit(solution)/shard_map/attend_forward/pallas_call | solution.py:569
  252.6 6.2 copy.175
  258.7 5.0 fusion.57.gmt_ref
  264.2 14.3 %copy.184.gm_ref = bf16[1376,1024]{1,0:T(8,128)(2,1)} copy(bf16[1376,1024]{0,1:T(8,128)(2,1)S(1)} %multiply_convert_fusion.1) | data formatting | bytes 5636096 | tf_op jit(solution)/shard_map/convert_element_type | solution.py:914
  278.5 10.2 %fusion.45 = (f32[1376]{0:T(1024)S(1)}, f32[1376,1024]{0,1:T(8,128)S(1)}, f32[1376,1024,1]{0,1,2:T(8,128)}) fusion(f32[1376,1024]{0,1:T(8,128)} %copy.165, f32[1024]{0:T(1024)S(1)} %add.101, f32[1024]{0:T(1024)S(1)} %mul.179, bf16[4,1024,1024]{2,1,0:T(8,128)(2,1)} %get-tuple-element.33.w_ref, bf16[172,4,8,256]{3,2,1,0:T(8,128)(2,1)} %bitcast.182), kind=kOutput, calls=%fused_computation.98 | convolution fusion | flops 2891315968 | bytes 21968256 | tf_op jit(solution)/shard_map/stc,tdc->sd/dot_general | solution.py:904
  295.9 94.0 %feed_forward.1 = (f32[1376,1024]{1,0:T(8,128)}, f32[1376,1024]{1,0:T(8,128)}, bf16[4,1024,2048]{2,1,0:T(8,128)(2,1)}, f32[1,4096]{1,0:T(1,128)}) custom-call(bf16[1376,1024]{1,0:T(8,128)(2,1)} %copy.183.n2_ref, bf16[1024,1376]{1,0:T(8,128)(2,1)} %fusion.58.n2t_ref, bf16[1376,1024]{1,0:T(8,128)(2,1)} %copy.184.gm_ref, bf16[1024,1376]{1,0:T(8,128)(2,1)} %fusion.57.gmt_ref, ...), custom_call_target="tpu_custom_call" | custom-call | flops 92341796864 | bytes 33554432 | tf_op jit(solution)/shard_map/feed_forward/pallas_call | solution.py:766
  395.5 6.3 copy.185
  401.7 5.4 multiply_reduce_fusion.2
  407.8 6.3 copy.188
  414.1 15.7 %multiply_reduce_fusion = (f32[1024]{0:T(1024)S(1)}, bf16[1376,1024]{0,1:T(8,128)(2,1)}, f32[1024]{0:T(1024)S(1)}, f32[1024]{0:T(1024)S(1)}, f32[1376,1024]{0,1:T(8,128)}) fusion(f32[1376,1024]{0,1:T(8,128)} %copy.188, f32[1376,1024]{0,1:T(8,128)} %copy.175, f32[1024]{0:T(1024)S(1)} %copy-done.26, f32[1376]{0:T(1024)S(1)} %fusion.43, ...), kind=kLoop, calls=%fused_computation.4 | loop fusion | flops 29586432 | bytes 36694912 | tf_op jit(solution)/shard_map/reduce_sum | solution.py:920
  432.5 8.4 %convert_bitcast_fusion = bf16[4,1024,256]{2,1,0:T(8,128)(2,1)} fusion(bf16[172,4,8,256]{3,2,1,0:T(8,128)(2,1)} %bitcast.183, f32[1376,1024]{0,1:T(8,128)} %get-tuple-element.114, f32[1024]{0:T(1024)S(1)} %mul.179), kind=kOutput, calls=%fused_computation.57 | convolution fusion | flops 2889547776 | bytes 10555392 | tf_op jit(solution)/shard_map/sd,stc->tdc/dot_general | solution.py:950
  441.0 4.8 fusion.38
  451.3 148.9 %attend_backward.1 = (bf16[1376,1024]{1,0:T(8,128)(2,1)}, bf16[1376,1024]{1,0:T(8,128)(2,1)}, bf16[1376,1024]{1,0:T(8,128)(2,1)}, bf16[3,344,1024]{2,1,0:T(8,128)(2,1)}, f32[128,2048]{1,0:T(8,128)}) custom-call(s32[1]{0:T(128)} %bitcast.1.len_ref, bf16[16,1376,128]{2,1,0:T(8,128)(2,1)} %get-tuple-element.34.qa_ref, ...), custom_call_target="tpu_custom_call" | custom-call | flops 77552680960 | bytes 22544384 | tf_op jit(solution)/shard_map/attend_backward/pallas_call | solution.py:685
  610.2 6.3 convert_bitcast_fusion.2
  628.2 5.7 fusion.10
  633.9 5.3 fusion.6
  639.2 9.8 %multiply_reduce_fusion.3 = (f32[1024]{0:T(1024)S(1)}, f32[1376]{0:T(1024)S(1)}, f32[1376]{0:T(1024)S(1)}, f32[1024]{0:T(1024)S(1)}, f32[1376,1024]{0,1:T(8,128)}) fusion(f32[1376,1024]{0,1:T(8,128)S(1)} %bitcast.149, f32[1376]{0:T(1024)S(1)} %copy-done.16, f32[1376]{0:T(1024)S(1)} %copy-done.14, f32[1024]{0:T(1024)S(1)} %copy-done.23, ...), kind=kOutput, calls=%fused_computation.7 | convolution fusion | flops 2901175808 | bytes 27630336 | tf_op jit(solution)/shard_map/stc,tdc->sd/dot_general | solution.py:960
  649.0 6.6 add_convert_fusion
  662.7 73.9 %leave.1 = (bf16[3,344,1024]{2,1,0:T(8,128)(2,1)S(1)}, f32[128,1024]{1,0:T(8,128)S(1)}, f32[8,128]{1,0:T(8,128)S(1)}) custom-call(bf16[4,344,1024]{2,1,0:T(8,128)(2,1)S(1)} %bitcast.145, bf16[4,1024,1024]{2,1,0:T(8,128)(2,1)S(1)} %copy-done, f32[4,64,128]{2,1,0:T(8,128)S(1)} %reshape.394.smalls_ref), custom_call_target="tpu_custom_call" | custom-call | tf_op jit(solution)/shard_map/leave/pallas_call | solution.py:453
  (197 shorter events, 110.2 us)
Async XLA Ops:
  85.4 16.7 %copy-start.5 = (bf16[4,344,1024]{2,1,0:T(8,128)(2,1)S(1)}, bf16[4,344,1024]{2,1,0:T(8,128)(2,1)}, u32[]{:S(2)}) copy-start(bf16[4,344,1024]{2,1,0:T(8,128)(2,1)} %get-tuple-element.31) | copy-start | bytes 8454148
  90.9 11.0 %copy-start.24 = (f32[4,344]{1,0:T(4,128)}, f32[4,344]{1,0:T(4,128)S(1)}, u32[]{:S(2)}) copy-start(f32[4,344]{1,0:T(4,128)S(1)} %add_rsqrt_fusion.1) | copy-start | bytes 16516
  91.0 26.3 %copy-start.13 = (f32[1376]{0:T(1024)}, f32[1376]{0:T(1024)S(1)}, u32[]{:S(2)}) copy-start(f32[1376]{0:T(1024)S(1)} %rsqrt.21) | copy-start | bytes 16516
  91.0 26.2 %copy-start.15 = (f32[1376]{0:T(1024)}, f32[1376]{0:T(1024)S(1)}, u32[]{:S(2)}) copy-start(f32[1376]{0:T(1024)S(1)} %div.27) | copy-start | bytes 16516
  100.7 16.5 %copy-start.22 = (f32[1024]{0:T(1024)}, f32[1024]{0:T(1024)S(1)}, u32[]{:S(2)}) copy-start(f32[1024]{0:T(1024)S(1)} %mul.174) | copy-start | bytes 12292
  141.8 103.4 %copy-start.25 = (f32[4,344]{1,0:T(4,128)S(1)}, f32[4,344]{1,0:T(4,128)}, u32[]{:S(2)}) copy-start(f32[4,344]{1,0:T(4,128)} %fusion.44) | copy-start | bytes 16516
  258.7 5.0 copy-start.4
  407.1 7.0 copy-start.26
  431.7 9.3 %slice-start.4 = ((s8[5767168]{0:T(1024)(128)(4,1)}), s8[1572864]{0:T(1024)(128)(4,1)S(1)}, s32[]{:S(2)}) async-start(s8[5767168]{0:T(1024)(128)(4,1)} %bitcast.150), calls=%async_computation.4 | async-start | bytes 3145728
  432.5 8.4 %slice-start.5 = ((s8[5767168]{0:T(1024)(128)(4,1)}), s8[4194304]{0:T(1024)(128)(4,1)S(1)}, s32[]{:S(2)}) async-start(s8[5767168]{0:T(1024)(128)(4,1)} %bitcast.150), calls=%async_computation.5 | async-start | bytes 8388608
  600.2 5.1 copy-start.12
  610.2 6.3 copy-start.7
  610.2 6.3 copy-start.9
  616.5 11.6 %slice-start = ((s8[8388608]{0:T(1024)(128)(4,1)}), s8[4194304]{0:T(1024)(128)(4,1)S(1)}, s32[]{:S(2)}) async-start(s8[8388608]{0:T(1024)(128)(4,1)} %bitcast.146), calls=%async_computation | async-start | bytes 8388608
  620.4 3.9 copy-start.11
  620.4 7.8 %slice-start.1 = ((s8[8388608]{0:T(1024)(128)(4,1)}), s8[4194304]{0:T(1024)(128)(4,1)S(1)}, s32[]{:S(2)}) async-start(s8[8388608]{0:T(1024)(128)(4,1)} %bitcast.146), calls=%async_computation.1 | async-start | bytes 8388608
  628.2 5.7 copy-start.27
  628.2 11.0 %slice-start.2 = ((s8[5767168]{0:T(1024)(128)(4,1)}), s8[4194304]{0:T(1024)(128)(4,1)S(1)}, s32[]{:S(2)}) async-start(s8[5767168]{0:T(1024)(128)(4,1)} %bitcast.148), calls=%async_computation.2 | async-start | bytes 8388608
  633.8 5.3 slice-start.3
  633.8 5.3 copy-start.14
  633.8 5.3 copy-start.16
  633.8 5.3 copy-start.23
  649.0 9.8 %copy-start.21 = (f32[1,8,4,32]{3,2,1,0:T(4,128)S(1)}, f32[1,8,4,32]{3,2,1,0:T(4,128)}, u32[]{:S(2)}) copy-start(f32[1,8,4,32]{3,2,1,0:T(4,128)} %stack.70) | copy-start | bytes 12292
  738.0 7.8 %copy-start.10 = (bf16[3,344,1024]{2,1,0:T(8,128)(2,1)S(1)}, bf16[3,344,1024]{2,1,0:T(8,128)(2,1)}, u32[]{:S(2)}) copy-start(bf16[3,344,1024]{2,1,0:T(8,128)(2,1)} %get-tuple-element.159) | copy-start | bytes 6340612
  (10 other events, 32.5 us)

commit v3 on v2

--- a/solution.py
+++ b/solution.py
@@ -14,6 +14,7 @@
 NEG = -1e30
 NT = (((1,), (1,)), ((), ()))
 NN = (((1,), (0,)), ((), ()))
+TN = (((0,), (0,)), ((), ()))
 f32 = jnp.float32
 bf16 = jnp.bfloat16
 
@@ -277,7 +278,7 @@
         return [
             pltpu.VMEM((chips, line, r, c), dtype),
             pltpu.VMEM((chips, line, r, c), dtype),
-            pltpu.VMEM((chips, line, r, c), dtype),
+            pltpu.VMEM((chips - 1, line, r, c), dtype),
             pltpu.VMEM((line, r, c), dtype),
             DMA((chips, line)),
             DMA((chips, line)),
@@ -317,7 +318,7 @@
         if at.square and mask == 6:
             peer = 4 if k < at.line // 2 else 2
         return remote(
-            self.sums.at[m, k], self.dbuf.at[m, k], self.ds.at[m, k], self.dr.at[m, k],
+            self.sums.at[m, k], self.dbuf.at[m - 1, k], self.ds.at[m, k], self.dr.at[m, k],
             (flipped(at.g, peer), at.z),
         )
 
@@ -355,13 +356,13 @@
         if at.square:
             mask = 2 if k < at.line // 2 else 4
             self.across(6, k).wait_recv()
-            self.add(mask // 2, k, self.dbuf[3, k])
+            self.add(mask // 2, k, self.dbuf[2, k])
             self.across(mask, k).start()
 
     def own(self, k):
         for mask in self.at.direct:
             self.across(mask, k).wait_recv()
-            self.add(0, k, self.dbuf[mask // 2, k])
+            self.add(0, k, self.dbuf[mask // 2 - 1, k])
         if k:
             self.along(k).start()
 
@@ -426,75 +427,321 @@
     )(x, shard, small)
 
 
-def leave_kernel(groups, line, r, y_ref, full_ref, smalls_ref, yo_ref, shard_ref, small_ref, *scratch):
+def leave_kernel(
+    groups, line, gq_ref, gk_ref, gv_ref, w_ref, n1t_ref, x_ref, gh_ref, v_ref, smalls_ref,
+    yo_ref, shard_ref, small_ref, gn, y, full, smalls, *scratch
+):
     at = Place(groups, line)
     n = len(ToOwner.sems(groups, line))
     m = (len(scratch) - n) // 2
-    rows = FromOwner(at, y_ref, yo_ref, scratch[:n])
-    weights = Reduce(at, full_ref, scratch[n : n + m], r)
-    small = Reduce(at, smalls_ref, scratch[n + m :], small_ref.shape[0])
-    at.barrier()
-    for one, two in zip(weights.steps(), small.steps()):
-        one()
-        two()
-        if two == small.start:
-            rows.start()
-    shard_ref[...] = weights.finish()
-    small_ref[...] = small.finish()
-    rows.finish()
-
-
-def leave(groups, line, images, y, full, smalls):
-    _, part_rows, width = y.shape
-    _, r, c = full.shape
-    r = r // groups
+    rows = FromOwner(at, y, yo_ref, scratch[:n])
+    weights = Reduce(at, full, scratch[n : n + m], shard_ref.shape[0])
+    small = Reduce(at, smalls, scratch[n + m :], small_ref.shape[0])
+    step = pl.program_id(0)
+    cols = gq_ref.shape[1]
+    grads = (gq_ref, gk_ref, gv_ref)
+
+    @pl.when(step == 0)
+    def _():
+        at.barrier()
+        smalls[...] = smalls_ref[...]
+        gn[...] = jnp.zeros_like(gn)
+
+    @pl.when(step < line)
+    def _():
+        for i, ref in enumerate(grads):
+            gn[...] += lax.dot_general(
+                ref[...], w_ref[0, :, i * cols : (i + 1) * cols], NT, preferred_element_type=f32
+            )
+
+    @pl.when(step == line - 1)
+    def _():
+        part = x_ref.shape[1]
+
+        def piece(p, carry):
+            gain, shift = carry
+            hat, inverse = norm_stats(x_ref[p].astype(f32))
+            g = gn[p * part : (p + 1) * part]
+            y[p] = (gh_ref[p] + norm_back(g, hat, inverse, v_ref[0:1])).astype(bf16)
+            gain += jnp.sum(g * hat, axis=0, keepdims=True)
+            return gain, shift + jnp.sum(g, axis=0, keepdims=True)
+
+        zero = jnp.zeros((1, gn.shape[1]), f32)
+        carry = (zero, zero)
+        for p in range(line):
+            carry = piece(p, carry)
+        rows.start()
+        wide = gn.shape[1] // groups
+        for j, total in enumerate(carry):
+            for g in range(groups):
+                row = total[:, g * wide : (g + 1) * wide]
+                if wide < LANES:
+                    row = jnp.concatenate([row, jnp.zeros((1, LANES - wide), f32)], axis=1)
+                at_row = g * small_ref.shape[0] + 2 * j
+                for t in range(line):
+                    smalls[t, at_row : at_row + 1, :] = row
+        small.start()
+
+    for t in range(line):
+
+        @pl.when(step == line + t)
+        def _(t=t):
+            for i, ref in enumerate(grads):
+                full[t, :, i * cols : (i + 1) * cols] = lax.dot_general(
+                    n1t_ref[...], ref[...], NN, preferred_element_type=f32
+                ).astype(bf16)
+
+    @pl.when(step == 2 * line - 1)
+    def _():
+        for one, two in zip(weights.steps(), small.steps()):
+            one()
+            if two != small.start:
+                two()
+        shard_ref[...] = weights.finish()
+        small_ref[...] = small.finish()
+        rows.finish()
+
+
+def leave(groups, line, images, gq, gk, gv, weights, n1t, x, ghid, vectors, smalls):
+    _, part, width = x.shape
+    rows = line * part
+    cols = width // line
+    r, c = width // groups, 3 * cols
     sr, sc = smalls.shape[1] // groups, smalls.shape[2]
-    vmem = pl.BlockSpec(memory_space=pltpu.VMEM)
+    grad = pl.BlockSpec((rows, cols), lambda j: (0, j % line))
     return pl.pallas_call(
-        functools.partial(leave_kernel, groups, line, r),
-        in_specs=[ANY] * 3,
-        out_specs=[ANY, vmem, vmem],
+        functools.partial(leave_kernel, groups, line),
+        grid=(2 * line,),
+        in_specs=[
+            grad,
+            grad,
+            grad,
+            pl.BlockSpec((1, width, c), lambda j: (jnp.minimum(j, line - 1), 0, 0)),
+            whole(width, rows),
+            whole(line, part, width),
+            whole(line, part, width),
+            whole(*vectors.shape),
+            whole(*smalls.shape),
+        ],
+        out_specs=[ANY, whole(r, c), whole(sr, sc)],
         out_shape=[
-            jax.ShapeDtypeStruct((images, part_rows, width), y.dtype),
+            jax.ShapeDtypeStruct((images, part, width), bf16),
             jax.ShapeDtypeStruct((r, c), f32),
             jax.ShapeDtypeStruct((sr, sc), f32),
         ],
-        scratch_shapes=ToOwner.sems(groups, line)
-        + Reduce.scratch(groups, line, r, c, full.dtype)
-        + Reduce.scratch(groups, line, sr, sc, smalls.dtype),
+        scratch_shapes=[
+            pltpu.VMEM((rows, width), f32),
+            pltpu.VMEM((line, part, width), bf16),
+            pltpu.VMEM((line, width, c), bf16),
+            pltpu.VMEM(smalls.shape, f32),
+        ]
+        + ToOwner.sems(groups, line)
+        + Reduce.scratch(groups, line, r, c, bf16)
+        + Reduce.scratch(groups, line, sr, sc, f32),
         compiler_params=pltpu.CompilerParams(
-            collective_id=2, has_side_effects=True, vmem_limit_bytes=40 * 2**20
+            collective_id=2, has_side_effects=True, vmem_limit_bytes=62 * 2**20
         ),
         name="leave",
-    )(y, full, smalls)
-
-
-def project_kernel(n1_ref, w_ref, b_ref, out_ref):
+    )(gq, gk, gv, weights, n1t, x, ghid, vectors, smalls)
+
+
+def norm_stats(values):
+    center = values - jnp.mean(values, axis=-1, keepdims=True)
+    inverse = lax.rsqrt(jnp.mean(center * center, axis=-1, keepdims=True) + 1e-06)
+    return center * inverse, inverse
+
+
+def norm_back(grad_norm, normed, inverse, gain):
+    scaled = grad_norm * gain
+    return inverse * (
+        scaled
+        - jnp.mean(scaled, axis=-1, keepdims=True)
+        - normed * jnp.mean(scaled * normed, axis=-1, keepdims=True)
+    )
+
+
+def project_kernel(flag_ref, x_ref, v_ref, w_ref, b_ref, out_ref, xc_ref, n1t_ref, n1):
+    @pl.when((pl.program_id(0) == 0) & (pl.program_id(1) == 0))
+    def _():
+        rows = x_ref.shape[0]
+        size = 32 if rows % 32 == 0 else 16
+
+        def chunk(i, carry):
+            r = pl.ds(pl.multiple_of(i * size, 16), size)
+            x = jnp.where(flag_ref[1] > 0, x_ref[r, :].astype(f32), 0.0)
+            xc_ref[r, :] = x.astype(bf16)
+            hat, _ = norm_stats(x)
+            n1[r, :] = (hat * v_ref[0:1] + v_ref[2:3]).astype(bf16)
+            return carry
+
+        lax.fori_loop(0, rows // size, chunk, 0)
+        n1t_ref[...] = n1[...].T
+
     scale = jnp.where(pl.program_id(1) == 0, HD ** (-0.5) * LOG2E, 1.0)
-    out = lax.dot_general(n1_ref[...], w_ref[0], NN, preferred_element_type=f32) + b_ref[0]
+    out = lax.dot_general(n1[...], w_ref[0], NN, preferred_element_type=f32) + b_ref[0]
     out_ref[0] = (out * scale).astype(bf16)
 
 
-def project(normed1, weights, bias):
-    rows, width = normed1.shape
+def whole(*shape):
+    return pl.BlockSpec(shape, lambda *_: (0,) * len(shape), pipeline_mode=pl.Buffered(1))
+
+
+SMEM = pl.BlockSpec(memory_space=pltpu.SMEM)
+
+
+def project(flags, x, vectors, weights, bias):
+    rows, width = x.shape
     line = weights.shape[0]
     cols = width // line
     return pl.pallas_call(
         project_kernel,
         grid=(line, 3),
         in_specs=[
-            pl.BlockSpec((rows, width), lambda t, k: (0, 0), pipeline_mode=pl.Buffered(1)),
+            SMEM,
+            whole(rows, width),
+            whole(*vectors.shape),
             pl.BlockSpec((1, width, cols), lambda t, k: (t, 0, k)),
             pl.BlockSpec((1, 1, cols), lambda t, k: (k, 0, t)),
         ],
-        out_specs=pl.BlockSpec((1, rows, cols), lambda t, k: (k, 0, t)),
-        out_shape=jax.ShapeDtypeStruct((3, rows, width), bf16),
+        out_specs=[
+            pl.BlockSpec((1, rows, cols), lambda t, k: (k, 0, t)),
+            whole(rows, width),
+            whole(width, rows),
+        ],
+        out_shape=[
+            jax.ShapeDtypeStruct((3, rows, width), bf16),
+            jax.ShapeDtypeStruct((rows, width), bf16),
+            jax.ShapeDtypeStruct((width, rows), bf16),
+        ],
+        scratch_shapes=[pltpu.VMEM((rows, width), bf16)],
         compiler_params=pltpu.CompilerParams(vmem_limit_bytes=40 * 2**20),
         cost_estimate=pl.CostEstimate(
             flops=6 * rows * width * width, bytes_accessed=16 * rows * width, transcendentals=0
         ),
         name="project",
-    )(normed1, weights, bias)
+    )(flags, x, vectors, weights, bias)
+
+
+def valid_rows(flag_ref, shape):
+    row = pl.program_id(0) * shape[0] + lax.broadcasted_iota(jnp.int32, shape, 0)
+    return row < flag_ref[0]
+
+
+def middle_kernel(flag_ref, ctx_ref, x_ref, cot_ref, v_ref, w_ref, hid_ref, n2_ref, gm_ref):
+    line, _, cols = w_ref.shape
+    attn = v_ref[6:7]
+    for t in range(line):
+        part = ctx_ref[0, :, t * cols : (t + 1) * cols]
+        attn = attn + lax.dot_general(part, w_ref[t], NT, preferred_element_type=f32)
+    hidden = x_ref[0].astype(f32) + v_ref[4:5] * attn
+    hid_ref[0] = hidden
+    hat, _ = norm_stats(hidden)
+    n2_ref[0] = (hat * v_ref[1:2] + v_ref[3:4]).astype(bf16)
+    gout = jnp.where(valid_rows(flag_ref, hidden.shape), cot_ref[0].astype(f32), 0.0)
+    gm_ref[0] = (gout * v_ref[5:6]).astype(bf16)
+
+
+def middle(flags, context, x, cot, vectors, weights):
+    line, part, width = x.shape
+    cols = width // line
+    piece = pl.BlockSpec((1, part, width), lambda p: (p, 0, 0))
+    return pl.pallas_call(
+        middle_kernel,
+        grid=(line,),
+        in_specs=[
+            SMEM,
+            piece,
+            piece,
+            piece,
+            whole(*vectors.shape),
+            pl.BlockSpec(
+                (line, width, cols), lambda p: (0, 0, 3), pipeline_mode=pl.Buffered(1)
+            ),
+        ],
+        out_specs=[piece] * 3,
+        out_shape=[
+            jax.ShapeDtypeStruct(x.shape, f32),
+            jax.ShapeDtypeStruct(x.shape, bf16),
+            jax.ShapeDtypeStruct(x.shape, bf16),
+        ],
+        compiler_params=pltpu.CompilerParams(vmem_limit_bytes=40 * 2**20),
+        name="middle",
+    )(flags, context, x, cot, vectors, weights)
+
+
+def turn_kernel(
+    flag_ref, mlp_ref, gn_ref, hid_ref, x_ref, cot_ref, ctx_ref, v_ref, w_ref,
+    out_ref, gh_ref, gc_ref, gw_ref, sum_ref, acc
+):
+    step = pl.program_id(0)
+    line, _, cols = w_ref.shape
+    hidden = hid_ref[0]
+    mlp = mlp_ref[0] + v_ref[7:8]
+    gn = gn_ref[0]
+    valid = valid_rows(flag_ref, hidden.shape)
+    out_ref[0] = jnp.where(valid, hidden + v_ref[5:6] * mlp, 0.0).astype(bf16)
+    gout = jnp.where(valid, cot_ref[0].astype(f32), 0.0)
+    hat, inverse = norm_stats(hidden)
+    ghid = gout + norm_back(gn, hat, inverse, v_ref[1:2])
+    gh_ref[0] = ghid
+    gattn = ghid * v_ref[4:5]
+    attn = (hidden - x_ref[0].astype(f32)) / v_ref[4:5]
+
+    def total(x):
+        return jnp.sum(x, axis=0, keepdims=True)
+
+    sums = [gn * hat, gn, ghid * attn, gout * mlp, gattn, gout * v_ref[5:6]]
+    sums = jnp.concatenate([total(x) for x in sums] + [jnp.zeros((2, gn.shape[1]), f32)], axis=0)
+
+    @pl.when(step == 0)
+    def _():
+        sum_ref[...] = sums
+        acc[...] = jnp.zeros_like(acc)
+
+    @pl.when(step > 0)
+    def _():
+        sum_ref[...] += sums
+
+    gattn = gattn.astype(bf16)
+    for t in range(line):
+        part = ctx_ref[0, :, t * cols : (t + 1) * cols]
+        gc_ref[0, :, t * cols : (t + 1) * cols] = lax.dot_general(
+            gattn, w_ref[t], NN, preferred_element_type=f32
+        ).astype(bf16)
+        acc[t] += lax.dot_general(gattn, part, TN, preferred_element_type=f32)
+
+    @pl.when(step == line - 1)
+    def _():
+        gw_ref[...] = acc[...].astype(bf16)
+
+
+def turn(flags, mlp, gn, hidden, x, cot, context, vectors, weights):
+    line, part, width = x.shape
+    cols = width // line
+    piece = pl.BlockSpec((1, part, width), lambda p: (p, 0, 0))
+    return pl.pallas_call(
+        turn_kernel,
+        grid=(line,),
+        in_specs=[SMEM]
+        + [piece] * 6
+        + [
+            whole(*vectors.shape),
+            pl.BlockSpec(
+                (line, width, cols), lambda p: (0, 0, 3), pipeline_mode=pl.Buffered(1)
+            ),
+        ],
+        out_specs=[piece] * 3 + [whole(line, width, cols), whole(8, width)],
+        out_shape=[
+            jax.ShapeDtypeStruct(x.shape, bf16),
+            jax.ShapeDtypeStruct(x.shape, f32),
+            jax.ShapeDtypeStruct(x.shape, bf16),
+            jax.ShapeDtypeStruct((line, width, cols), bf16),
+            jax.ShapeDtypeStruct((8, width), f32),
+        ],
+        scratch_shapes=[pltpu.VMEM((line, width, cols), f32)],
+        compiler_params=pltpu.CompilerParams(vmem_limit_bytes=56 * 2**20),
+        name="turn",
+    )(flags, mlp, gn, hidden, x, cot, context, vectors, weights)
 
 
 def attend_forward_kernel(
@@ -594,14 +841,25 @@
 
 def attend_backward_kernel(
     groups, line, rows, padded, blocks, len_ref, qa_ref, k_ref, v_ref, gc_ref, ctx_ref, y_ref, full_ref,
-    gq_ref, gk_ref, gv_ref, yo_ref, shard_ref, ka, va, qs, ga, acc, *scratch
+    out_ref, gq_ref, gk_ref, gv_ref, gb_ref, yo_ref, shard_ref, oshard_ref, ka, va, qs, ga, acc, *scratch
 ):
     at = Place(groups, line)
     n = len(ToOwner.sems(groups, line))
     back = FromOwner(at, y_ref, yo_ref, scratch[:n])
-    weights = Reduce(at, full_ref, scratch[n:], shard_ref.shape[0])
-    steps = weights.steps()
+    m = (len(scratch) - n) // 2
+    weights = Reduce(at, full_ref, scratch[n : n + m], shard_ref.shape[0])
+    out_weights = Reduce(at, out_ref, scratch[n + m :], oshard_ref.shape[0])
+    pairs = list(zip(weights.steps(), out_weights.steps()))
     chips = groups // 2
+
+    def both(i):
+        def run():
+            for work in pairs[i]:
+                work()
+
+        return run
+
+    steps = [both(i) for i in range(len(pairs))]
 
     def begin():
         at.barrier()
@@ -651,16 +909,24 @@
             gv = lax.dot_general(p.astype(bf16), ga[...], NN, preferred_element_type=f32)
             gk = lax.dot_general(ds, qs[...], NN, preferred_element_type=f32) * (1.0 / LOG2E)
             acc[...] += lax.dot_general(kb.T, ds, NN, preferred_element_type=f32)
+            bv = carry + jnp.sum(gv, axis=0, keepdims=True)
             if half == 0:
                 gv_ref[r, :] = gv.astype(bf16)
                 gk_ref[r, :] = gk.astype(bf16)
             else:
                 gv_ref[r, :] = jnp.where(ownb, gv, gv_ref[r, :].astype(f32)).astype(bf16)
                 gk_ref[r, :] = jnp.where(ownb, gk, gk_ref[r, :].astype(f32)).astype(bf16)
-            return carry
-
-        lax.fori_loop(0, blocks, block, 0)
+            return bv
+
+        bv = lax.fori_loop(0, blocks, block, jnp.zeros((1, LANES), f32))
         gq = acc[...].T[:rows] * HD ** (-0.5)
+        sums = jnp.concatenate(
+            [jnp.sum(gq, axis=0, keepdims=True), bv, jnp.zeros((6, LANES), f32)], axis=0
+        )
+        if half == 0:
+            gb_ref[0] = sums
+        else:
+            gb_ref[0] = jnp.where(own[:8], sums, gb_ref[0])
         if half == 0:
             gq_ref[...] = gq.astype(bf16)
         else:
@@ -669,15 +935,16 @@
     @pl.when(step == pl.num_programs(0) - 1)
     def _():
         shard_ref[...] = weights.finish()
+        oshard_ref[...] = out_weights.finish()
         back.finish()
 
 
-def attend_backward(groups, line, images, length, qa, qkv, gc, ctx, y, full):
+def attend_backward(groups, line, images, length, qa, qkv, gc, ctx, y, full, out_full):
     _, rows, width = qkv.shape
     padded = round_up(rows, LANES)
     blocks = 2 if rows % 32 == 0 else 1
     spec = pl.BlockSpec((rows, LANES), lambda j: (0, j))
-    r, c = full.shape[1] // groups, full.shape[2]
+    r, c, oc = full.shape[1] // groups, full.shape[2], out_full.shape[2]
 
     def third(n):
         return pl.BlockSpec((None, rows, LANES), lambda j: (n, 0, j))
@@ -694,10 +961,17 @@
             spec,
             ANY,
             ANY,
-        ],
-        out_specs=[spec] * 3 + [ANY, pl.BlockSpec((r, c), lambda j: (0, 0))],
+            ANY,
+        ],
+        out_specs=[spec] * 3
+        + [pl.BlockSpec((1, 8, LANES), lambda j: (j, 0, 0)), ANY, whole(r, c), whole(r, oc)],
         out_shape=[jax.ShapeDtypeStruct((rows, width), bf16)] * 3
-        + [jax.ShapeDtypeStruct((images,) + y.shape[1:], y.dtype), jax.ShapeDtypeStruct((r, c), f32)],
+        + [
+            jax.ShapeDtypeStruct((width // LANES, 8, LANES), f32),
+            jax.ShapeDtypeStruct((images,) + y.shape[1:], y.dtype),
+            jax.ShapeDtypeStruct((r, c), f32),
+            jax.ShapeDtypeStruct((r, oc), f32),
+        ],
         scratch_shapes=[
             pltpu.VMEM((rows, LANES), bf16),
             pltpu.VMEM((rows, LANES), bf16),
@@ -706,7 +980,8 @@
             pltpu.VMEM((LANES, padded), f32),
         ]
         + ToOwner.sems(groups, line)
-        + Reduce.scratch(groups, line, r, c, full.dtype),
+        + Reduce.scratch(groups, line, r, c, full.dtype)
+        + Reduce.scratch(groups, line, r, oc, full.dtype),
         compiler_params=pltpu.CompilerParams(
             collective_id=4, has_side_effects=True, vmem_limit_bytes=62 * 2**20
         ),
@@ -716,13 +991,19 @@
             transcendentals=rows * rows * width // HD,
         ),
         name="attend_backward",
-    )(length, qa, qkv, qkv, gc, ctx, y, full)
+    )(length, qa, qkv, qkv, gc, ctx, y, full, out_full)
 
 
 def feed_forward_kernel(
-    tile, n2_ref, n2t_ref, gm_ref, gmt_ref, w_ref, b1_ref, mlp_ref, gn_ref, gw_ref, gb_ref
+    tile, n2_ref, gm_ref, w_ref, b1_ref, mlp_ref, gn_ref, gw_ref, gb_ref, n2t, gmt
 ):
     step = pl.program_id(0)
+
+    @pl.when(step == 0)
+    def _():
+        n2t[...] = n2_ref[...].T
+        gmt[...] = gm_ref[...].T
+
     w1 = w_ref[0, :, :tile]
     w2t = w_ref[0, :, tile:]
     pre = lax.dot_general(n2_ref[...], w1, NN, preferred_element_type=f32) + b1_ref[...]
@@ -747,20 +1028,17 @@
         gn_ref[...] += gn
 
     gw_ref[0, :, :tile] = lax.dot_general(
-        n2t_ref[...], gpre, NN, preferred_element_type=f32
+        n2t[...], gpre, NN, preferred_element_type=f32
     ).astype(bf16)
     gw_ref[0, :, tile:] = lax.dot_general(
-        gmt_ref[...], act, NN, preferred_element_type=f32
+        gmt[...], act, NN, preferred_element_type=f32
     ).astype(bf16)
 
 
-def feed_forward(n2, n2t, gm, gmt, weights, b1, tile):
+def feed_forward(n2, gm, weights, b1, tile):
     rows, width = n2.shape
     units = b1.shape[1]
     per = weights.shape[2] // (2 * tile)
-
-    def whole(a, b):
-        return pl.BlockSpec((a, b), lambda j: (0, 0), pipeline_mode=pl.Buffered(1))
 
     both = pl.BlockSpec((1, width, 2 * tile), lambda j: (j // per, 0, j % per))
     return pl.pallas_call(
@@ -768,9 +1046,7 @@
         grid=(units // tile,),
         in_specs=[
             whole(rows, width),
-            whole(width, rows),
             whole(rows, width),
-            whole(width, rows),
             both,
             pl.BlockSpec((1, tile), lambda j: (0, j)),
         ],
@@ -786,6 +1062,7 @@
             jax.ShapeDtypeStruct(weights.shape, bf16),
             jax.ShapeDtypeStruct((1, units), f32),
         ],
+        scratch_shapes=[pltpu.VMEM((width, rows), bf16), pltpu.VMEM((width, rows), bf16)],
         compiler_params=pltpu.CompilerParams(vmem_limit_bytes=60 * 2**20),
         cost_estimate=pl.CostEstimate(
             flops=16 * rows * width * units,
@@ -793,23 +1070,7 @@
             transcendentals=2 * rows * units,
         ),
         name="feed_forward",
-    )(n2, n2t, gm, gmt, weights, b1)
-
-
-def norm_rows(values, gain, shift):
-    center = values - jnp.mean(values, axis=-1, keepdims=True)
-    inverse = lax.rsqrt(jnp.mean(center * center, axis=-1, keepdims=True) + 1e-06)
-    normed = center * inverse
-    return normed * gain + shift, normed, inverse
-
-
-def norm_back(grad_norm, normed, inverse, gain):
-    scaled = grad_norm * gain
-    return inverse * (
-        scaled
-        - jnp.mean(scaled, axis=-1, keepdims=True)
-        - normed * jnp.mean(scaled * normed, axis=-1, keepdims=True)
-    )
+    )(n2, gm, weights, b1)
 
 
 def body(
@@ -833,8 +1094,7 @@
     rows = part_rows * line
     group = lax.axis_index("dp")
     place = lax.axis_index("tensor")
-    flip = group % 2
-    mine = jnp.where(flip == 1, line - 1 - place, place)
+    mine = place + (group % 2) * (line - 1 - 2 * place)
     active = mine < images
 
     tile = min(512, w_fc1.shape[1])
@@ -843,178 +1103,116 @@
     fc_both = jnp.concatenate([w_fc1.reshape(tiles), w_fc2.T.reshape(tiles)], axis=2).reshape(
         w_fc1.shape[0], -1
     )
-    small = jnp.concatenate(
-        [
-            ln_gain.reshape(-1),
-            ln_shift.reshape(-1),
-            layer_scale.reshape(-1),
-            out_bias.reshape(-1),
-            b_qv.astype(f32).reshape(-1),
-            b_fc1.astype(f32).reshape(-1),
-        ]
+
+    def lanes(x):
+        return jnp.pad(x, ((0, 0), (0, LANES - x.shape[1])))
+
+    own_width = ln_gain.shape[1]
+    _, bq_rows, bq_cols = b_qv.shape
+    f_rows, f_cols = b_fc1.shape
+    small = [ln_gain, ln_shift, layer_scale, out_bias, b_qv.astype(f32).reshape(-1, bq_cols)]
+    small = jnp.concatenate([lanes(x) for x in small + [b_fc1.astype(f32)]], axis=0)
+    small_rows = round_up(small.shape[0], 8)
+    small = jnp.pad(small, ((0, small_rows - small.shape[0]), (0, 0)))
+    b_at = 8 + 2 * bq_rows
+
+    x_all, weights, small = arrive(groups, line, block_input, qkv_out, small)
+    small = small.reshape(line, groups, small_rows, LANES)
+    vectors = jnp.transpose(small[:, :, :8, :own_width], (2, 1, 0, 3)).reshape(8, width)
+    qv_bias = jnp.transpose(
+        small[:, :, 8:b_at, :bq_cols].reshape(line, groups, 2, bq_rows, bq_cols), (2, 0, 4, 1, 3)
+    ).reshape(2, 1, width)
+    fc1_bias = jnp.transpose(
+        small[:, :, b_at : b_at + f_rows, :f_cols], (0, 3, 1, 2)
+    ).reshape(1, -1)
+
+    length = jnp.where(active, lengths[jnp.minimum(mine, images - 1)], 0).astype(jnp.int32)
+    flags = jnp.stack([length, active.astype(jnp.int32)])
+    pieces = (line, part_rows, width)
+
+    zero = jnp.zeros((1, 1, width), f32)
+    qkv, x_all, normed1_t = project(
+        flags,
+        x_all.reshape(rows, width),
+        vectors,
+        weights,
+        jnp.concatenate([qv_bias[:1], zero, qv_bias[1:]]),
     )
-    small = jnp.pad(small, (0, round_up(small.size, 8 * LANES) - small.size)).reshape(-1, LANES)
-    x_all, weights, small = arrive(groups, line, block_input, qkv_out, small)
-    x_all = jnp.where(active, x_all.reshape(rows, width), 0)
-    small = jnp.transpose(small.reshape(line, groups, -1), (1, 0, 2))
-    own_width = ln_gain.shape[1]
-    at = 0
-
-    def take(count):
-        nonlocal at
-        at += count
-        return small[:, :, at - count : at]
-
-    def vectors(x):
-        return jnp.transpose(x.reshape(groups, line, 2, own_width), (2, 0, 1, 3)).reshape(2, width)
-
-    gains = vectors(take(2 * own_width))
-    shifts = vectors(take(2 * own_width))
-    scales = vectors(take(2 * own_width))
-    biases = vectors(take(2 * own_width))
-    _, bq_rows, bq_cols = b_qv.shape
-    qv_bias = jnp.transpose(
-        take(2 * bq_rows * bq_cols).reshape(groups, line, 2, bq_rows, bq_cols), (2, 1, 4, 0, 3)
-    ).reshape(2, width)
-    f_rows, f_cols = b_fc1.shape
-    fc1_bias = jnp.transpose(
-        take(f_rows * f_cols).reshape(groups, line, f_rows, f_cols), (1, 3, 0, 2)
-    ).reshape(1, -1)
-
-    length = jnp.where(active, lengths[jnp.minimum(mine, images - 1)], 0).astype(jnp.int32)
-    length_array = length.reshape(1)
-    valid = (jnp.arange(rows, dtype=jnp.int32) < length).astype(f32)[:, None]
-
-    source = x_all.astype(f32)
-    normed_one, hat_first, inv_first = norm_rows(source, gains[0], shifts[0])
-    normed1 = normed_one.astype(bf16)
-
-    def dot(a, b, dims=NN):
-        return lax.dot_general(a, b, dims, preferred_element_type=f32)
-
-    cols = width // line
-    zero = jnp.zeros_like(qv_bias[:1])
-    qkv = project(normed1, weights, jnp.stack([qv_bias[:1], zero, qv_bias[1:]]))
+    x_all = x_all.reshape(pieces)
     context, query_stats, fc_weights, cot = attend_forward(
-        groups, line, length_array, qkv, fc_both, cotangent
+        groups, line, flags, qkv, fc_both, cotangent
     )
-    cot = jnp.where(active, cot.reshape(rows, width), 0)
-    wout_t = weights[:, :, 3 * cols :]
-    attn = (
-        jnp.einsum(
-            "stc,tdc->sd", context.reshape(rows, line, cols), wout_t, preferred_element_type=f32
-        )
-        + biases[0]
+    context3 = context.reshape(pieces)
+    hidden, normed2, grad_mlp = middle(flags, context3, x_all, cot, vectors, weights)
+    mlp, grad_normed2, grad_fc, grad_bfc1 = feed_forward(
+        normed2.reshape(rows, width), grad_mlp.reshape(rows, width), fc_weights, fc1_bias, tile
     )
-    hidden = source + scales[0] * attn
-    normed_two, hat_second, inv_second = norm_rows(hidden, gains[1], shifts[1])
-    normed2 = normed_two.astype(bf16)
-    grad_out = valid * cot.astype(f32)
-    grad_mlp = grad_out * scales[1]
-    grad_mlp_b = grad_mlp.astype(bf16)
-    mlp, grad_normed2, grad_fc, grad_bfc1 = feed_forward(
-        normed2, normed2.T, grad_mlp_b, grad_mlp_b.T, fc_weights, fc1_bias, tile
+    block_out, grad_hidden, grad_context, grad_wout, sums = turn(
+        flags,
+        mlp.reshape(pieces),
+        grad_normed2.reshape(pieces),
+        hidden,
+        x_all,
+        cot,
+        context3,
+        vectors,
+        weights,
     )
-    mlp = mlp + biases[1]
-    block_out = (valid * (hidden + scales[1] * mlp)).astype(bf16).reshape(line, part_rows, width)
-    grad_scale2 = jnp.sum(grad_out * mlp, axis=0)
-    grad_bias2 = jnp.sum(grad_mlp, axis=0)
-    grad_gain2 = jnp.sum(grad_normed2 * hat_second, axis=0)
-    grad_shift2 = jnp.sum(grad_normed2, axis=0)
-    grad_hidden = grad_out + norm_back(grad_normed2, hat_second, inv_second, gains[1])
-    grad_scale1 = jnp.sum(grad_hidden * attn, axis=0)
-    grad_attn = grad_hidden * scales[0]
-    grad_bias1 = jnp.sum(grad_attn, axis=0)
-    grad_attn_b = grad_attn.astype(bf16)
-    grad_context = (
-        jnp.einsum("sd,tdc->stc", grad_attn_b, wout_t, preferred_element_type=f32)
-        .astype(bf16)
-        .reshape(rows, width)
-    )
-    grad_query, grad_key, grad_value, block_out, shard_fc = attend_backward(
+    grad_query, grad_key, grad_value, grad_bqv, block_out, shard_fc, shard_wout = attend_backward(
         groups,
         line,
         images,
-        length_array,
+        flags,
         query_stats,
         qkv,
-        grad_context,
+        grad_context.reshape(rows, width),
         context,
         block_out,
         grad_fc,
+        grad_wout,
     )
-    grad_bq = jnp.sum(grad_query.astype(f32), axis=0)
-    grad_bv = jnp.sum(grad_value.astype(f32), axis=0)
-    split = (rows, line, cols)
-    grad_parts = [
-        jnp.einsum("sd,stc->tdc", a, b.reshape(split), preferred_element_type=f32).astype(bf16)
-        for a, b in (
-            (normed1, grad_query),
-            (normed1, grad_key),
-            (normed1, grad_value),
-            (grad_attn_b, context),
-        )
-    ]
-    grad_weights = jnp.concatenate(grad_parts, axis=2)
-    grad_normed1 = sum(
-        jnp.einsum(
-            "stc,tdc->sd",
-            g.reshape(split),
-            weights[:, :, n * cols : (n + 1) * cols],
-            preferred_element_type=f32,
-        )
-        for n, g in enumerate((grad_query, grad_key, grad_value))
-    )
-    grad_gain1 = jnp.sum(grad_normed1 * hat_first, axis=0)
-    grad_shift1 = jnp.sum(grad_normed1, axis=0)
-    grad_source = grad_hidden + norm_back(grad_normed1, hat_first, inv_first, gains[0])
-    grad_source = grad_source.astype(bf16).reshape(line, part_rows, width)
-
-    by_device = [
-        jnp.transpose(
-            jnp.stack(pair).reshape(2, groups, line, own_width), (2, 1, 0, 3)
-        ).reshape(line, groups, -1)
-        for pair in (
-            (grad_gain1, grad_gain2),
-            (grad_shift1, grad_shift2),
-            (grad_scale1, grad_scale2),
-            (grad_bias1, grad_bias2),
-        )
-    ]
-    by_device.append(
-        jnp.transpose(
-            jnp.stack([grad_bq, grad_bv]).reshape(2, line, bq_cols, groups, bq_rows), (1, 3, 0, 4, 2)
-        ).reshape(line, groups, -1)
-    )
-    by_device.append(
-        jnp.transpose(grad_bfc1.reshape(line, f_cols, groups, f_rows), (0, 2, 3, 1)).reshape(
-            line, groups, -1
-        )
-    )
-    by_device = jnp.concatenate(by_device, axis=2)
-    short = small.shape[2] - by_device.shape[2]
-    by_device = jnp.pad(by_device, ((0, 0), (0, 0), (0, short))).reshape(line, -1, LANES)
+
+    wide = width // groups
+    none = jnp.zeros((1, width), f32)
+    by_vector = jnp.concatenate(
+        [none, sums[0:1], none, sums[1:2], sums[2:6]], axis=0
+    ).reshape(8, groups, wide)
+    by_vector = jnp.pad(jnp.transpose(by_vector, (1, 0, 2)), ((0, 0), (0, 0), (0, LANES - wide)))
+    by_vector = jnp.broadcast_to(by_vector[None], (line, groups, 8, LANES))
+    by_head = jnp.transpose(grad_bqv[:, :2], (1, 0, 2)).reshape(2, line, bq_cols, groups, bq_rows)
+    by_head = jnp.transpose(by_head, (1, 3, 0, 4, 2)).reshape(line, groups, 2 * bq_rows, bq_cols)
+    by_unit = jnp.transpose(grad_bfc1.reshape(line, f_cols, groups, f_rows), (0, 2, 3, 1))
+
+    def wider(x):
+        return jnp.pad(x, ((0, 0), (0, 0), (0, 0), (0, LANES - x.shape[3])))
+
+    smalls = jnp.concatenate([by_vector, wider(by_head), wider(by_unit)], axis=2)
+    smalls = jnp.pad(smalls, ((0, 0), (0, 0), (0, small_rows - smalls.shape[2]), (0, 0)))
     grad_input, shard_weights, shard_small = leave(
-        groups, line, images, grad_source, grad_weights, by_device
+        groups,
+        line,
+        images,
+        grad_query,
+        grad_key,
+        grad_value,
+        weights,
+        normed1_t,
+        x_all,
+        grad_hidden,
+        vectors,
+        smalls.reshape(line, groups * small_rows, LANES),
     )
     grad_input = grad_input.astype(f32)
-    own = cols
-    shard_wqkv = jnp.stack([shard_weights[:, n * own : (n + 1) * own] for n in range(3)])
-    shard_wout = shard_weights[:, 3 * own :].T
+    cols = width // line
+    shard_wqkv = jnp.stack([shard_weights[:, n * cols : (n + 1) * cols] for n in range(3)])
+    shard_wout = shard_wout.T
     shard_fc = shard_fc.reshape(shard_fc.shape[0], -1, 2, tile)
     shard_fc1 = shard_fc[:, :, 0].reshape(w_fc1.shape)
     shard_fc2 = shard_fc[:, :, 1].reshape(w_fc1.shape).T
-    shard_small = shard_small.reshape(-1)
-    at = 0
-
-    def give(shape):
-        nonlocal at
-        at += math.prod(shape)
-        return shard_small[at - math.prod(shape) : at].reshape(shape)
-
-    shard_gain, shard_shift, shard_scale, shard_bias = (give(ln_gain.shape) for _ in range(4))
-    shard_bqv = give(b_qv.shape)
-    shard_bfc1 = give(b_fc1.shape)
+    own = lax.dynamic_slice_in_dim(shard_small[:8], place * own_width, own_width, 1)
+    shard_gain, shard_shift, shard_scale, shard_bias = (own[2 * n : 2 * n + 2] for n in range(4))
+    shard_bqv = shard_small[8:b_at, :bq_cols].reshape(b_qv.shape)
+    shard_bfc1 = shard_small[b_at : b_at + f_rows, :f_cols]
     return (
         block_out,
         grad_input,

time: 757 us -> 632 us (0.83)
  Pallas kernels: 501 us -> 576 us
  other arithmetic: 84.9 us -> 10.3 us
  local copies, waits for them, and re-layouts: 101 us -> 40.7 us
  matrix products: 58 us -> 0 us
    pallas_call x2 -> x4, Pallas kernels: 86.8 us -> 147 us  [the longest x1 90 us: leave(): pl.pallas_call(functools.partial(leave_kernel, groups, line), grid=(2 * l...]
    dot_general x9 -> x0, matrix products: 58 us -> none  [the longest x4 22.3 us: body(): jnp.einsum('sd,stc->tdc', a, b.reshape(split), preferred_element_type=f32)]
    convert_element_type x7 -> x0, local copies, waits for them, and re-layouts: 38.4 us -> none  [the longest x1 14.3 us: body(): grad_mlp_b = grad_mlp.astype(bf16)]
    reduce_sum x9 -> x0, other arithmetic: 37.5 us -> none  [the longest x1 15.7 us: body(): grad_scale2 = jnp.sum(grad_out * mlp, axis=0)]
    convert_element_type x9 -> x0, other arithmetic: 27.3 us -> none  [the longest x2 11.3 us: body(): normed1 = normed_one.astype(bf16)]
    pallas_call x1, Pallas kernels: 149 us -> 162 us  [attend_backward(): pl.pallas_call(functools.partial(attend_backward_kernel, groups, line, ro...]
    pallas_call x3 -> x1, local copies, waits for them, and re-layouts: 13.1 us -> 0.51 us  [feed_forward(): pl.pallas_call(functools.partial(feed_forward_kernel, tile), grid=(units...]
    reshape x23 -> x7, local copies, waits for them, and re-layouts: 15.2 us -> 3.26 us  [the longest x2 1.47 us: body(): small[:, :, 8:b_at, :bq_cols].reshape(line, groups, 2, bq_rows, bq_cols)]
where the time goes in v3:
time: 632 us; the launch traced here: 629 us
  Pallas kernels  576 us (91%)
  local copies, waits for them, and re-layouts  40.7 us (6%)
  other arithmetic  10.3 us (2%)
    pallas_call x1, Pallas kernels, attend_backward(): pl.pallas_call(functools.partial(attend_backward_kernel, groups, line, ro...  162 us
    pallas_call x1, Pallas kernels, attend_forward(): pl.pallas_call(functools.partial(attend_forward_kernel, groups, line, row...  103 us
    pallas_call x1, Pallas kernels, feed_forward(): pl.pallas_call(functools.partial(feed_forward_kernel, tile), grid=(units...  93.8 us
    pallas_call x1, Pallas kernels, leave(): pl.pallas_call(functools.partial(leave_kernel, groups, line), grid=(2 * l...  90 us
    pallas_call x1, Pallas kernels, arrive(): pl.pallas_call(functools.partial(arrive_kernel, groups, line), in_specs=[...  69.4 us
    pallas_call x1, Pallas kernels, project(): pl.pallas_call(project_kernel, grid=(line, 3), in_specs=[SMEM, whole(rows...  24.8 us
    pallas_call x1, Pallas kernels, turn(): pl.pallas_call(turn_kernel, grid=(line,), in_specs=[SMEM] + [piece] * 6 +...  22.9 us
    unnamed x45, local copies, waits for them, and re-layouts  15.6 us

profile of v3, /device:TPU:0, one launch (start us, length us, event | category | flops | bytes accessed | tf_op | source)
XLA Modules:
  0.0 628.9 jit_solution(10621697980142599233)
XLA Ops:
  0.7 1.2 dynamic_slice.6
  9.4 1.8 concatenate.20.small_ref
  11.2 69.4 %arrive.1 = (bf16[4,344,1024]{2,1,0:T(8,128)(2,1)}, bf16[4,1024,1024]{2,1,0:T(8,128)(2,1)}, f32[4,256,128]{2,1,0:T(8,128)}) custom-call(bf16[3,344,1024]{2,1,0:T(8,128)(2,1)} %x_ref.1, bf16[128,1024]{1,0:T(8,128)(2,1)} %pad_maximum_fusion.2.shard_ref, f32[32,128]{1,0:T(8,128)} %concatenate.20.small_ref), custom_call_target="tpu_custom_call" | custom-call | tf_op jit(solution)/shard_map/arrive/pallas_call | solution.py:415
  84.0 1.8 copy-done.7
  85.8 24.8 %project.1 = (bf16[3,1376,1024]{2,1,0:T(8,128)(2,1)}, bf16[1376,1024]{1,0:T(8,128)(2,1)S(1)}, bf16[1024,1376]{1,0:T(8,128)(2,1)S(1)}) custom-call(s32[2]{0:T(128)S(1)} %pad_add_fusion.flag_ref.len_ref, bf16[1376,1024]{1,0:T(8,128)(2,1)S(1)} %bitcast.66, f32[8,1024]{1,0:T(8,128)S(1)} %reshape.101.v_ref, bf16[4,1024,1024]{2,1,0:T(8,128)(2,1)} %get-tuple-element.46.w_ref, ...), custom_call_target="tpu_custom_call" | custom-call | flops 8657043456 | bytes 22544384 | tf_op jit(solution)/shard_map/project/pallas_call | solution.py:596
  110.7 1.6 copy-done.3
  112.3 1.4 copy.73
  114.6 2.3 pad_maximum_fusion
  116.9 1.2 reshape.105.shard_ref
  118.1 103.2 %attend_forward.1 = (bf16[1376,1024]{1,0:T(8,128)(2,1)}, bf16[16,1376,128]{2,1,0:T(8,128)(2,1)}, bf16[4,1024,2048]{2,1,0:T(8,128)(2,1)}, bf16[4,344,1024]{2,1,0:T(8,128)(2,1)}) custom-call(s32[2]{0:T(128)} %copy-done.5, bf16[3,1376,1024]{2,1,0:T(8,128)(2,1)} %get-tuple-element.47.q_ref.k_ref.v_ref, ...), custom_call_target="tpu_custom_call" | custom-call | flops 31021072384 | bytes 16908288 | tf_op jit(solution)/shard_map/attend_forward/pallas_call | solution.py:816
  221.3 1.8 copy-done.1
  223.1 1.8 copy-done.2
  224.9 9.5 %middle.1 = (f32[4,344,1024]{2,1,0:T(8,128)}, bf16[4,344,1024]{2,1,0:T(8,128)(2,1)S(1)}, bf16[4,344,1024]{2,1,0:T(8,128)(2,1)S(1)}) custom-call(s32[2]{0:T(128)S(1)} %copy-done.6, bf16[4,344,1024]{2,1,0:T(8,128)(2,1)S(1)} %bitcast.65, bf16[4,344,1024]{2,1,0:T(8,128)(2,1)S(1)} %bitcast.61, bf16[4,344,1024]{2,1,0:T(8,128)(2,1)S(1)} %copy-done.2, ...), custom_call_target="tpu_custom_call" | custom-call | tf_op jit(solution)/shard_map/middle/pallas_call | solution.py:648
  234.5 1.7 copy-done.8
  236.2 1.6 copy-done.9
  239.5 93.8 %feed_forward.1 = (f32[1376,1024]{1,0:T(8,128)}, f32[1376,1024]{1,0:T(8,128)}, bf16[4,1024,2048]{2,1,0:T(8,128)(2,1)}, f32[1,4096]{1,0:T(1,128)}) custom-call(bf16[1376,1024]{1,0:T(8,128)(2,1)} %bitcast.67, bf16[1376,1024]{1,0:T(8,128)(2,1)} %bitcast.68, bf16[4,1024,2048]{2,1,0:T(8,128)(2,1)} %get-tuple-element.54.w_ref, f32[1,4096]{1,0:T(1,128)} %reshape.110.b1_ref), custom_call_target="tpu_custom_call" | custom-call | flops 92341796864 | bytes 33554432 | tf_op jit(solution)/shard_map/feed_forward/pallas_call | solution.py:1044
  333.4 22.9 %turn.1 = (bf16[4,344,1024]{2,1,0:T(8,128)(2,1)}, f32[4,344,1024]{2,1,0:T(8,128)}, bf16[4,344,1024]{2,1,0:T(8,128)(2,1)}, bf16[4,1024,256]{2,1,0:T(8,128)(2,1)}, f32[8,1024]{1,0:T(8,128)}) custom-call(s32[2]{0:T(128)} %copy-done.5, f32[4,344,1024]{2,1,0:T(8,128)} %bitcast.69, f32[4,344,1024]{2,1,0:T(8,128)} %bitcast.70, ...), custom_call_target="tpu_custom_call" | custom-call | tf_op jit(solution)/shard_map/turn/pallas_call | solution.py:722
  356.3 162.3 %attend_backward.1 = (bf16[1376,1024]{1,0:T(8,128)(2,1)}, bf16[1376,1024]{1,0:T(8,128)(2,1)}, bf16[1376,1024]{1,0:T(8,128)(2,1)}, f32[8,8,128]{2,1,0:T(8,128)}, ...) custom-call(s32[2]{0:T(128)} %copy-done.5, ...), custom_call_target="tpu_custom_call" | custom-call | flops 77552680960 | bytes 22544384 | tf_op jit(solution)/shard_map/attend_backward/pallas_call | solution.py:952
  522.4 90.0 %leave.1 = (bf16[3,344,1024]{2,1,0:T(8,128)(2,1)}, f32[128,768]{1,0:T(8,128)}, f32[32,128]{1,0:T(8,128)}) custom-call(bf16[1376,1024]{1,0:T(8,128)(2,1)} %get-tuple-element.63.gq_ref, bf16[1376,1024]{1,0:T(8,128)(2,1)} %get-tuple-element.64.gk_ref, bf16[1376,1024]{1,0:T(8,128)(2,1)} %get-tuple-element.65.gv_ref, ...), custom_call_target="tpu_custom_call" | custom-call | tf_op jit(solution)/shard_map/leave/pallas_call | solution.py:512
  612.4 4.1 convert_element_type.19
  618.8 2.3 reshape.120
  621.1 2.1 fusion.1
  624.7 1.9 copy.80
  627.3 1.3 copy.99
  (79 shorter events, 21.1 us)
Async XLA Ops:
  2.6 108.0 %copy-start.5 = (s32[2]{0:T(128)}, s32[2]{0:T(128)S(1)}, u32[]{:S(2)}) copy-start(s32[2]{0:T(128)S(1)} %pad_add_fusion.flag_ref.len_ref) | copy-start | bytes 28
  81.8 139.5 %copy-start.4 = (f32[8,1024]{1,0:T(8,128)}, f32[8,1024]{1,0:T(8,128)S(1)}, u32[]{:S(2)}) copy-start(f32[8,1024]{1,0:T(8,128)S(1)} %reshape.101.v_ref) | copy-start | bytes 98308
  84.0 1.8 copy-start.7
  85.8 26.4 %copy-start.12 = (bf16[1024,128]{1,0:T(8,128)(2,1)S(1)}, bf16[1024,128]{1,0:T(8,128)(2,1)}, u32[]{:S(2)}) copy-start(bf16[1024,128]{1,0:T(8,128)(2,1)} %param.21) | copy-start | bytes 786436
  85.8 27.9 %copy-start.13 = (bf16[128,1024]{1,0:T(8,128)(2,1)S(1)}, bf16[128,1024]{1,0:T(8,128)(2,1)}, u32[]{:S(2)}) copy-start(bf16[128,1024]{1,0:T(8,128)(2,1)} %param.19) | copy-start | bytes 786436
  110.7 1.6 copy-start.3
  112.2 109.1 %copy-start = (bf16[1376,1024]{1,0:T(8,128)(2,1)}, bf16[1376,1024]{1,0:T(8,128)(2,1)S(1)}, u32[]{:S(2)}) copy-start(bf16[1376,1024]{1,0:T(8,128)(2,1)S(1)} %get-tuple-element.50) | copy-start | bytes 8454148
  118.1 103.3 %copy-start.6 = (s32[2]{0:T(128)S(1)}, s32[2]{0:T(128)}, u32[]{:S(2)}) copy-start(s32[2]{0:T(128)} %copy-done.5) | copy-start | bytes 28
  221.3 1.8 copy-start.1
  223.1 1.8 copy-start.2
  234.5 1.7 copy-start.8
  236.1 1.6 copy-start.9
  356.2 162.9 %copy-start.17 = (f32[1,4096]{1,0:T(1,128)S(1)}, f32[1,4096]{1,0:T(1,128)}, u32[]{:S(2)}) copy-start(f32[1,4096]{1,0:T(1,128)} %get-tuple-element.70) | copy-start | bytes 49156
  356.3 165.2 %copy-start.15 = (f32[8,1024]{1,0:T(8,128)S(1)}, f32[8,1024]{1,0:T(8,128)}, u32[]{:S(2)}) copy-start(f32[8,1024]{1,0:T(8,128)} %get-tuple-element.68) | copy-start | bytes 98308
  612.4 4.2 copy-start.11
  612.4 5.0 copy-start.16
  612.4 5.6 copy-start.14
  618.8 8.5 %copy-start.10 = (bf16[3,344,1024]{2,1,0:T(8,128)(2,1)S(1)}, bf16[3,344,1024]{2,1,0:T(8,128)(2,1)}, u32[]{:S(2)}) copy-start(bf16[3,344,1024]{2,1,0:T(8,128)(2,1)} %get-tuple-element.150) | copy-start | bytes 6340612

commit v4 on v3

--- a/solution.py
+++ b/solution.py
@@ -62,6 +62,17 @@
         odd = self.g % 2
         return z + odd * (self.line - 1 - 2 * z)
 
+    def near(self, k):
+        place = 0
+        if not isinstance(k, int):
+            for i in range(self.line):
+                place = jnp.where(k == i, self.near(i), place)
+            return place
+        for z in range(self.line):
+            order = sorted(range(self.line), key=lambda t: (abs(t - z), t))
+            place = jnp.where(self.z == z, order[k], place)
+        return place
+
     def up(self, k):
         return lax.rem(self.z + k, self.line)
 
@@ -87,59 +98,55 @@
     @staticmethod
     def sems(groups, line):
         chips = groups // 2
-        return [
-            DMA((line,)),
-            DMA((line,)),
-            DMA((chips, line)),
-            DMA((chips, line)),
-            DMA((chips, line)),
-            DMA((chips, line)),
-        ]
+        return [DMA((line,))] * 2 + [DMA((chips, line))] * 4
 
     def __init__(self, at, shard, full, sems):
         self.at, self.shard, self.full = at, shard, full
         self.zs, self.zr, self.ds, self.dr, self.cs, self.cr = sems
         self.rows = shard.shape[0]
 
-    def piece(self, mask, k):
-        at = self.at
-        rows = pl.ds(pl.multiple_of(flipped(at.g, mask) * self.rows, 8), self.rows)
-        return self.full.at[at.down(k), rows, :]
-
-    def own(self, k):
-        return self.shard if k == 0 else self.piece(0, k)
+    def piece(self, mask, t):
+        rows = pl.ds(pl.multiple_of(flipped(self.at.g, mask) * self.rows, 8), self.rows)
+        return self.full.at[t, rows, :]
+
+    def source(self, mask, k):
+        own = mask == 0 and k == 0
+        return self.shard if own else self.piece(mask, self.at.near(k))
 
     def local(self):
-        return pltpu.make_async_copy(self.shard, self.piece(0, 0), self.zs.at[0])
-
-    def along(self, k, arriving=False):
-        dst = self.piece(0, k if arriving else 0)
-        src = dst if arriving else self.shard
-        return remote(src, dst, self.zs.at[k], self.zr.at[k], (self.at.g, self.at.up(k)))
-
-    def across(self, mask, k, arriving=False):
-        at = self.at
+        return pltpu.make_async_copy(self.shard, self.piece(0, self.at.z), self.zr.at[self.at.z])
+
+    def along(self, k):
+        at = self.at
+        t = at.near(k)
+        return remote(
+            self.shard, self.piece(0, at.z), self.zs.at[t], self.zr.at[at.z], (at.g, t)
+        )
+
+    def across(self, mask, k):
+        at = self.at
+        via, peer = 0, mask
         if at.square and mask == 6:
-            via, peer = (2, 4) if k < at.line // 2 else (4, 2)
-            src = dst = self.piece(via, k)
-        else:
-            peer = mask
-            src, dst = self.own(k), self.piece(0, k)
-        if arriving:
-            src = dst = self.piece(mask, k)
+            via, peer = (2, 4) if k % 2 == 0 else (4, 2)
+        t = at.near(k)
+        m = mask // 2
         return remote(
-            src, dst, self.ds.at[mask // 2, k], self.dr.at[mask // 2, k], (flipped(at.g, peer), at.z)
+            self.source(via, k), self.piece(via, t), self.ds.at[m, t], self.dr.at[m, t],
+            (flipped(at.g, peer), at.z),
         )
 
-    def core(self, mask, k, arriving=False):
-        at = self.at
-        if arriving:
-            dst = self.piece(mask ^ 1, k)
-            src = dst
-        else:
-            dst = self.piece(mask, k)
-            src = self.own(k) if mask == 0 else dst
-        return remote(src, dst, self.cs.at[mask // 2, k], self.cr.at[mask // 2, k], (flipped(at.g, 1), at.z))
+    def core(self, mask, k):
+        at = self.at
+        t = at.near(k)
+        m = mask // 2
+        return remote(
+            self.source(mask, k), self.piece(mask, t), self.cs.at[m, t], self.cr.at[m, t],
+            (flipped(at.g, 1), at.z),
+        )
+
+    def arrived(self, mask, t, sem):
+        piece = self.piece(mask, t)
+        remote(piece, piece, sem, sem, (flipped(self.at.g, 1), self.at.z)).wait_recv()
 
     def start(self):
         self.local().start()
@@ -148,48 +155,51 @@
         self.spread(0)
 
     def spread(self, k):
+        at = self.at
         if k:
-            self.along(k, True).wait_recv()
-        for mask in self.at.direct:
+            t = at.near(k)
+            self.arrived(0, t, self.zr.at[t])
+        for mask in at.direct:
             self.across(mask, k).start()
         self.core(0, k).start()
 
     def passing(self, k):
         at = self.at
+        t = at.near(k)
         for mask in at.direct:
-            self.across(mask, k, True).wait_recv()
-            if at.square and mask == (2 if k < at.line // 2 else 4):
+            self.arrived(mask, t, self.dr.at[mask // 2, t])
+            if at.square and mask == (2 if k % 2 == 0 else 4):
                 self.across(6, k).start()
             self.core(mask, k).start()
 
     def last(self, k):
-        if self.at.square:
-            self.across(6, k, True).wait_recv()
+        at = self.at
+        if at.square:
+            t = at.near(k)
+            self.arrived(6, t, self.dr.at[3, t])
             self.core(6, k).start()
 
     def finish(self):
         at = self.at
         for k in range(at.line):
+            t = at.near(k)
+            if k:
+                self.along(k).wait_send()
             for mask in at.masks:
-                self.core(mask, k, True).wait_recv()
+                self.arrived(mask ^ 1, t, self.cr.at[mask // 2, t])
                 self.core(mask, k).wait_send()
                 if mask:
                     self.across(mask, k).wait_send()
-            if k:
-                self.along(k).wait_send()
         self.local().wait()
 
     def steps(self):
         line = self.at.line
-        out = [self.start]
-        for k in range(1, line):
-            out.append(functools.partial(self.spread, k))
-        for k in range(line):
-            out.append(functools.partial(self.passing, k))
-        for k in range(line):
-            out.append(functools.partial(self.last, k))
-        out.append(self.finish)
-        return out
+        out = []
+        for i in range(line + 2):
+            for work, k in ((self.spread, i), (self.passing, i - 1), (self.last, i - 2)):
+                if 0 <= k < line:
+                    out.append(functools.partial(work, k) if i else self.start)
+        return out + [self.finish]
 
 
 class ToOwner:
@@ -210,21 +220,26 @@
 
     def copy(self, k, arriving=False):
         at = self.at
-        to = at.up(k)
+        to = at.near(k)
         src = self.rows.at[jnp.minimum(at.image(to), self.count - 1)]
-        dst = self.image.at[at.down(k) if arriving else at.z]
-        return remote(src, dst, self.send.at[k], self.recv.at[k], (at.g, to))
+        slot = to if arriving else at.z
+        return remote(src, self.image.at[slot], self.send.at[k], self.recv.at[slot], (at.g, to))
+
+    def start_one(self, k):
+        at = self.at
+        if k == 0:
+            self.local().start()
+        else:
+            pl.when(at.image(at.near(k)) < self.count)(self.copy(k).start)
 
     def start(self):
-        at = self.at
-        self.local().start()
+        for k in range(self.at.line):
+            self.start_one(k)
+
+    def finish(self):
+        at = self.at
         for k in range(1, at.line):
-            pl.when(at.image(at.up(k)) < self.count)(self.copy(k).start)
-
-    def finish(self):
-        at = self.at
-        for k in range(1, at.line):
-            pl.when(at.image(at.up(k)) < self.count)(self.copy(k).wait_send)
+            pl.when(at.image(at.near(k)) < self.count)(self.copy(k).wait_send)
             pl.when(at.image(at.z) < self.count)(self.copy(k, True).wait_recv)
         self.local().wait()
 
@@ -249,14 +264,16 @@
         dst = self.rows.at[jnp.minimum(at.image(owner), self.count - 1)]
         return remote(self.image.at[at.up(k)], dst, self.send.at[k], self.recv.at[k], (at.g, at.up(k)))
 
+    def start_piece(self, p):
+        at = self.at
+        own = at.image(at.z) < self.count
+        k = lax.rem(p - at.z + at.line, at.line)
+        pl.when(own & (k == 0))(lambda: self.local().start())
+        pl.when(own & (k > 0))(lambda: self.copy(k).start())
+
     def start(self):
-        at = self.at
-
-        @pl.when(at.image(at.z) < self.count)
-        def _():
-            self.local().start()
-            for k in range(1, at.line):
-                self.copy(k).start()
+        for p in range(self.at.line):
+            self.start_piece(p)
 
     def finish(self):
         at = self.at
@@ -280,119 +297,156 @@
             pltpu.VMEM((chips, line, r, c), dtype),
             pltpu.VMEM((chips - 1, line, r, c), dtype),
             pltpu.VMEM((line, r, c), dtype),
-            DMA((chips, line)),
-            DMA((chips, line)),
-            DMA((chips, line)),
-            DMA((chips, line)),
-            DMA((chips, line)),
-            DMA((line,)),
-            DMA((line,)),
-        ]
+        ] + [DMA((chips, line))] * 5 + [DMA((line,))] * 2
 
     def __init__(self, at, full, scratch, rows):
-        self.at, self.full, self.rows = at, full, rows
+        self.at, self.full, self.rows, self.apart = at, full, rows, False
         self.cbuf, self.sums, self.dbuf, self.zbuf = scratch[:4]
         self.ls, self.cs, self.cr, self.ds, self.dr, self.zs, self.zr = scratch[4:]
         self.order = [6, 2, 4, 0] if at.square else at.masks[1:] + [0]
 
-    def piece(self, mask, k):
-        at = self.at
-        rows = pl.ds(pl.multiple_of(flipped(at.g, mask) * self.rows, 8), self.rows)
-        return self.full.at[at.down(k), rows, :]
-
-    def local(self, mask, k):
-        return pltpu.make_async_copy(
-            self.piece(mask, k), self.sums.at[mask // 2, k], self.ls.at[mask // 2, k]
-        )
-
-    def core(self, mask, k):
+    def far(self, k):
+        return self.at.near(self.at.line - 1 - k)
+
+    def piece(self, mask, t):
+        rows = pl.ds(pl.multiple_of(flipped(self.at.g, mask) * self.rows, 8), self.rows)
+        return self.full.at[t, rows, :]
+
+    def local(self, mask, t):
+        m = mask // 2
+        return pltpu.make_async_copy(self.piece(mask, t), self.sums.at[m, t], self.ls.at[m, t])
+
+    def core(self, mask, t):
         at, m = self.at, mask // 2
         return remote(
-            self.piece(mask ^ 1, k), self.cbuf.at[m, k], self.cs.at[m, k], self.cr.at[m, k],
+            self.piece(mask ^ 1, t), self.cbuf.at[m, t], self.cs.at[m, t], self.cr.at[m, t],
             (flipped(at.g, 1), at.z),
         )
 
     def across(self, mask, k):
         at, m = self.at, mask // 2
-        peer = mask
+        peer, t = mask, self.far(k)
         if at.square and mask == 6:
-            peer = 4 if k < at.line // 2 else 2
+            peer = 4 if k % 2 == 0 else 2
         return remote(
-            self.sums.at[m, k], self.dbuf.at[m - 1, k], self.ds.at[m, k], self.dr.at[m, k],
+            self.sums.at[m, t], self.dbuf.at[m - 1, t], self.ds.at[m, t], self.dr.at[m, t],
             (flipped(at.g, peer), at.z),
         )
 
-    def along(self, k):
+    def along(self, t):
         at = self.at
         return remote(
-            self.sums.at[0, k], self.zbuf.at[k], self.zs.at[k], self.zr.at[k], (at.g, at.down(k))
+            self.sums.at[0, t], self.zbuf.at[at.z], self.zs.at[t], self.zr.at[at.z], (at.g, t)
         )
 
-    def start(self):
+    def add(self, m, t, other):
+        total = self.sums[m, t].astype(f32) + other.astype(f32)
+        self.sums[m, t] = total.astype(self.sums.dtype)
+
+    def begin(self, k):
+        t = self.far(k)
         for mask in self.order:
-            for k in range(self.at.line):
-                self.core(mask, k).start()
-                self.local(mask, k).start()
-
-    def add(self, m, k, other):
-        total = self.sums[m, k].astype(f32) + other.astype(f32)
-        self.sums[m, k] = total.astype(self.sums.dtype)
-
-    def pair(self, mask, k):
-        self.local(mask, k).wait()
-        self.core(mask, k).wait_recv()
-        self.add(mask // 2, k, self.cbuf[mask // 2, k])
-
-    def pairs(self, mask):
-        at = self.at
-        for k in range(at.line):
-            self.pair(mask, k)
-            waits = at.square and mask == (2 if k < at.line // 2 else 4)
+            self.core(mask, t).start()
+            self.local(mask, t).start()
+
+    def pair(self, k):
+        at = self.at
+        t = self.far(k)
+        for mask in self.order:
+            m = mask // 2
+            self.local(mask, t).wait()
+            self.core(mask, t).wait_recv()
+            self.add(m, t, self.cbuf[m, t])
+            waits = at.square and mask == (2 if k % 2 == 0 else 4)
             if mask and not waits:
                 self.across(mask, k).start()
+        if k + 2 < at.line and not self.apart:
+            self.begin(k + 2)
 
     def joined(self, k):
         at = self.at
         if at.square:
-            mask = 2 if k < at.line // 2 else 4
+            mask = 2 if k % 2 == 0 else 4
+            t = self.far(k)
             self.across(6, k).wait_recv()
-            self.add(mask // 2, k, self.dbuf[2, k])
+            self.add(mask // 2, t, self.dbuf[2, t])
             self.across(mask, k).start()
 
     def own(self, k):
-        for mask in self.at.direct:
+        at = self.at
+        t = self.far(k)
+        for mask in at.direct:
             self.across(mask, k).wait_recv()
-            self.add(0, k, self.dbuf[mask // 2 - 1, k])
-        if k:
-            self.along(k).start()
-
-    def finish(self):
-        at = self.at
+            self.add(0, t, self.dbuf[mask // 2 - 1, t])
+        if k < at.line - 1:
+            self.along(t).start()
+
+    def finish(self, out_ref):
+        at = self.at
+        total = self.sums[0, at.z].astype(f32)
+        for k in range(1, at.line):
+            t = at.near(k)
+            buf, sem = self.zbuf.at[t], self.zr.at[t]
+            remote(buf, buf, sem, sem, (flipped(at.g, 1), at.z)).wait_recv()
+            total += self.zbuf[t].astype(f32)
+        out_ref[...] = total
         for k in range(at.line):
+            t = self.far(k)
             for mask in at.masks:
-                self.core(mask, k).wait_send()
+                self.core(mask, t).wait_send()
                 if mask:
                     self.across(mask, k).wait_send()
-            if k:
-                self.along(k).wait_send()
-                self.along(k).wait_recv()
-        total = self.sums[0, 0].astype(f32)
-        for k in range(1, at.line):
-            total += self.zbuf[k].astype(f32)
-        return total
+            if k < at.line - 1:
+                self.along(t).wait_send()
+
+    def early(self):
+        self.apart = True
+        line = self.at.line
+        out = []
+        for i in range(line):
+            todo = [functools.partial(self.begin, i)]
+            for work, late in ((self.pair, 1), (self.joined, 3)):
+                if i >= late:
+                    todo.append(functools.partial(work, i - late))
+            out.append(todo)
+        return out
+
+    def late(self):
+        line = self.at.line
+        out = [functools.partial(self.pair, line - 1)]
+        done = max(line - 3, 0)
+        for i in range(line):
+            if done + i < line:
+                out.append(functools.partial(self.joined, done + i))
+            out.append(functools.partial(self.own, i))
+        return out
+
+    def start(self):
+        self.begin(0)
+        self.begin(1)
 
     def steps(self):
-        ks = range(self.at.line)
+        line = self.at.line
         out = [self.start]
-        out += [functools.partial(self.pairs, mask) for mask in self.order]
-        out += [functools.partial(self.joined, k) for k in ks]
-        return out + [functools.partial(self.own, k) for k in ks]
-
-
-def run_ticks(ticks, step, half):
+        for i in range(line + 4):
+            for work, late in ((self.pair, 0), (self.joined, 2), (self.own, 4)):
+                if 0 <= i - late < line:
+                    out.append(functools.partial(work, i - late))
+        return out
+
+
+FWD = (3, 4, 7, 8, 8, 11, 12, 12, 15, 16)
+COT = 4
+ARRIVE = (0, 0, 1, 3)
+FFC = 2
+BACK = 6
+BWD = (2, 2, 7, 7, 7, 7, 16, 16, 16, 16, 27, 27)
+
+
+def run_ticks(ticks, step, part, parts):
     for at, work in ticks:
-        if at % 2 == half:
-            pl.when(step == at // 2)(work)
+        if at % parts == part:
+            pl.when(step == at // parts)(work)
 
 
 def arrive_kernel(groups, line, x_ref, shard_ref, small_ref, xo_ref, full_ref, smalls_ref, *sems):
@@ -402,11 +456,12 @@
     weights = Gather(at, shard_ref, full_ref, sems[:n])
     small = Gather(at, small_ref, smalls_ref, sems[n : 2 * n])
     at.barrier()
-    for one, two in zip(small.steps(), weights.steps()):
+    for i, (one, two) in enumerate(zip(small.steps(), weights.steps())):
         one()
         two()
-        if one == small.start:
-            rows.start()
+        for k in range(line):
+            if ARRIVE[min(k, 3)] == i:
+                rows.start_one(k)
     rows.finish()
 
 
@@ -429,7 +484,7 @@
 
 def leave_kernel(
     groups, line, gq_ref, gk_ref, gv_ref, w_ref, n1t_ref, x_ref, gh_ref, v_ref, smalls_ref,
-    yo_ref, shard_ref, small_ref, gn, y, full, smalls, *scratch
+    yo_ref, shard_ref, small_ref, gn, y, full, smalls, sums, *scratch
 ):
     at = Place(groups, line)
     n = len(ToOwner.sems(groups, line))
@@ -457,20 +512,20 @@
     @pl.when(step == line - 1)
     def _():
         part = x_ref.shape[1]
-
-        def piece(p, carry):
-            gain, shift = carry
-            hat, inverse = norm_stats(x_ref[p].astype(f32))
-            g = gn[p * part : (p + 1) * part]
-            y[p] = (gh_ref[p] + norm_back(g, hat, inverse, v_ref[0:1])).astype(bf16)
-            gain += jnp.sum(g * hat, axis=0, keepdims=True)
-            return gain, shift + jnp.sum(g, axis=0, keepdims=True)
-
-        zero = jnp.zeros((1, gn.shape[1]), f32)
-        carry = (zero, zero)
+        sums[...] = jnp.zeros_like(sums)
         for p in range(line):
-            carry = piece(p, carry)
-        rows.start()
+
+            def work(r, first, count, p=p):
+                at_rows = slice(p * part + first, p * part + first + count)
+                hat, inverse = norm_stats(x_ref[p, r].astype(f32))
+                g = gn[at_rows, :]
+                y[p, r] = (gh_ref[p, r] + norm_back(g, hat, inverse, v_ref[0:1])).astype(bf16)
+                add_rows(sums, 0, g * hat)
+                add_rows(sums, 8, g)
+
+            work(slice(0, part), 0, part)
+            rows.start_piece(p)
+        carry = [jnp.sum(sums[8 * j : 8 * j + 8], axis=0, keepdims=True) for j in range(2)]
         wide = gn.shape[1] // groups
         for j, total in enumerate(carry):
             for g in range(groups):
@@ -482,23 +537,29 @@
                     smalls[t, at_row : at_row + 1, :] = row
         small.start()
 
-    for t in range(line):
-
-        @pl.when(step == line + t)
-        def _(t=t):
-            for i, ref in enumerate(grads):
-                full[t, :, i * cols : (i + 1) * cols] = lax.dot_general(
-                    n1t_ref[...], ref[...], NN, preferred_element_type=f32
-                ).astype(bf16)
+    @pl.when(step >= line)
+    def _():
+        t = weights.far(step - line)
+        for i, ref in enumerate(grads):
+            full[t, :, i * cols : (i + 1) * cols] = lax.dot_general(
+                n1t_ref[...], ref[...], NN, preferred_element_type=f32
+            ).astype(bf16)
+
+    for i, todo in enumerate(weights.early()):
+
+        @pl.when(step == line + i)
+        def _(todo=todo):
+            for work in todo:
+                work()
 
     @pl.when(step == 2 * line - 1)
     def _():
-        for one, two in zip(weights.steps(), small.steps()):
-            one()
-            if two != small.start:
-                two()
-        shard_ref[...] = weights.finish()
-        small_ref[...] = small.finish()
+        for work in small.steps()[1:]:
+            work()
+        for work in weights.late():
+            work()
+        weights.finish(shard_ref)
+        small.finish(small_ref)
         rows.finish()
 
 
@@ -508,7 +569,12 @@
     cols = width // line
     r, c = width // groups, 3 * cols
     sr, sc = smalls.shape[1] // groups, smalls.shape[2]
-    grad = pl.BlockSpec((rows, cols), lambda j: (0, j % line))
+
+    def column(j):
+        far = Place(groups, line).near(jnp.clip(2 * line - 1 - j, 0, line - 1))
+        return 0, jnp.where(j < line, j, far)
+
+    grad = pl.BlockSpec((rows, cols), column)
     return pl.pallas_call(
         functools.partial(leave_kernel, groups, line),
         grid=(2 * line,),
@@ -534,6 +600,7 @@
             pltpu.VMEM((line, part, width), bf16),
             pltpu.VMEM((line, width, c), bf16),
             pltpu.VMEM(smalls.shape, f32),
+            pltpu.VMEM((16, width), f32),
         ]
         + ToOwner.sems(groups, line)
         + Reduce.scratch(groups, line, r, c, bf16)
@@ -561,7 +628,7 @@
 
 
 def project_kernel(flag_ref, x_ref, v_ref, w_ref, b_ref, out_ref, xc_ref, n1t_ref, n1):
-    @pl.when((pl.program_id(0) == 0) & (pl.program_id(1) == 0))
+    @pl.when(pl.program_id(0) == 0)
     def _():
         rows = x_ref.shape[0]
         size = 32 if rows % 32 == 0 else 16
@@ -575,15 +642,23 @@
             return carry
 
         lax.fori_loop(0, rows // size, chunk, 0)
-        n1t_ref[...] = n1[...].T
-
-    scale = jnp.where(pl.program_id(1) == 0, HD ** (-0.5) * LOG2E, 1.0)
-    out = lax.dot_general(n1[...], w_ref[0], NN, preferred_element_type=f32) + b_ref[0]
-    out_ref[0] = (out * scale).astype(bf16)
+    cols = out_ref.shape[2]
+    part = pl.ds(pl.multiple_of(pl.program_id(0) * cols, LANES), cols)
+    n1t_ref[part, :] = n1[:, part].T
+    for i in range(3):
+        w = w_ref[0, :, i * cols : (i + 1) * cols]
+        out = lax.dot_general(n1[...], w, NN, preferred_element_type=f32) + b_ref[i]
+        if i == 0:
+            out = out * (HD ** (-0.5) * LOG2E)
+        out_ref[i] = out.astype(bf16)
 
 
 def whole(*shape):
     return pl.BlockSpec(shape, lambda *_: (0,) * len(shape), pipeline_mode=pl.Buffered(1))
+
+
+def add_rows(ref, first, x):
+    ref[first : first + 1] += jnp.sum(x, axis=0, keepdims=True)
 
 
 SMEM = pl.BlockSpec(memory_space=pltpu.SMEM)
@@ -595,16 +670,16 @@
     cols = width // line
     return pl.pallas_call(
         project_kernel,
-        grid=(line, 3),
+        grid=(line,),
         in_specs=[
             SMEM,
             whole(rows, width),
             whole(*vectors.shape),
-            pl.BlockSpec((1, width, cols), lambda t, k: (t, 0, k)),
-            pl.BlockSpec((1, 1, cols), lambda t, k: (k, 0, t)),
+            pl.BlockSpec((1, width, 3 * cols), lambda t: (t, 0, 0)),
+            pl.BlockSpec((3, 1, cols), lambda t: (0, 0, t)),
         ],
         out_specs=[
-            pl.BlockSpec((1, rows, cols), lambda t, k: (k, 0, t)),
+            pl.BlockSpec((3, rows, cols), lambda t: (0, 0, t)),
             whole(rows, width),
             whole(width, rows),
         ],
@@ -671,44 +746,48 @@
 
 def turn_kernel(
     flag_ref, mlp_ref, gn_ref, hid_ref, x_ref, cot_ref, ctx_ref, v_ref, w_ref,
-    out_ref, gh_ref, gc_ref, gw_ref, sum_ref, acc
+    out_ref, gh_ref, gc_ref, gw_ref, sum_ref, acc, gattn, sums
 ):
     step = pl.program_id(0)
     line, _, cols = w_ref.shape
-    hidden = hid_ref[0]
-    mlp = mlp_ref[0] + v_ref[7:8]
-    gn = gn_ref[0]
-    valid = valid_rows(flag_ref, hidden.shape)
-    out_ref[0] = jnp.where(valid, hidden + v_ref[5:6] * mlp, 0.0).astype(bf16)
-    gout = jnp.where(valid, cot_ref[0].astype(f32), 0.0)
-    hat, inverse = norm_stats(hidden)
-    ghid = gout + norm_back(gn, hat, inverse, v_ref[1:2])
-    gh_ref[0] = ghid
-    gattn = ghid * v_ref[4:5]
-    attn = (hidden - x_ref[0].astype(f32)) / v_ref[4:5]
-
-    def total(x):
-        return jnp.sum(x, axis=0, keepdims=True)
-
-    sums = [gn * hat, gn, ghid * attn, gout * mlp, gattn, gout * v_ref[5:6]]
-    sums = jnp.concatenate([total(x) for x in sums] + [jnp.zeros((2, gn.shape[1]), f32)], axis=0)
+    part = hid_ref.shape[1]
 
     @pl.when(step == 0)
     def _():
-        sum_ref[...] = sums
+        sums[...] = jnp.zeros_like(sums)
         acc[...] = jnp.zeros_like(acc)
 
-    @pl.when(step > 0)
+    def work(r, first, count):
+        hidden = hid_ref[0, r]
+        mlp = mlp_ref[0, r] + v_ref[7:8]
+        gn = gn_ref[0, r]
+        row = step * part + first + lax.broadcasted_iota(jnp.int32, hidden.shape, 0)
+        valid = row < flag_ref[0]
+        out_ref[0, r] = jnp.where(valid, hidden + v_ref[5:6] * mlp, 0.0).astype(bf16)
+        gout = jnp.where(valid, cot_ref[0, r].astype(f32), 0.0)
+        hat, inverse = norm_stats(hidden)
+        ghid = gout + norm_back(gn, hat, inverse, v_ref[1:2])
+        gh_ref[0, r] = ghid
+        attn = (hidden - x_ref[0, r].astype(f32)) / v_ref[4:5]
+        grad = ghid * v_ref[4:5]
+        gattn[r] = grad.astype(bf16)
+        terms = (gn * hat, gn, ghid * attn, gout * mlp, grad, gout * v_ref[5:6])
+        for j, term in enumerate(terms):
+            add_rows(sums, 8 * j, term)
+
+    work(slice(0, part), 0, part)
+
+    @pl.when(step == line - 1)
     def _():
-        sum_ref[...] += sums
-
-    gattn = gattn.astype(bf16)
+        rows = [jnp.sum(sums[8 * j : 8 * j + 8], axis=0, keepdims=True) for j in range(6)]
+        sum_ref[...] = jnp.concatenate(rows + [jnp.zeros((2, sums.shape[1]), f32)], axis=0)
+
     for t in range(line):
-        part = ctx_ref[0, :, t * cols : (t + 1) * cols]
+        ctx = ctx_ref[0, :, t * cols : (t + 1) * cols]
         gc_ref[0, :, t * cols : (t + 1) * cols] = lax.dot_general(
-            gattn, w_ref[t], NN, preferred_element_type=f32
+            gattn[...], w_ref[t], NN, preferred_element_type=f32
         ).astype(bf16)
-        acc[t] += lax.dot_general(gattn, part, TN, preferred_element_type=f32)
+        acc[t] += lax.dot_general(gattn[...], ctx, TN, preferred_element_type=f32)
 
     @pl.when(step == line - 1)
     def _():
@@ -738,7 +817,11 @@
             jax.ShapeDtypeStruct((line, width, cols), bf16),
             jax.ShapeDtypeStruct((8, width), f32),
         ],
-        scratch_shapes=[pltpu.VMEM((line, width, cols), f32)],
+        scratch_shapes=[
+            pltpu.VMEM((line, width, cols), f32),
+            pltpu.VMEM((part, width), bf16),
+            pltpu.VMEM((48, width), f32),
+        ],
         compiler_params=pltpu.CompilerParams(vmem_limit_bytes=56 * 2**20),
         name="turn",
     )(flags, mlp, gn, hidden, x, cot, context, vectors, weights)
@@ -753,18 +836,14 @@
     weights = Gather(at, shard_ref, full_ref, sems[:n])
     cot = ToOwner(at, cot_ref, coto_ref, sems[n:])
     steps = weights.steps()
-    halves = 2 * pl.num_programs(0)
-    first, spreads, passes, rest = steps[0], steps[1:line], steps[line : 2 * line], steps[2 * line :]
 
     def begin():
         at.barrier()
-        first()
-
-    ticks = [(0, begin), (6, cot.start)]
-    for k in range(1, line):
-        ticks.append((min(4 * k, 15), spreads[k - 1]))
-    for k in range(line):
-        ticks.append((min(4 * k + 4, 15), passes[k]))
+        steps[0]()
+
+    ticks = [(0, begin), (COT, cot.start)]
+    for i, work in enumerate(steps[1:]):
+        ticks.append((FWD[min(i, len(FWD) - 1)], work))
     step = pl.program_id(0)
     length = len_ref[0]
     lane = lax.broadcasted_iota(jnp.int32, (padded, LANES), 1)
@@ -773,7 +852,7 @@
     if padded > rows:
         va[rows:] = jnp.zeros((padded - rows, LANES), bf16)
     for half in range(2):
-        run_ticks(ticks, step, half)
+        run_ticks(ticks, step, half, 2)
         own = (lb < HD) if half == 0 else (lb >= HD)
         spare = HD if half == 0 else 0
         ka[:rows] = keys_with_bias(k_ref[...].astype(f32), lb, row[:rows], length, own, spare)
@@ -800,8 +879,9 @@
 
     @pl.when(step == pl.num_programs(0) - 1)
     def _():
-        for work in rest:
-            work()
+        for at_tick, work in ticks:
+            if at_tick > 15:
+                work()
         cot.finish()
 
 
@@ -850,7 +930,6 @@
     weights = Reduce(at, full_ref, scratch[n : n + m], shard_ref.shape[0])
     out_weights = Reduce(at, out_ref, scratch[n + m :], oshard_ref.shape[0])
     pairs = list(zip(weights.steps(), out_weights.steps()))
-    chips = groups // 2
 
     def both(i):
         def run():
@@ -864,15 +943,10 @@
     def begin():
         at.barrier()
         steps[0]()
-        back.start()
-
-    ticks = [(0, begin)]
-    for i in range(chips):
-        ticks.append((min(i + 1, 4), steps[1 + i]))
-    for k in range(line):
-        ticks.append((min(6 + k // 2, 15), steps[1 + chips + k]))
-    for k in range(line):
-        ticks.append((12, steps[1 + chips + line + k]))
+
+    ticks = [(0, begin), (BACK * blocks // 2, back.start)]
+    for i, work in enumerate(steps[1:]):
+        ticks.append((BWD[min(i, len(BWD) - 1)] * blocks // 2, work))
     step = pl.program_id(0)
     length = len_ref[0]
     lane = lax.broadcasted_iota(jnp.int32, (padded, LANES), 1)
@@ -880,7 +954,6 @@
     size = rows // blocks
     ls = lane[:rows]
     for half in range(2):
-        run_ticks(ticks, step, half)
         own = (ls < HD) if half == 0 else (ls >= HD)
         spare = HD if half == 0 else 0
         ownb = own[:size]
@@ -898,27 +971,25 @@
         ka[...] = keys_with_bias(k_ref[...].astype(f32), ls, row[:rows], length, own, spare)
         ones = jnp.where((ls >= spare) & (ls < spare + 3), 1.0, 0.0)
         va[...] = jnp.where(own, v_ref[...].astype(f32), ones).astype(bf16)
-        acc[...] = jnp.zeros_like(acc)
-
-        def block(b, carry):
-            r = pl.ds(pl.multiple_of(b * size, 16), size)
-            kb = ka[r, :]
+        bv = jnp.zeros((1, LANES), f32)
+        for b in range(blocks):
+            run_ticks(ticks, step, half * blocks + b, 2 * blocks)
+            r = slice(b * size, (b + 1) * size)
+            kb = ka[r]
             p = jnp.exp2(lax.dot_general(kb, qs[...], NT, preferred_element_type=f32))
-            gp = lax.dot_general(va[r, :], ga[...], NT, preferred_element_type=f32)
+            gp = lax.dot_general(va[r], ga[...], NT, preferred_element_type=f32)
             ds = (p * gp).astype(bf16)
             gv = lax.dot_general(p.astype(bf16), ga[...], NN, preferred_element_type=f32)
             gk = lax.dot_general(ds, qs[...], NN, preferred_element_type=f32) * (1.0 / LOG2E)
-            acc[...] += lax.dot_general(kb.T, ds, NN, preferred_element_type=f32)
-            bv = carry + jnp.sum(gv, axis=0, keepdims=True)
+            gqt = lax.dot_general(kb.T, ds, NN, preferred_element_type=f32)
+            acc[...] = gqt if b == 0 else acc[...] + gqt
+            bv += jnp.sum(gv, axis=0, keepdims=True)
             if half == 0:
-                gv_ref[r, :] = gv.astype(bf16)
-                gk_ref[r, :] = gk.astype(bf16)
+                gv_ref[r] = gv.astype(bf16)
+                gk_ref[r] = gk.astype(bf16)
             else:
-                gv_ref[r, :] = jnp.where(ownb, gv, gv_ref[r, :].astype(f32)).astype(bf16)
-                gk_ref[r, :] = jnp.where(ownb, gk, gk_ref[r, :].astype(f32)).astype(bf16)
-            return bv
-
-        bv = lax.fori_loop(0, blocks, block, jnp.zeros((1, LANES), f32))
+                gv_ref[r] = jnp.where(ownb, gv, gv_ref[r].astype(f32)).astype(bf16)
+                gk_ref[r] = jnp.where(ownb, gk, gk_ref[r].astype(f32)).astype(bf16)
         gq = acc[...].T[:rows] * HD ** (-0.5)
         sums = jnp.concatenate(
             [jnp.sum(gq, axis=0, keepdims=True), bv, jnp.zeros((6, LANES), f32)], axis=0
@@ -934,8 +1005,11 @@
 
     @pl.when(step == pl.num_programs(0) - 1)
     def _():
-        shard_ref[...] = weights.finish()
-        oshard_ref[...] = out_weights.finish()
+        for at_tick, work in ticks:
+            if at_tick >= 2 * blocks * 8:
+                work()
+        weights.finish(shard_ref)
+        out_weights.finish(oshard_ref)
         back.finish()
 
 
@@ -995,43 +1069,36 @@
 
 
 def feed_forward_kernel(
-    tile, n2_ref, gm_ref, w_ref, b1_ref, mlp_ref, gn_ref, gw_ref, gb_ref, n2t, gmt
+    tile, chunks, n2_ref, gm_ref, w_ref, b1_ref, mlp_ref, gn_ref, gw_ref, gb_ref, n2t, gmt, act_s, gpre_s
 ):
-    step = pl.program_id(0)
-
-    @pl.when(step == 0)
+    @pl.when(pl.program_id(0) == 0)
     def _():
         n2t[...] = n2_ref[...].T
         gmt[...] = gm_ref[...].T
+        mlp_ref[...] = jnp.zeros_like(mlp_ref)
+        gn_ref[...] = jnp.zeros_like(gn_ref)
 
     w1 = w_ref[0, :, :tile]
     w2t = w_ref[0, :, tile:]
-    pre = lax.dot_general(n2_ref[...], w1, NN, preferred_element_type=f32) + b1_ref[...]
-    gact = lax.dot_general(gm_ref[...], w2t, NN, preferred_element_type=f32)
-    cdf = 0.5 * (1.0 + lax.erf(pre * (1 / math.sqrt(2))))
-    act = (pre * cdf).astype(bf16)
-    pdf = jnp.exp2(pre * pre * (-0.5 * LOG2E)) * (1 / math.sqrt(2 * math.pi))
-    gpre = gact * (cdf + pre * pdf)
-    gb_ref[...] = jnp.sum(gpre, axis=0, keepdims=True)
-    gpre = gpre.astype(bf16)
-    mlp = lax.dot_general(act, w2t, NT, preferred_element_type=f32)
-    gn = lax.dot_general(gpre, w1, NT, preferred_element_type=f32)
-
-    @pl.when(step == 0)
-    def _():
-        mlp_ref[...] = mlp
-        gn_ref[...] = gn
-
-    @pl.when(step > 0)
-    def _():
-        mlp_ref[...] += mlp
-        gn_ref[...] += gn
-
+    size = n2_ref.shape[0] // chunks
+    for c in range(chunks):
+        r = slice(c * size, (c + 1) * size)
+        pre = lax.dot_general(n2_ref[r], w1, NN, preferred_element_type=f32) + b1_ref[...]
+        gact = lax.dot_general(gm_ref[r], w2t, NN, preferred_element_type=f32)
+        cdf = 0.5 * (1.0 + lax.erf(pre * (1 / math.sqrt(2))))
+        act_s[r] = (pre * cdf).astype(bf16)
+        pdf = jnp.exp2(pre * pre * (-0.5 * LOG2E)) * (1 / math.sqrt(2 * math.pi))
+        gpre = gact * (cdf + pre * pdf)
+        total = jnp.sum(gpre, axis=0, keepdims=True)
+        gb_ref[...] = total if c == 0 else gb_ref[...] + total
+        gpre_s[r] = gpre.astype(bf16)
+        mlp_ref[r] += lax.dot_general(act_s[r], w2t, NT, preferred_element_type=f32)
+        gn_ref[r] += lax.dot_general(gpre_s[r], w1, NT, preferred_element_type=f32)
     gw_ref[0, :, :tile] = lax.dot_general(
-        n2t[...], gpre, NN, preferred_element_type=f32
+        n2t[...], gpre_s[...], NN, preferred_element_type=f32
     ).astype(bf16)
     gw_ref[0, :, tile:] = lax.dot_general(
-        gmt[...], act, NN, preferred_element_type=f32
+        gmt[...], act_s[...], NN, preferred_element_type=f32
     ).astype(bf16)
 
 
@@ -1042,7 +1109,7 @@
 
     both = pl.BlockSpec((1, width, 2 * tile), lambda j: (j // per, 0, j % per))
     return pl.pallas_call(
-        functools.partial(feed_forward_kernel, tile),
+        functools.partial(feed_forward_kernel, tile, FFC if rows % (16 * FFC) == 0 else 1),
         grid=(units // tile,),
         in_specs=[
             whole(rows, width),
@@ -1062,8 +1129,8 @@
             jax.ShapeDtypeStruct(weights.shape, bf16),
             jax.ShapeDtypeStruct((1, units), f32),
         ],
-        scratch_shapes=[pltpu.VMEM((width, rows), bf16), pltpu.VMEM((width, rows), bf16)],
-        compiler_params=pltpu.CompilerParams(vmem_limit_bytes=60 * 2**20),
+        scratch_shapes=[pltpu.VMEM((width, rows), bf16)] * 2 + [pltpu.VMEM((rows, tile), bf16)] * 2,
+        compiler_params=pltpu.CompilerParams(vmem_limit_bytes=62 * 2**20),
         cost_estimate=pl.CostEstimate(
             flops=16 * rows * width * units,
             bytes_accessed=8 * width * units,

time: 632 us -> 589 us (0.932)
  Pallas kernels: 576 us -> 529 us
    pallas_call x1, Pallas kernels: 162 us -> 130 us  [attend_backward(): pl.pallas_call(functools.partial(attend_backward_kernel, groups, line, ro...]
    pallas_call x2, Pallas kernels: 119 us -> 105 us  [the longest x1 83.7 us: feed_forward(): pl.pallas_call(functools.partial(feed_forward_kernel, tile, FFC if rows %...]
    pallas_call x1, Pallas kernels: 69.4 us -> 76.9 us  [arrive(): pl.pallas_call(functools.partial(arrive_kernel, groups, line), in_specs=[...]
    pallas_call x1, Pallas kernels: 90 us -> 83.5 us  [leave(): pl.pallas_call(functools.partial(leave_kernel, groups, line), grid=(2 * l...]
where the time goes in v4:
time: 589 us; the launch traced here: 582 us
  Pallas kernels  529 us (90%)
  local copies, waits for them, and re-layouts  40.7 us (7%)
  other arithmetic  10.3 us (2%)
    pallas_call x1, Pallas kernels, attend_backward(): pl.pallas_call(functools.partial(attend_backward_kernel, groups, line, ro...  130 us
    pallas_call x1, Pallas kernels, attend_forward(): pl.pallas_call(functools.partial(attend_forward_kernel, groups, line, row...  101 us
    pallas_call x1, Pallas kernels, feed_forward(): pl.pallas_call(functools.partial(feed_forward_kernel, tile, FFC if rows %...  83.7 us
    pallas_call x1, Pallas kernels, leave(): pl.pallas_call(functools.partial(leave_kernel, groups, line), grid=(2 * l...  83.5 us
    pallas_call x1, Pallas kernels, arrive(): pl.pallas_call(functools.partial(arrive_kernel, groups, line), in_specs=[...  76.9 us
    pallas_call x1, Pallas kernels, turn(): pl.pallas_call(turn_kernel, grid=(line,), in_specs=[SMEM] + [piece] * 6 +...  23 us
    pallas_call x1, Pallas kernels, project(): pl.pallas_call(project_kernel, grid=(line,), in_specs=[SMEM, whole(rows,...  21.2 us
    unnamed x45, local copies, waits for them, and re-layouts  15.6 us

profile of v4, /device:TPU:0, one launch (start us, length us, event | category | flops | bytes accessed | tf_op | source)
XLA Modules:
  0.0 582.0 jit_solution(17376555058402059382)
XLA Ops:
  0.7 1.2 dynamic_slice.6
  9.4 1.8 concatenate.20.small_ref
  11.2 76.9 %arrive.1 = (bf16[4,344,1024]{2,1,0:T(8,128)(2,1)}, bf16[4,1024,1024]{2,1,0:T(8,128)(2,1)}, f32[4,256,128]{2,1,0:T(8,128)}) custom-call(bf16[3,344,1024]{2,1,0:T(8,128)(2,1)} %x_ref.1, bf16[128,1024]{1,0:T(8,128)(2,1)} %pad_maximum_fusion.2.shard_ref, f32[32,128]{1,0:T(8,128)} %concatenate.20.small_ref), custom_call_target="tpu_custom_call" | custom-call | tf_op jit(solution)/shard_map/arrive/pallas_call | solution.py:470
  91.6 1.8 copy-done.7
  93.4 21.2 %project.1 = (bf16[3,1376,1024]{2,1,0:T(8,128)(2,1)}, bf16[1376,1024]{1,0:T(8,128)(2,1)S(1)}, bf16[1024,1376]{1,0:T(8,128)(2,1)S(1)}) custom-call(s32[2]{0:T(128)S(1)} %pad_add_fusion.flag_ref.len_ref, bf16[1376,1024]{1,0:T(8,128)(2,1)S(1)} %bitcast.66, f32[8,1024]{1,0:T(8,128)S(1)} %reshape.101.v_ref, bf16[4,1024,1024]{2,1,0:T(8,128)(2,1)} %get-tuple-element.46.w_ref, ...), custom_call_target="tpu_custom_call" | custom-call | flops 8657043456 | bytes 22544384 | tf_op jit(solution)/shard_map/project/pallas_call | solution.py:671
  114.6 1.6 copy-done.3
  116.2 1.4 copy.73
  118.5 2.3 pad_maximum_fusion
  120.8 1.2 reshape.105.shard_ref
  122.0 101.2 %attend_forward.1 = (bf16[1376,1024]{1,0:T(8,128)(2,1)}, bf16[16,1376,128]{2,1,0:T(8,128)(2,1)}, bf16[4,1024,2048]{2,1,0:T(8,128)(2,1)}, bf16[4,344,1024]{2,1,0:T(8,128)(2,1)}) custom-call(s32[2]{0:T(128)} %copy-done.5, bf16[3,1376,1024]{2,1,0:T(8,128)(2,1)} %get-tuple-element.47.q_ref.k_ref.v_ref, ...), custom_call_target="tpu_custom_call" | custom-call | flops 31021072384 | bytes 16908288 | tf_op jit(solution)/shard_map/attend_forward/pallas_call | solution.py:896
  223.3 1.8 copy-done.1
  225.1 1.8 copy-done.2
  226.9 9.1 %middle.1 = (f32[4,344,1024]{2,1,0:T(8,128)}, bf16[4,344,1024]{2,1,0:T(8,128)(2,1)S(1)}, bf16[4,344,1024]{2,1,0:T(8,128)(2,1)S(1)}) custom-call(s32[2]{0:T(128)S(1)} %copy-done.6, bf16[4,344,1024]{2,1,0:T(8,128)(2,1)S(1)} %bitcast.65, bf16[4,344,1024]{2,1,0:T(8,128)(2,1)S(1)} %bitcast.61, bf16[4,344,1024]{2,1,0:T(8,128)(2,1)S(1)} %copy-done.2, ...), custom_call_target="tpu_custom_call" | custom-call | tf_op jit(solution)/shard_map/middle/pallas_call | solution.py:723
  236.0 1.7 copy-done.8
  237.7 1.6 copy-done.9
  241.1 83.7 %feed_forward.1 = (f32[1376,1024]{1,0:T(8,128)}, f32[1376,1024]{1,0:T(8,128)}, bf16[4,1024,2048]{2,1,0:T(8,128)(2,1)}, f32[1,4096]{1,0:T(1,128)}) custom-call(bf16[1376,1024]{1,0:T(8,128)(2,1)} %bitcast.67, bf16[1376,1024]{1,0:T(8,128)(2,1)} %bitcast.68, bf16[4,1024,2048]{2,1,0:T(8,128)(2,1)} %get-tuple-element.54.w_ref, f32[1,4096]{1,0:T(1,128)} %reshape.110.b1_ref), custom_call_target="tpu_custom_call" | custom-call | flops 92341796864 | bytes 33554432 | tf_op jit(solution)/shard_map/feed_forward/pallas_call | solution.py:1111
  324.8 23.0 %turn.1 = (bf16[4,344,1024]{2,1,0:T(8,128)(2,1)}, f32[4,344,1024]{2,1,0:T(8,128)}, bf16[4,344,1024]{2,1,0:T(8,128)(2,1)}, bf16[4,1024,256]{2,1,0:T(8,128)(2,1)}, f32[8,1024]{1,0:T(8,128)}) custom-call(s32[2]{0:T(128)} %copy-done.5, f32[4,344,1024]{2,1,0:T(8,128)} %bitcast.69, f32[4,344,1024]{2,1,0:T(8,128)} %bitcast.70, ...), custom_call_target="tpu_custom_call" | custom-call | tf_op jit(solution)/shard_map/turn/pallas_call | solution.py:801
  347.8 130.2 %attend_backward.1 = (bf16[1376,1024]{1,0:T(8,128)(2,1)}, bf16[1376,1024]{1,0:T(8,128)(2,1)}, bf16[1376,1024]{1,0:T(8,128)(2,1)}, f32[8,8,128]{2,1,0:T(8,128)}, ...) custom-call(s32[2]{0:T(128)} %copy-done.5, ...), custom_call_target="tpu_custom_call" | custom-call | flops 77552680960 | bytes 22544384 | tf_op jit(solution)/shard_map/attend_backward/pallas_call | solution.py:1026
  481.8 83.5 %leave.1 = (bf16[3,344,1024]{2,1,0:T(8,128)(2,1)}, f32[128,768]{1,0:T(8,128)}, f32[32,128]{1,0:T(8,128)}) custom-call(bf16[1376,1024]{1,0:T(8,128)(2,1)} %get-tuple-element.63.gq_ref, bf16[1376,1024]{1,0:T(8,128)(2,1)} %get-tuple-element.64.gk_ref, bf16[1376,1024]{1,0:T(8,128)(2,1)} %get-tuple-element.65.gv_ref, ...), custom_call_target="tpu_custom_call" | custom-call | tf_op jit(solution)/shard_map/leave/pallas_call | solution.py:578
  565.3 4.1 convert_element_type.19
  571.7 2.3 reshape.120
  574.0 2.1 fusion.1
  577.6 1.9 copy.80
  580.2 1.3 copy.99
  (79 shorter events, 21.1 us)
Async XLA Ops:
  2.6 112.0 %copy-start.5 = (s32[2]{0:T(128)}, s32[2]{0:T(128)S(1)}, u32[]{:S(2)}) copy-start(s32[2]{0:T(128)S(1)} %pad_add_fusion.flag_ref.len_ref) | copy-start | bytes 28
  89.3 133.9 %copy-start.4 = (f32[8,1024]{1,0:T(8,128)}, f32[8,1024]{1,0:T(8,128)S(1)}, u32[]{:S(2)}) copy-start(f32[8,1024]{1,0:T(8,128)S(1)} %reshape.101.v_ref) | copy-start | bytes 98308
  91.6 1.8 copy-start.7
  93.4 22.8 %copy-start.12 = (bf16[1024,128]{1,0:T(8,128)(2,1)S(1)}, bf16[1024,128]{1,0:T(8,128)(2,1)}, u32[]{:S(2)}) copy-start(bf16[1024,128]{1,0:T(8,128)(2,1)} %param.21) | copy-start | bytes 786436
  93.4 24.3 %copy-start.13 = (bf16[128,1024]{1,0:T(8,128)(2,1)S(1)}, bf16[128,1024]{1,0:T(8,128)(2,1)}, u32[]{:S(2)}) copy-start(bf16[128,1024]{1,0:T(8,128)(2,1)} %param.19) | copy-start | bytes 786436
  114.6 1.6 copy-start.3
  116.2 107.1 %copy-start = (bf16[1376,1024]{1,0:T(8,128)(2,1)}, bf16[1376,1024]{1,0:T(8,128)(2,1)S(1)}, u32[]{:S(2)}) copy-start(bf16[1376,1024]{1,0:T(8,128)(2,1)S(1)} %get-tuple-element.50) | copy-start | bytes 8454148
  122.0 101.3 %copy-start.6 = (s32[2]{0:T(128)S(1)}, s32[2]{0:T(128)}, u32[]{:S(2)}) copy-start(s32[2]{0:T(128)} %copy-done.5) | copy-start | bytes 28
  223.3 1.8 copy-start.1
  225.1 1.8 copy-start.2
  236.0 1.7 copy-start.8
  237.7 1.6 copy-start.9
  347.8 130.7 %copy-start.17 = (f32[1,4096]{1,0:T(1,128)S(1)}, f32[1,4096]{1,0:T(1,128)}, u32[]{:S(2)}) copy-start(f32[1,4096]{1,0:T(1,128)} %get-tuple-element.70) | copy-start | bytes 49156
  347.8 133.0 %copy-start.15 = (f32[8,1024]{1,0:T(8,128)S(1)}, f32[8,1024]{1,0:T(8,128)}, u32[]{:S(2)}) copy-start(f32[8,1024]{1,0:T(8,128)} %get-tuple-element.68) | copy-start | bytes 98308
  565.3 4.2 copy-start.11
  565.3 5.0 copy-start.16
  565.3 5.6 copy-start.14
  571.7 8.5 %copy-start.10 = (bf16[3,344,1024]{2,1,0:T(8,128)(2,1)S(1)}, bf16[3,344,1024]{2,1,0:T(8,128)(2,1)}, u32[]{:S(2)}) copy-start(bf16[3,344,1024]{2,1,0:T(8,128)(2,1)} %get-tuple-element.150) | copy-start | bytes 6340612

commit v5 on v4

--- a/solution.py
+++ b/solution.py
@@ -340,8 +340,7 @@
         )
 
     def add(self, m, t, other):
-        total = self.sums[m, t].astype(f32) + other.astype(f32)
-        self.sums[m, t] = total.astype(self.sums.dtype)
+        self.sums[m, t] = self.sums[m, t] + other
 
     def begin(self, k):
         t = self.far(k)
@@ -689,7 +688,7 @@
             jax.ShapeDtypeStruct((width, rows), bf16),
         ],
         scratch_shapes=[pltpu.VMEM((rows, width), bf16)],
-        compiler_params=pltpu.CompilerParams(vmem_limit_bytes=40 * 2**20),
+        compiler_params=pltpu.CompilerParams(vmem_limit_bytes=62 * 2**20),
         cost_estimate=pl.CostEstimate(
             flops=6 * rows * width * width, bytes_accessed=16 * rows * width, transcendentals=0
         ),
@@ -739,7 +738,7 @@
             jax.ShapeDtypeStruct(x.shape, bf16),
             jax.ShapeDtypeStruct(x.shape, bf16),
         ],
-        compiler_params=pltpu.CompilerParams(vmem_limit_bytes=40 * 2**20),
+        compiler_params=pltpu.CompilerParams(vmem_limit_bytes=62 * 2**20),
         name="middle",
     )(flags, context, x, cot, vectors, weights)
 
@@ -822,7 +821,7 @@
             pltpu.VMEM((part, width), bf16),
             pltpu.VMEM((48, width), f32),
         ],
-        compiler_params=pltpu.CompilerParams(vmem_limit_bytes=56 * 2**20),
+        compiler_params=pltpu.CompilerParams(vmem_limit_bytes=62 * 2**20),
         name="turn",
     )(flags, mlp, gn, hidden, x, cot, context, vectors, weights)
 
@@ -908,7 +907,7 @@
         + Gather.sems(groups, line)
         + ToOwner.sems(groups, line),
         compiler_params=pltpu.CompilerParams(
-            collective_id=3, has_side_effects=True, vmem_limit_bytes=56 * 2**20
+            collective_id=3, has_side_effects=True, vmem_limit_bytes=62 * 2**20
         ),
         cost_estimate=pl.CostEstimate(
             flops=16 * rows * rows * width,
@@ -1166,9 +1165,14 @@
 
     tile = min(512, w_fc1.shape[1])
     qkv_out = jnp.concatenate([w_qkv[0], w_qkv[1], w_qkv[2], w_out.T], axis=1)
-    tiles = (w_fc1.shape[0], -1, 1, tile)
-    fc_both = jnp.concatenate([w_fc1.reshape(tiles), w_fc2.T.reshape(tiles)], axis=2).reshape(
-        w_fc1.shape[0], -1
+    w_fc2_t = w_fc2.T
+    fc_both = jnp.concatenate(
+        [
+            w[:, at : at + tile]
+            for at in range(0, w_fc1.shape[1], tile)
+            for w in (w_fc1, w_fc2_t)
+        ],
+        axis=1,
     )
 
     def lanes(x):
@@ -1177,8 +1181,9 @@
     own_width = ln_gain.shape[1]
     _, bq_rows, bq_cols = b_qv.shape
     f_rows, f_cols = b_fc1.shape
-    small = [ln_gain, ln_shift, layer_scale, out_bias, b_qv.astype(f32).reshape(-1, bq_cols)]
-    small = jnp.concatenate([lanes(x) for x in small + [b_fc1.astype(f32)]], axis=0)
+    small = jnp.concatenate([ln_gain, ln_shift, layer_scale, out_bias], axis=0)
+    small = [small, b_qv.reshape(-1, bq_cols).astype(f32), b_fc1.astype(f32)]
+    small = jnp.concatenate([lanes(x) for x in small], axis=0)
     small_rows = round_up(small.shape[0], 8)
     small = jnp.pad(small, ((0, small_rows - small.shape[0]), (0, 0)))
     b_at = 8 + 2 * bq_rows
@@ -1273,9 +1278,17 @@
     cols = width // line
     shard_wqkv = jnp.stack([shard_weights[:, n * cols : (n + 1) * cols] for n in range(3)])
     shard_wout = shard_wout.T
-    shard_fc = shard_fc.reshape(shard_fc.shape[0], -1, 2, tile)
-    shard_fc1 = shard_fc[:, :, 0].reshape(w_fc1.shape)
-    shard_fc2 = shard_fc[:, :, 1].reshape(w_fc1.shape).T
+    shard_fc1, shard_fc2 = (
+        jnp.concatenate(
+            [
+                shard_fc[:, at : at + tile]
+                for at in range(first, shard_fc.shape[1], 2 * tile)
+            ],
+            axis=1,
+        )
+        for first in (0, tile)
+    )
+    shard_fc2 = shard_fc2.T
     own = lax.dynamic_slice_in_dim(shard_small[:8], place * own_width, own_width, 1)
     shard_gain, shard_shift, shard_scale, shard_bias = (own[2 * n : 2 * n + 2] for n in range(4))
     shard_bqv = shard_small[8:b_at, :bq_cols].reshape(b_qv.shape)

time: 589 us -> 567 us (0.963)
  local copies, waits for them, and re-layouts: 40.7 us -> 17 us
    unnamed x45 -> x28, local copies, waits for them, and re-layouts: 15.6 us -> 5.68 us
    reshape x5 -> x0, local copies, waits for them, and re-layouts: 6.57 us -> none  [the longest x1 2.26 us: body(): shard_fc = shard_fc.reshape(shard_fc.shape[0], -1, 2, tile)]
where the time goes in v5:
time: 567 us; the launch traced here: 562 us
  Pallas kernels  531 us (94%)
  local copies, waits for them, and re-layouts  17 us (3%)
  other arithmetic  12.3 us (2%)
    pallas_call x1, Pallas kernels, attend_backward(): pl.pallas_call(functools.partial(attend_backward_kernel, groups, line, ro...  130 us
    pallas_call x1, Pallas kernels, attend_forward(): pl.pallas_call(functools.partial(attend_forward_kernel, groups, line, row...  101 us
    pallas_call x1, Pallas kernels, leave(): pl.pallas_call(functools.partial(leave_kernel, groups, line), grid=(2 * l...  83.5 us
    pallas_call x1, Pallas kernels, feed_forward(): pl.pallas_call(functools.partial(feed_forward_kernel, tile, FFC if rows %...  83.3 us
    pallas_call x1, Pallas kernels, arrive(): pl.pallas_call(functools.partial(arrive_kernel, groups, line), in_specs=[...  76.9 us
    pallas_call x1, Pallas kernels, project(): pl.pallas_call(project_kernel, grid=(line,), in_specs=[SMEM, whole(rows,...  23.2 us
    pallas_call x1, Pallas kernels, turn(): pl.pallas_call(turn_kernel, grid=(line,), in_specs=[SMEM] + [piece] * 6 +...  23 us

profile of v5, /device:TPU:0, one launch (start us, length us, event | category | flops | bytes accessed | tf_op | source)
XLA Modules:
  0.0 562.5 jit_solution(14381807937645110701)
XLA Ops:
  0.7 1.2 dynamic_slice.6
  3.1 0.9 copy.64
  4.1 0.9 slice_bitcast_fusion.6
  6.4 0.8 copy.79
  8.6 76.9 %arrive.1 = (bf16[4,344,1024]{2,1,0:T(8,128)(2,1)}, bf16[4,1024,1024]{2,1,0:T(8,128)(2,1)}, f32[4,256,128]{2,1,0:T(8,128)}) custom-call(bf16[3,344,1024]{2,1,0:T(8,128)(2,1)} %x_ref.1, bf16[128,1024]{1,0:T(8,128)(2,1)} %pad_maximum_fusion.3.shard_ref, f32[32,128]{1,0:T(8,128)} %pad_maximum_fusion.4.small_ref), custom_call_target="tpu_custom_call" | custom-call | tf_op jit(solution)/shard_map/arrive/pallas_call | solution.py:469
  85.5 0.9 slice.126
  87.3 1.0 slice_bitcast_fusion
  90.1 23.2 %project.1 = (bf16[3,1376,1024]{2,1,0:T(8,128)(2,1)}, bf16[1376,1024]{1,0:T(8,128)(2,1)}, bf16[1024,1376]{1,0:T(8,128)(2,1)}) custom-call(s32[2]{0:T(128)} %pad_add_fusion.flag_ref.len_ref, bf16[1376,1024]{1,0:T(8,128)(2,1)} %bitcast.77, f32[8,1024]{1,0:T(8,128)} %reshape.87.v_ref, bf16[4,1024,1024]{2,1,0:T(8,128)(2,1)} %get-tuple-element.46.w_ref, ...), custom_call_target="tpu_custom_call" | custom-call | flops 8657043456 | bytes 22544384 | tf_op jit(solution)/shard_map/project/pallas_call | solution.py:670
  113.5 0.8 pad_maximum_fusion.shard_ref
  114.4 101.0 %attend_forward.1 = (bf16[1376,1024]{1,0:T(8,128)(2,1)}, bf16[16,1376,128]{2,1,0:T(8,128)(2,1)}, bf16[4,1024,2048]{2,1,0:T(8,128)(2,1)}, bf16[4,344,1024]{2,1,0:T(8,128)(2,1)}) custom-call(s32[2]{0:T(128)} %pad_add_fusion.flag_ref.len_ref, bf16[3,1376,1024]{2,1,0:T(8,128)(2,1)} %get-tuple-element.47.q_ref.k_ref.v_ref, ...), custom_call_target="tpu_custom_call" | custom-call | flops 31021072384 | bytes 16908288 | tf_op jit(solution)/shard_map/attend_forward/pallas_call | solution.py:895
  215.4 10.7 %middle.1 = (f32[4,344,1024]{2,1,0:T(8,128)}, bf16[4,344,1024]{2,1,0:T(8,128)(2,1)}, bf16[4,344,1024]{2,1,0:T(8,128)(2,1)}) custom-call(s32[2]{0:T(128)} %pad_add_fusion.flag_ref.len_ref, bf16[4,344,1024]{2,1,0:T(8,128)(2,1)} %bitcast.59, bf16[4,344,1024]{2,1,0:T(8,128)(2,1)} %bitcast.56, bf16[4,344,1024]{2,1,0:T(8,128)(2,1)} %get-tuple-element.51.cot_ref, ...), custom_call_target="tpu_custom_call" | custom-call | tf_op jit(solution)/shard_map/middle/pallas_call | solution.py:722
  226.1 0.9 slice.132
  227.2 0.8 reshape.93.b1_ref
  228.0 83.3 %feed_forward.1 = (f32[1376,1024]{1,0:T(8,128)}, f32[1376,1024]{1,0:T(8,128)}, bf16[4,1024,2048]{2,1,0:T(8,128)(2,1)}, f32[1,4096]{1,0:T(1,128)}) custom-call(bf16[1376,1024]{1,0:T(8,128)(2,1)} %bitcast.79, bf16[1376,1024]{1,0:T(8,128)(2,1)} %bitcast.80, bf16[4,1024,2048]{2,1,0:T(8,128)(2,1)} %get-tuple-element.54.w_ref, f32[1,4096]{1,0:T(1,128)} %reshape.93.b1_ref), custom_call_target="tpu_custom_call" | custom-call | flops 92341796864 | bytes 33554432 | tf_op jit(solution)/shard_map/feed_forward/pallas_call | solution.py:1110
  311.3 23.0 %turn.1 = (bf16[4,344,1024]{2,1,0:T(8,128)(2,1)}, f32[4,344,1024]{2,1,0:T(8,128)}, bf16[4,344,1024]{2,1,0:T(8,128)(2,1)}, bf16[4,1024,256]{2,1,0:T(8,128)(2,1)}, f32[8,1024]{1,0:T(8,128)}) custom-call(s32[2]{0:T(128)} %pad_add_fusion.flag_ref.len_ref, f32[4,344,1024]{2,1,0:T(8,128)} %bitcast.61, f32[4,344,1024]{2,1,0:T(8,128)} %bitcast.62, ...), custom_call_target="tpu_custom_call" | custom-call | tf_op jit(solution)/shard_map/turn/pallas_call | solution.py:800
  334.3 129.6 %attend_backward.1 = (bf16[1376,1024]{1,0:T(8,128)(2,1)}, bf16[1376,1024]{1,0:T(8,128)(2,1)}, bf16[1376,1024]{1,0:T(8,128)(2,1)}, f32[8,8,128]{2,1,0:T(8,128)}, ...) custom-call(s32[2]{0:T(128)} %pad_add_fusion.flag_ref.len_ref, ...), custom_call_target="tpu_custom_call" | custom-call | flops 77552680960 | bytes 22544384 | tf_op jit(solution)/shard_map/attend_backward/pallas_call | solution.py:1025
  465.4 0.8 slice_bitcast_fusion.8
  466.8 0.8 select_maximum_fusion
  467.7 83.5 %leave.1 = (bf16[3,344,1024]{2,1,0:T(8,128)(2,1)}, f32[128,768]{1,0:T(8,128)}, f32[32,128]{1,0:T(8,128)}) custom-call(bf16[1376,1024]{1,0:T(8,128)(2,1)} %get-tuple-element.63.gq_ref, bf16[1376,1024]{1,0:T(8,128)(2,1)} %get-tuple-element.64.gk_ref, bf16[1376,1024]{1,0:T(8,128)(2,1)} %get-tuple-element.65.gv_ref, ...), custom_call_target="tpu_custom_call" | custom-call | tf_op jit(solution)/shard_map/leave/pallas_call | solution.py:577
  551.2 4.2 convert_element_type.20
  555.5 0.8 pad_maximum_fusion.2
  557.8 0.8 pad_maximum_fusion.1
  559.3 1.0 copy.78
  560.9 1.3 copy.94
  (57 shorter events, 11.3 us)
Async XLA Ops:
  90.1 23.2 %copy-start.3 = (bf16[1024,128]{1,0:T(8,128)(2,1)S(1)}, bf16[1024,128]{1,0:T(8,128)(2,1)}, u32[]{:S(2)}) copy-start(bf16[1024,128]{1,0:T(8,128)(2,1)} %param.21) | copy-start | bytes 786436
  90.1 23.4 %copy-start.4 = (bf16[128,1024]{1,0:T(8,128)(2,1)S(1)}, bf16[128,1024]{1,0:T(8,128)(2,1)}, u32[]{:S(2)}) copy-start(bf16[128,1024]{1,0:T(8,128)(2,1)} %param.19) | copy-start | bytes 786436
  334.3 130.2 %copy-start.8 = (f32[1,4096]{1,0:T(1,128)S(1)}, f32[1,4096]{1,0:T(1,128)}, u32[]{:S(2)}) copy-start(f32[1,4096]{1,0:T(1,128)} %get-tuple-element.70) | copy-start | bytes 49156
  334.3 132.5 %copy-start.6 = (f32[8,1024]{1,0:T(8,128)S(1)}, f32[8,1024]{1,0:T(8,128)}, u32[]{:S(2)}) copy-start(f32[8,1024]{1,0:T(8,128)} %get-tuple-element.68) | copy-start | bytes 98308
  551.2 4.2 copy-start.2
  551.2 5.0 copy-start.7
  551.2 5.7 %copy-start.5 = (f32[128,256]{1,0:T(8,128)S(1)}, f32[128,256]{1,0:T(8,128)}, u32[]{:S(2)}) copy-start(f32[128,256]{1,0:T(8,128)} %get-tuple-element.74) | copy-start | bytes 393220
  551.2 6.5 %copy-start.1 = (f32[128,2048]{1,0:T(8,128)S(1)}, f32[128,2048]{1,0:T(8,128)}, u32[]{:S(2)}) copy-start(f32[128,2048]{1,0:T(8,128)} %get-tuple-element.75) | copy-start | bytes 3145732
  556.3 4.7 copy-start

commit v6 on v5

--- a/solution.py
+++ b/solution.py
@@ -14,7 +14,6 @@
 NEG = -1e30
 NT = (((1,), (1,)), ((), ()))
 NN = (((1,), (0,)), ((), ()))
-TN = (((0,), (0,)), ((), ()))
 f32 = jnp.float32
 bf16 = jnp.bfloat16
 
@@ -482,8 +481,8 @@
 
 
 def leave_kernel(
-    groups, line, gq_ref, gk_ref, gv_ref, w_ref, n1t_ref, x_ref, gh_ref, v_ref, smalls_ref,
-    yo_ref, shard_ref, small_ref, gn, y, full, smalls, sums, *scratch
+    groups, line, gq_ref, gk_ref, gv_ref, w_ref, n1t_hbm, x_hbm, gh_hbm, v_ref, smalls_ref,
+    yo_ref, shard_ref, small_ref, gn, y, full, smalls, sums, n1t_ref, x_ref, gh_ref, loads, *scratch
 ):
     at = Place(groups, line)
     n = len(ToOwner.sems(groups, line))
@@ -494,23 +493,27 @@
     step = pl.program_id(0)
     cols = gq_ref.shape[1]
     grads = (gq_ref, gk_ref, gv_ref)
+    pairs = ((x_hbm, x_ref), (gh_hbm, gh_ref), (n1t_hbm, n1t_ref))
+    copies = [pltpu.make_async_copy(a, b, loads.at[i]) for i, (a, b) in enumerate(pairs)]
 
     @pl.when(step == 0)
     def _():
+        for copy in copies:
+            copy.start()
         at.barrier()
         smalls[...] = smalls_ref[...]
         gn[...] = jnp.zeros_like(gn)
 
     @pl.when(step < line)
     def _():
-        for i, ref in enumerate(grads):
-            gn[...] += lax.dot_general(
-                ref[...], w_ref[0, :, i * cols : (i + 1) * cols], NT, preferred_element_type=f32
-            )
+        g = jnp.concatenate([ref[...] for ref in grads], axis=1)
+        gn[...] += lax.dot_general(g, w_ref[0], NT, preferred_element_type=f32)
 
     @pl.when(step == line - 1)
     def _():
         part = x_ref.shape[1]
+        copies[0].wait()
+        copies[1].wait()
         sums[...] = jnp.zeros_like(sums)
         for p in range(line):
 
@@ -536,6 +539,10 @@
                     smalls[t, at_row : at_row + 1, :] = row
         small.start()
 
+    @pl.when(step == line)
+    def _():
+        copies[2].wait()
+
     @pl.when(step >= line)
     def _():
         t = weights.far(step - line)
@@ -582,9 +589,9 @@
             grad,
             grad,
             pl.BlockSpec((1, width, c), lambda j: (jnp.minimum(j, line - 1), 0, 0)),
-            whole(width, rows),
-            whole(line, part, width),
-            whole(line, part, width),
+            ANY,
+            ANY,
+            ANY,
             whole(*vectors.shape),
             whole(*smalls.shape),
         ],
@@ -600,6 +607,10 @@
             pltpu.VMEM((line, width, c), bf16),
             pltpu.VMEM(smalls.shape, f32),
             pltpu.VMEM((16, width), f32),
+            pltpu.VMEM((width, rows), bf16),
+            pltpu.VMEM((line, part, width), bf16),
+            pltpu.VMEM((line, part, width), f32),
+            DMA((3,)),
         ]
         + ToOwner.sems(groups, line)
         + Reduce.scratch(groups, line, r, c, bf16)
@@ -630,17 +641,14 @@
     @pl.when(pl.program_id(0) == 0)
     def _():
         rows = x_ref.shape[0]
-        size = 32 if rows % 32 == 0 else 16
-
-        def chunk(i, carry):
-            r = pl.ds(pl.multiple_of(i * size, 16), size)
-            x = jnp.where(flag_ref[1] > 0, x_ref[r, :].astype(f32), 0.0)
-            xc_ref[r, :] = x.astype(bf16)
+        size = rows // 2 if rows % 32 == 0 else rows
+        for first in range(0, rows, size):
+            r = slice(first, first + size)
+            x = jnp.where(flag_ref[1] > 0, x_ref[r].astype(f32), 0.0)
+            xc_ref[r] = x.astype(bf16)
             hat, _ = norm_stats(x)
-            n1[r, :] = (hat * v_ref[0:1] + v_ref[2:3]).astype(bf16)
-            return carry
-
-        lax.fori_loop(0, rows // size, chunk, 0)
+            n1[r] = (hat * v_ref[0:1] + v_ref[2:3]).astype(bf16)
+
     cols = out_ref.shape[2]
     part = pl.ds(pl.multiple_of(pl.program_id(0) * cols, LANES), cols)
     n1t_ref[part, :] = n1[:, part].T
@@ -767,7 +775,7 @@
         hat, inverse = norm_stats(hidden)
         ghid = gout + norm_back(gn, hat, inverse, v_ref[1:2])
         gh_ref[0, r] = ghid
-        attn = (hidden - x_ref[0, r].astype(f32)) / v_ref[4:5]
+        attn = (hidden - x_ref[0, r].astype(f32)) * (1.0 / v_ref[4:5])
         grad = ghid * v_ref[4:5]
         gattn[r] = grad.astype(bf16)
         terms = (gn * hat, gn, ghid * attn, gout * mlp, grad, gout * v_ref[5:6])
@@ -781,12 +789,13 @@
         rows = [jnp.sum(sums[8 * j : 8 * j + 8], axis=0, keepdims=True) for j in range(6)]
         sum_ref[...] = jnp.concatenate(rows + [jnp.zeros((2, sums.shape[1]), f32)], axis=0)
 
+    gattn_t = gattn[...].T
     for t in range(line):
         ctx = ctx_ref[0, :, t * cols : (t + 1) * cols]
         gc_ref[0, :, t * cols : (t + 1) * cols] = lax.dot_general(
             gattn[...], w_ref[t], NN, preferred_element_type=f32
         ).astype(bf16)
-        acc[t] += lax.dot_general(gattn[...], ctx, TN, preferred_element_type=f32)
+        acc[t] += lax.dot_general(gattn_t, ctx, NN, preferred_element_type=f32)
 
     @pl.when(step == line - 1)
     def _():

time: 567 us -> 560 us (0.988)
  Pallas kernels: 531 us -> 521 us
    pallas_call x1, Pallas kernels: 23.2 us -> 16.5 us  [project(): pl.pallas_call(project_kernel, grid=(line,), in_specs=[SMEM, whole(rows,...]
where the time goes in v6:
time: 560 us; the launch traced here: 552 us
  Pallas kernels  521 us (93%)
  local copies, waits for them, and re-layouts  17 us (3%)
  other arithmetic  12.3 us (2%)
    pallas_call x1, Pallas kernels, attend_backward(): pl.pallas_call(functools.partial(attend_backward_kernel, groups, line, ro...  130 us
    pallas_call x1, Pallas kernels, attend_forward(): pl.pallas_call(functools.partial(attend_forward_kernel, groups, line, row...  101 us
    pallas_call x1, Pallas kernels, feed_forward(): pl.pallas_call(functools.partial(feed_forward_kernel, tile, FFC if rows %...  83.7 us
    pallas_call x1, Pallas kernels, leave(): pl.pallas_call(functools.partial(leave_kernel, groups, line), grid=(2 * l...  80 us
    pallas_call x1, Pallas kernels, arrive(): pl.pallas_call(functools.partial(arrive_kernel, groups, line), in_specs=[...  76.9 us
    pallas_call x1, Pallas kernels, turn(): pl.pallas_call(turn_kernel, grid=(line,), in_specs=[SMEM] + [piece] * 6 +...  22.8 us
    pallas_call x1, Pallas kernels, project(): pl.pallas_call(project_kernel, grid=(line,), in_specs=[SMEM, whole(rows,...  16.5 us

profile of v6, /device:TPU:0, one launch (start us, length us, event | category | flops | bytes accessed | tf_op | source)
XLA Modules:
  0.0 552.3 jit_solution(8842198967287899021)
XLA Ops:
  0.7 1.2 dynamic_slice.6
  3.1 0.9 copy.64
  4.1 0.9 slice_bitcast_fusion.6
  6.4 0.8 copy.79
  8.6 76.9 %arrive.1 = (bf16[4,344,1024]{2,1,0:T(8,128)(2,1)}, bf16[4,1024,1024]{2,1,0:T(8,128)(2,1)}, f32[4,256,128]{2,1,0:T(8,128)}) custom-call(bf16[3,344,1024]{2,1,0:T(8,128)(2,1)} %x_ref.1, bf16[128,1024]{1,0:T(8,128)(2,1)} %pad_maximum_fusion.3.shard_ref, f32[32,128]{1,0:T(8,128)} %pad_maximum_fusion.4.small_ref), custom_call_target="tpu_custom_call" | custom-call | tf_op jit(solution)/shard_map/arrive/pallas_call | solution.py:468
  85.5 0.9 slice.126
  87.3 1.0 slice_bitcast_fusion
  90.1 16.5 %project.1 = (bf16[3,1376,1024]{2,1,0:T(8,128)(2,1)}, bf16[1376,1024]{1,0:T(8,128)(2,1)}, bf16[1024,1376]{1,0:T(8,128)(2,1)}) custom-call(s32[2]{0:T(128)} %pad_add_fusion.flag_ref.len_ref, bf16[1376,1024]{1,0:T(8,128)(2,1)} %bitcast.77, f32[8,1024]{1,0:T(8,128)} %reshape.87.v_ref, bf16[4,1024,1024]{2,1,0:T(8,128)(2,1)} %get-tuple-element.46.w_ref, ...), custom_call_target="tpu_custom_call" | custom-call | flops 8657043456 | bytes 22544384 | tf_op jit(solution)/shard_map/project/pallas_call | solution.py:678
  106.8 0.8 pad_maximum_fusion.shard_ref
  107.6 101.2 %attend_forward.1 = (bf16[1376,1024]{1,0:T(8,128)(2,1)}, bf16[16,1376,128]{2,1,0:T(8,128)(2,1)}, bf16[4,1024,2048]{2,1,0:T(8,128)(2,1)}, bf16[4,344,1024]{2,1,0:T(8,128)(2,1)}) custom-call(s32[2]{0:T(128)} %pad_add_fusion.flag_ref.len_ref, bf16[3,1376,1024]{2,1,0:T(8,128)(2,1)} %get-tuple-element.47.q_ref.k_ref.v_ref, ...), custom_call_target="tpu_custom_call" | custom-call | flops 31021072384 | bytes 16908288 | tf_op jit(solution)/shard_map/attend_forward/pallas_call | solution.py:904
  208.8 10.3 %middle.1 = (f32[4,344,1024]{2,1,0:T(8,128)}, bf16[4,344,1024]{2,1,0:T(8,128)(2,1)}, bf16[4,344,1024]{2,1,0:T(8,128)(2,1)}) custom-call(s32[2]{0:T(128)} %pad_add_fusion.flag_ref.len_ref, bf16[4,344,1024]{2,1,0:T(8,128)(2,1)} %bitcast.59, bf16[4,344,1024]{2,1,0:T(8,128)(2,1)} %bitcast.56, bf16[4,344,1024]{2,1,0:T(8,128)(2,1)} %get-tuple-element.51.cot_ref, ...), custom_call_target="tpu_custom_call" | custom-call | tf_op jit(solution)/shard_map/middle/pallas_call | solution.py:730
  219.1 0.9 slice.132
  220.2 0.8 reshape.93.b1_ref
  221.0 83.7 %feed_forward.1 = (f32[1376,1024]{1,0:T(8,128)}, f32[1376,1024]{1,0:T(8,128)}, bf16[4,1024,2048]{2,1,0:T(8,128)(2,1)}, f32[1,4096]{1,0:T(1,128)}) custom-call(bf16[1376,1024]{1,0:T(8,128)(2,1)} %bitcast.79, bf16[1376,1024]{1,0:T(8,128)(2,1)} %bitcast.80, bf16[4,1024,2048]{2,1,0:T(8,128)(2,1)} %get-tuple-element.54.w_ref, f32[1,4096]{1,0:T(1,128)} %reshape.93.b1_ref), custom_call_target="tpu_custom_call" | custom-call | flops 92341796864 | bytes 33554432 | tf_op jit(solution)/shard_map/feed_forward/pallas_call | solution.py:1119
  304.7 22.8 %turn.1 = (bf16[4,344,1024]{2,1,0:T(8,128)(2,1)}, f32[4,344,1024]{2,1,0:T(8,128)}, bf16[4,344,1024]{2,1,0:T(8,128)(2,1)}, bf16[4,1024,256]{2,1,0:T(8,128)(2,1)}, f32[8,1024]{1,0:T(8,128)}) custom-call(s32[2]{0:T(128)} %pad_add_fusion.flag_ref.len_ref, f32[4,344,1024]{2,1,0:T(8,128)} %bitcast.61, f32[4,344,1024]{2,1,0:T(8,128)} %bitcast.62, ...), custom_call_target="tpu_custom_call" | custom-call | tf_op jit(solution)/shard_map/turn/pallas_call | solution.py:809
  327.5 129.6 %attend_backward.1 = (bf16[1376,1024]{1,0:T(8,128)(2,1)}, bf16[1376,1024]{1,0:T(8,128)(2,1)}, bf16[1376,1024]{1,0:T(8,128)(2,1)}, f32[8,8,128]{2,1,0:T(8,128)}, ...) custom-call(s32[2]{0:T(128)} %pad_add_fusion.flag_ref.len_ref, ...), custom_call_target="tpu_custom_call" | custom-call | flops 77552680960 | bytes 22544384 | tf_op jit(solution)/shard_map/attend_backward/pallas_call | solution.py:1034
  458.7 0.8 slice_bitcast_fusion.8
  460.1 0.8 select_maximum_fusion
  460.9 80.0 %leave.1 = (bf16[3,344,1024]{2,1,0:T(8,128)(2,1)}, f32[128,768]{1,0:T(8,128)}, f32[32,128]{1,0:T(8,128)}) custom-call(bf16[1376,1024]{1,0:T(8,128)(2,1)} %get-tuple-element.63.gq_ref, bf16[1376,1024]{1,0:T(8,128)(2,1)} %get-tuple-element.64.gk_ref, bf16[1376,1024]{1,0:T(8,128)(2,1)} %get-tuple-element.65.gv_ref, ...), custom_call_target="tpu_custom_call" | custom-call | tf_op jit(solution)/shard_map/leave/pallas_call | solution.py:584
  541.0 4.2 convert_element_type.20
  545.3 0.8 pad_maximum_fusion.2
  547.6 0.8 pad_maximum_fusion.1
  549.0 1.0 copy.78
  550.7 1.3 copy.94
  (57 shorter events, 11.3 us)
Async XLA Ops:
  90.1 16.5 %copy-start.3 = (bf16[1024,128]{1,0:T(8,128)(2,1)S(1)}, bf16[1024,128]{1,0:T(8,128)(2,1)}, u32[]{:S(2)}) copy-start(bf16[1024,128]{1,0:T(8,128)(2,1)} %param.21) | copy-start | bytes 786436
  90.1 16.6 %copy-start.4 = (bf16[128,1024]{1,0:T(8,128)(2,1)S(1)}, bf16[128,1024]{1,0:T(8,128)(2,1)}, u32[]{:S(2)}) copy-start(bf16[128,1024]{1,0:T(8,128)(2,1)} %param.19) | copy-start | bytes 786436
  327.5 130.2 %copy-start.8 = (f32[1,4096]{1,0:T(1,128)S(1)}, f32[1,4096]{1,0:T(1,128)}, u32[]{:S(2)}) copy-start(f32[1,4096]{1,0:T(1,128)} %get-tuple-element.70) | copy-start | bytes 49156
  327.5 132.5 %copy-start.6 = (f32[8,1024]{1,0:T(8,128)S(1)}, f32[8,1024]{1,0:T(8,128)}, u32[]{:S(2)}) copy-start(f32[8,1024]{1,0:T(8,128)} %get-tuple-element.68) | copy-start | bytes 98308
  541.0 4.2 copy-start.2
  541.0 5.0 copy-start.7
  541.0 5.7 %copy-start.5 = (f32[128,256]{1,0:T(8,128)S(1)}, f32[128,256]{1,0:T(8,128)}, u32[]{:S(2)}) copy-start(f32[128,256]{1,0:T(8,128)} %get-tuple-element.74) | copy-start | bytes 393220
  541.0 6.5 %copy-start.1 = (f32[128,2048]{1,0:T(8,128)S(1)}, f32[128,2048]{1,0:T(8,128)}, u32[]{:S(2)}) copy-start(f32[128,2048]{1,0:T(8,128)} %get-tuple-element.75) | copy-start | bytes 3145732
  546.0 4.7 copy-start

commit v7 on v6

--- a/solution.py
+++ b/solution.py
@@ -438,7 +438,7 @@
 ARRIVE = (0, 0, 1, 3)
 FFC = 2
 BACK = 6
-BWD = (2, 2, 7, 7, 7, 7, 16, 16, 16, 16, 27, 27)
+BWD = (2, 3, 7, 11, 8, 11, 19, 23, 19, 23, 28, 28)
 
 
 def run_ticks(ticks, step, part, parts):

time: 560 us -> 568 us (1.014)
  Pallas kernels: 521 us -> 527 us
    pallas_call x1, Pallas kernels: 80 us -> 88 us  [leave(): pl.pallas_call(functools.partial(leave_kernel, groups, line), grid=(2 * l...]
where the time goes in v7:
time: 568 us; the launch traced here: 558 us
  Pallas kernels  527 us (93%)
  local copies, waits for them, and re-layouts  17 us (3%)
  other arithmetic  12.3 us (2%)
    pallas_call x1, Pallas kernels, attend_backward(): pl.pallas_call(functools.partial(attend_backward_kernel, groups, line, ro...  128 us
    pallas_call x1, Pallas kernels, attend_forward(): pl.pallas_call(functools.partial(attend_forward_kernel, groups, line, row...  101 us
    pallas_call x1, Pallas kernels, leave(): pl.pallas_call(functools.partial(leave_kernel, groups, line), grid=(2 * l...  88 us
    pallas_call x1, Pallas kernels, feed_forward(): pl.pallas_call(functools.partial(feed_forward_kernel, tile, FFC if rows %...  83.7 us
    pallas_call x1, Pallas kernels, arrive(): pl.pallas_call(functools.partial(arrive_kernel, groups, line), in_specs=[...  76.9 us
    pallas_call x1, Pallas kernels, turn(): pl.pallas_call(turn_kernel, grid=(line,), in_specs=[SMEM] + [piece] * 6 +...  22.8 us
    pallas_call x1, Pallas kernels, project(): pl.pallas_call(project_kernel, grid=(line,), in_specs=[SMEM, whole(rows,...  16.5 us

profile of v7, /device:TPU:0, one launch (start us, length us, event | category | flops | bytes accessed | tf_op | source)
XLA Modules:
  0.0 558.4 jit_solution(10600916829924427235)
XLA Ops:
  0.7 1.2 dynamic_slice.6
  3.1 0.9 copy.64
  4.1 0.9 slice_bitcast_fusion.6
  6.4 0.8 copy.79
  8.6 76.9 %arrive.1 = (bf16[4,344,1024]{2,1,0:T(8,128)(2,1)}, bf16[4,1024,1024]{2,1,0:T(8,128)(2,1)}, f32[4,256,128]{2,1,0:T(8,128)}) custom-call(bf16[3,344,1024]{2,1,0:T(8,128)(2,1)} %x_ref.1, bf16[128,1024]{1,0:T(8,128)(2,1)} %pad_maximum_fusion.3.shard_ref, f32[32,128]{1,0:T(8,128)} %pad_maximum_fusion.4.small_ref), custom_call_target="tpu_custom_call" | custom-call | tf_op jit(solution)/shard_map/arrive/pallas_call | solution.py:468
  85.5 0.9 slice.126
  87.3 1.0 slice_bitcast_fusion
  90.1 16.5 %project.1 = (bf16[3,1376,1024]{2,1,0:T(8,128)(2,1)}, bf16[1376,1024]{1,0:T(8,128)(2,1)}, bf16[1024,1376]{1,0:T(8,128)(2,1)}) custom-call(s32[2]{0:T(128)} %pad_add_fusion.flag_ref.len_ref, bf16[1376,1024]{1,0:T(8,128)(2,1)} %bitcast.77, f32[8,1024]{1,0:T(8,128)} %reshape.87.v_ref, bf16[4,1024,1024]{2,1,0:T(8,128)(2,1)} %get-tuple-element.46.w_ref, ...), custom_call_target="tpu_custom_call" | custom-call | flops 8657043456 | bytes 22544384 | tf_op jit(solution)/shard_map/project/pallas_call | solution.py:678
  106.8 0.8 pad_maximum_fusion.shard_ref
  107.6 101.2 %attend_forward.1 = (bf16[1376,1024]{1,0:T(8,128)(2,1)}, bf16[16,1376,128]{2,1,0:T(8,128)(2,1)}, bf16[4,1024,2048]{2,1,0:T(8,128)(2,1)}, bf16[4,344,1024]{2,1,0:T(8,128)(2,1)}) custom-call(s32[2]{0:T(128)} %pad_add_fusion.flag_ref.len_ref, bf16[3,1376,1024]{2,1,0:T(8,128)(2,1)} %get-tuple-element.47.q_ref.k_ref.v_ref, ...), custom_call_target="tpu_custom_call" | custom-call | flops 31021072384 | bytes 16908288 | tf_op jit(solution)/shard_map/attend_forward/pallas_call | solution.py:904
  208.8 10.3 %middle.1 = (f32[4,344,1024]{2,1,0:T(8,128)}, bf16[4,344,1024]{2,1,0:T(8,128)(2,1)}, bf16[4,344,1024]{2,1,0:T(8,128)(2,1)}) custom-call(s32[2]{0:T(128)} %pad_add_fusion.flag_ref.len_ref, bf16[4,344,1024]{2,1,0:T(8,128)(2,1)} %bitcast.59, bf16[4,344,1024]{2,1,0:T(8,128)(2,1)} %bitcast.56, bf16[4,344,1024]{2,1,0:T(8,128)(2,1)} %get-tuple-element.51.cot_ref, ...), custom_call_target="tpu_custom_call" | custom-call | tf_op jit(solution)/shard_map/middle/pallas_call | solution.py:730
  219.1 0.9 slice.132
  220.2 0.8 reshape.93.b1_ref
  221.0 83.7 %feed_forward.1 = (f32[1376,1024]{1,0:T(8,128)}, f32[1376,1024]{1,0:T(8,128)}, bf16[4,1024,2048]{2,1,0:T(8,128)(2,1)}, f32[1,4096]{1,0:T(1,128)}) custom-call(bf16[1376,1024]{1,0:T(8,128)(2,1)} %bitcast.79, bf16[1376,1024]{1,0:T(8,128)(2,1)} %bitcast.80, bf16[4,1024,2048]{2,1,0:T(8,128)(2,1)} %get-tuple-element.54.w_ref, f32[1,4096]{1,0:T(1,128)} %reshape.93.b1_ref), custom_call_target="tpu_custom_call" | custom-call | flops 92341796864 | bytes 33554432 | tf_op jit(solution)/shard_map/feed_forward/pallas_call | solution.py:1119
  304.7 22.8 %turn.1 = (bf16[4,344,1024]{2,1,0:T(8,128)(2,1)}, f32[4,344,1024]{2,1,0:T(8,128)}, bf16[4,344,1024]{2,1,0:T(8,128)(2,1)}, bf16[4,1024,256]{2,1,0:T(8,128)(2,1)}, f32[8,1024]{1,0:T(8,128)}) custom-call(s32[2]{0:T(128)} %pad_add_fusion.flag_ref.len_ref, f32[4,344,1024]{2,1,0:T(8,128)} %bitcast.61, f32[4,344,1024]{2,1,0:T(8,128)} %bitcast.62, ...), custom_call_target="tpu_custom_call" | custom-call | tf_op jit(solution)/shard_map/turn/pallas_call | solution.py:809
  327.5 127.8 %attend_backward.1 = (bf16[1376,1024]{1,0:T(8,128)(2,1)}, bf16[1376,1024]{1,0:T(8,128)(2,1)}, bf16[1376,1024]{1,0:T(8,128)(2,1)}, f32[8,8,128]{2,1,0:T(8,128)}, ...) custom-call(s32[2]{0:T(128)} %pad_add_fusion.flag_ref.len_ref, ...), custom_call_target="tpu_custom_call" | custom-call | flops 77552680960 | bytes 22544384 | tf_op jit(solution)/shard_map/attend_backward/pallas_call | solution.py:1034
  456.8 0.8 slice_bitcast_fusion.8
  458.2 0.8 select_maximum_fusion
  459.1 88.0 %leave.1 = (bf16[3,344,1024]{2,1,0:T(8,128)(2,1)}, f32[128,768]{1,0:T(8,128)}, f32[32,128]{1,0:T(8,128)}) custom-call(bf16[1376,1024]{1,0:T(8,128)(2,1)} %get-tuple-element.63.gq_ref, bf16[1376,1024]{1,0:T(8,128)(2,1)} %get-tuple-element.64.gk_ref, bf16[1376,1024]{1,0:T(8,128)(2,1)} %get-tuple-element.65.gv_ref, ...), custom_call_target="tpu_custom_call" | custom-call | tf_op jit(solution)/shard_map/leave/pallas_call | solution.py:584
  547.2 4.2 convert_element_type.20
  551.4 0.8 pad_maximum_fusion.2
  553.7 0.8 pad_maximum_fusion.1
  555.2 1.0 copy.78
  556.8 1.3 copy.94
  (57 shorter events, 11.3 us)
Async XLA Ops:
  90.1 16.5 %copy-start.3 = (bf16[1024,128]{1,0:T(8,128)(2,1)S(1)}, bf16[1024,128]{1,0:T(8,128)(2,1)}, u32[]{:S(2)}) copy-start(bf16[1024,128]{1,0:T(8,128)(2,1)} %param.21) | copy-start | bytes 786436
  90.1 16.6 %copy-start.4 = (bf16[128,1024]{1,0:T(8,128)(2,1)S(1)}, bf16[128,1024]{1,0:T(8,128)(2,1)}, u32[]{:S(2)}) copy-start(bf16[128,1024]{1,0:T(8,128)(2,1)} %param.19) | copy-start | bytes 786436
  327.5 128.3 %copy-start.8 = (f32[1,4096]{1,0:T(1,128)S(1)}, f32[1,4096]{1,0:T(1,128)}, u32[]{:S(2)}) copy-start(f32[1,4096]{1,0:T(1,128)} %get-tuple-element.70) | copy-start | bytes 49156
  327.5 130.6 %copy-start.6 = (f32[8,1024]{1,0:T(8,128)S(1)}, f32[8,1024]{1,0:T(8,128)}, u32[]{:S(2)}) copy-start(f32[8,1024]{1,0:T(8,128)} %get-tuple-element.68) | copy-start | bytes 98308
  547.1 4.2 copy-start.2
  547.1 5.0 copy-start.7
  547.1 5.7 %copy-start.5 = (f32[128,256]{1,0:T(8,128)S(1)}, f32[128,256]{1,0:T(8,128)}, u32[]{:S(2)}) copy-start(f32[128,256]{1,0:T(8,128)} %get-tuple-element.74) | copy-start | bytes 393220
  547.1 6.5 %copy-start.1 = (f32[128,2048]{1,0:T(8,128)S(1)}, f32[128,2048]{1,0:T(8,128)}, u32[]{:S(2)}) copy-start(f32[128,2048]{1,0:T(8,128)} %get-tuple-element.75) | copy-start | bytes 3145732
  552.2 4.7 copy-start
